TPU v7x, 32 devices: a whole 2x2x4 slice. The times are simulated.
32 devices in a mesh: fsdp: 8 (over y, x, core), rep: 4 (over z).
Axes of the slice: x: 2, y: 2, z: 4, core: 2. Of those that a mesh axis runs over, the one named last changes fastest.
Arguments:
- tokens: bfloat16 [4, 1024, 2048], P('rep', 'fsdp'), may hold values from -6 to 6
- upstream: bfloat16 [4, 7168, 1024], P('rep', 'fsdp'), may hold values from -0.5 to 0.5
- weight: bfloat16 [2, 7168, 2048], P(None, 'fsdp'), may hold values from -0.125 to 0.125
- feedback: float32 [4, 2, 7168, 2048], P('rep', None, 'fsdp'), may hold values from -6 to 6
- momentum: float32 [2, 7168, 2048], P(None, 'fsdp', 'rep'), may hold values from -6 to 6
- right_factor: float32 [2, 7168, 64], P(None, 'fsdp'), may hold values from -6 to 6
Outputs:
- feedback_next: float32 [4, 2, 7168, 2048], P('rep', None, 'fsdp')
- momentum_next: float32 [2, 7168, 2048], P(None, 'fsdp', 'rep')
- weight_next: bfloat16 [2, 7168, 2048], P(None, 'fsdp', 'rep')
- right_next: float32 [2, 7168, 64], P(None, 'fsdp')
All inputs are finite; a program needn't handle non-finite values.
Results may differ from a plain program's by a relative error of at most 0.0023.
Values may be sent and summed in bfloat16 or wider, within the bound.
No kernel may reach another device: no remote copies, remote signals or barrier semaphores. Data moves between devices by JAX's collectives and lax.ppermute only.
A program may use at most 128 MiB of HBM per device.

v0:
```python
import jax
import jax.numpy as jnp
from jax import lax
from jax.experimental import pallas as pl
from jax.experimental.pallas import tpu as pltpu
from jax.sharding import PartitionSpec as P

momentum_decay = 0.9
step_rate = 0.05
highest = lax.Precision.HIGHEST
f32 = jnp.float32
bf16 = jnp.bfloat16
contract_last = (((1,), (1,)), ((), ()))
MIB = 1024 * 1024
vmem = pl.BlockSpec(memory_space=pltpu.VMEM)
smem = pl.BlockSpec(memory_space=pltpu.SMEM)
anywhere = pl.BlockSpec(memory_space=pl.ANY)
hbm = pl.BlockSpec(memory_space=pltpu.HBM)


def split2(x):
    hi = x.astype(bf16)
    return hi, (x - hi.astype(f32)).astype(bf16)


def stacked(x):
    return jnp.concatenate(split2(x), 0)


def fold(x):
    half = x.shape[0] // 2
    return x[:half] + x[half:]


def dot(a, b):
    return jnp.dot(a, b, preferred_element_type=f32)


def dot_nt(a, b):
    return lax.dot_general(a, b, contract_last, preferred_element_type=f32)


def shape(*dims, dtype=f32):
    return jax.ShapeDtypeStruct(dims, dtype)


def call(body, place, operands, out_shape, mib, macs=0, **more):
    nbytes = sum(x.size * x.dtype.itemsize for x in operands)
    spec = dict(
        in_specs=[smem] + [vmem] * len(operands),
        out_specs=jax.tree.map(lambda _: vmem, out_shape),
    ) | more
    return pl.pallas_call(
        body,
        out_shape=out_shape,
        compiler_params=pltpu.CompilerParams(vmem_limit_bytes=mib * MIB),
        cost_estimate=pl.CostEstimate(flops=2 * macs, bytes_accessed=nbytes, transcendentals=0),
        **spec,
    )(place, *operands)


def divisor(size, most, unit):
    return max(b for b in range(unit, min(size, most) + 1, unit) if size % b == 0)


def span(i, size):
    return pl.ds(pl.multiple_of(i * size, size), size)


def grant(total, feats):
    return 16 if total * feats <= 4 * MIB else 28


def feedback_left(place, feedback, weight, right_t):
    _, rows, feats = feedback.shape
    rank = right_t.shape[1]
    block = 512
    steps = feats // block

    def body(place_ref, fb_ref, w_ref, r_ref, held_ref, held_w_ref, out_ref, sems, w_sems):
        def copy(k, d):
            cols = slice(d * block, (d + 1) * block)
            return pltpu.make_async_copy(
                fb_ref.at[k, :, cols], held_ref.at[k, :, cols], sems.at[k, d]
            )

        order = [(k, d) for k in range(2) for d in range(steps)]
        for k, d in order:
            copy(k, d).start()
        w_copies = [
            pltpu.make_async_copy(w_ref.at[k], held_w_ref.at[k], w_sems.at[k]) for k in range(2)
        ]
        for c in w_copies:
            c.start()
        for k, d in order:
            cols = slice(d * block, (d + 1) * block)
            r_cat = stacked(r_ref[k])
            copy(k, d).wait()
            fb_hi, fb_lo = split2(held_ref[k, :, cols])
            out_ref[k, :, cols] = fold(dot(r_cat, fb_hi)) + dot(r_cat[:rank], fb_lo)
        for c in w_copies:
            c.wait()

    return call(
        body, place, (feedback, weight, right_t),
        [shape(*feedback.shape), shape(*weight.shape, dtype=bf16), shape(2, rank, feats)], 16,
        2 * rows * feats * 256, name="feedback_left", in_specs=[smem, hbm, hbm, vmem],
        scratch_shapes=[pltpu.SemaphoreType.DMA((2, steps)), pltpu.SemaphoreType.DMA((2,))],
    )


def forward_chunk(place, parts, offsets, weight, upstream, right_t, left_in):
    count = len(parts)
    feats = parts[0].shape[1]
    width = sum(p.shape[0] for p in parts)
    per = width // len(offsets)
    rows = weight.shape[1]
    rank = right_t.shape[1]

    def body(place_ref, *refs):
        tok_refs, refs = refs[:count], refs[count:]
        w_ref, up_ref, r_ref, left_ref, grad_ref, tok_ref, left_out = refs
        me = place_ref[0]
        at = 0
        for t in tok_refs:
            tok_ref[at : at + t.shape[0], :] = t[...]
            at += t.shape[0]
        gate_pre = dot_nt(w_ref[0], tok_ref[...])
        up_pre = dot_nt(w_ref[1], tok_ref[...])
        cot = jnp.concatenate([up_ref[:, span(me ^ o, per)] for o in offsets], 1).astype(f32)
        s = jax.nn.sigmoid(gate_pre)
        cot_s = cot * s
        grad_ref[0] = (cot_s * up_pre * (1.0 + gate_pre * (1.0 - s))).astype(bf16)
        grad_ref[1] = (cot_s * gate_pre).astype(bf16)
        for k in range(2):
            h = fold(dot(stacked(r_ref[k]), grad_ref[k]))
            left_out[k] = left_ref[k] + fold(dot(stacked(h), tok_ref[...]))

    return call(
        body, place, (*parts, weight, upstream, right_t, left_in),
        [shape(2, rows, width, dtype=bf16), shape(width, feats, dtype=bf16), shape(2, rank, feats)],
        grant(width, feats), 2 * rows * feats * width, name="forward_chunk",
    )


def gradient(place, delta, grads, toks, k, part, parts):
    _, rows, feats = delta.shape
    total = sum(t.shape[0] for t in toks)
    block = feats // parts
    cols = slice(part * block, (part + 1) * block)
    count = len(toks)

    def body(place_ref, fb_ref, *refs):
        acc = fb_ref[k, :, cols]
        for g, t in zip(refs[:count], refs[count : 2 * count]):
            acc = acc + dot(g[k], t[:, cols])
        refs[2 * count][k, :, cols] = acc

    return call(
        body, place, (delta, *grads, *toks), shape(*delta.shape), grant(total // 2, feats),
        rows * block * total, name="gradient", input_output_aliases={1: 0},
    )


def project(place, delta, mine, other, k, scale):
    _, rows, feats = delta.shape
    rank = mine.shape[0]
    block = 512

    def body(place_ref, delta_ref, mine_ref, other_ref, out_ref):
        own = (place_ref[0] & 1) == k
        acc = None
        for d in range(feats // block):
            cols = slice(d * block, (d + 1) * block)
            cat = stacked(jnp.where(own, mine_ref[:, cols], other_ref[:, cols]) * scale)
            hi, lo = split2(delta_ref[k, :, cols])
            part = fold(dot_nt(cat, hi)) + dot_nt(cat[:rank], lo)
            acc = part if acc is None else acc + part
        out_ref[...] = acc

    return call(
        body, place, (delta, mine, other), shape(rank, rows), 16, rows * feats * 256, name="project"
    )


def factorize(place, mine, other, scale):
    rank, feats = mine.shape

    def body(place_ref, mine_ref, other_ref, inv_ref):
        core = place_ref[0] & 1
        row_id = lax.broadcasted_iota(jnp.int32, (rank, 1), 0)
        eye = (
            lax.broadcasted_iota(jnp.int32, (rank, rank), 0)
            == lax.broadcasted_iota(jnp.int32, (rank, rank), 1)
        ).astype(f32)
        work, roots = [], []
        for k in range(2):
            x = jnp.where(core == k, mine_ref[...], other_ref[...]) * scale
            gram = lax.dot_general(x, x, contract_last, precision=highest, preferred_element_type=f32)
            work.append(jnp.concatenate([gram, eye], 1))
            roots.append(jnp.zeros((rank, 1), f32))
        for j in range(rank):
            for k in range(2):
                a = work[k]
                pivot = a[j : j + 1, j : j + 1]
                ratio = jnp.where(row_id > j, a[:, j : j + 1] / pivot, 0.0)
                roots[k] = jnp.where(row_id == j, lax.rsqrt(pivot), roots[k])
                work[k] = a - ratio * a[j : j + 1, :]
        for k in range(2):
            inv_ref[k] = work[k][:, rank:] * roots[k]

    return call(
        body, place, (mine, other), shape(2, rank, rank), 8, 1000000000, name="factorize"
    )


def make_basis(place, mine, other, inverse, scale):
    rank, feats = mine.shape

    def body(place_ref, mine_ref, other_ref, inv_ref, cat_ref):
        core = place_ref[0] & 1
        for k in range(2):
            x = jnp.where(core == k, mine_ref[...], other_ref[...]) * scale
            basis = jnp.dot(inv_ref[k], x, precision=highest, preferred_element_type=f32)
            b_hi, b_lo = split2(basis)
            cat_ref[k] = jnp.concatenate([b_hi, b_lo, b_hi], 0)

    return call(
        body, place, (mine, other, inverse), shape(2, 3 * rank, feats, dtype=bf16), 8, 500000000,
        name="make_basis",
    )


def finish(place, ys, gots, inverse, basis_cat, delta, momentum, weight, replicas):
    _, rows, feats = delta.shape
    rank = ys[0].shape[0]
    cols = momentum.shape[2]
    block = divisor(rows, 128, 16)
    steps = rows // block
    slots = min(4, 2 * steps)

    def body(
        place_ref, y0_ref, y1_ref, got0_ref, got1_ref, inv_ref, cat_ref, delta_ref, mom_ref, w_ref,
        fb_out, mom_out, w_out, rn_out, rn_cat, fb_slot, mom_slot, w_slot, sems,
    ):
        slab = span(place_ref[1], cols)
        for k, (y_ref, got_ref) in enumerate(((y0_ref, got0_ref), (y1_ref, got1_ref))):
            mean = (y_ref[...] + got_ref[...]) * (1.0 / replicas)
            rn_t = jnp.dot(inv_ref[k], mean, precision=highest, preferred_element_type=f32)
            rn_out[k] = rn_t
            hi, lo = split2(rn_t.T)
            rn_cat[k] = jnp.concatenate([hi, hi, lo], 1)

        def copies(i):
            k, at, slot = i // steps, span(i % steps, block), i % slots
            return [
                pltpu.make_async_copy(src.at[slot], dst.at[k, at, :], sems.at[j, slot])
                for j, (src, dst) in enumerate(
                    ((fb_slot, fb_out), (mom_slot, mom_out), (w_slot, w_out))
                )
            ]

        def step(i, _):
            k, at, slot = i // steps, span(i % steps, block), i % slots

            @pl.when(i >= slots)
            def _():
                for c in copies(i - slots):
                    c.wait()

            part = rn_cat[k, at, :]
            fb_slot[slot] = delta_ref[k, at, :] - dot(part, cat_ref[k])
            mom = momentum_decay * mom_ref[k, at, :] + dot(part, cat_ref[k, :, slab])
            mom_slot[slot] = mom
            w_slot[slot] = (w_ref[k, at, slab].astype(f32) - step_rate * mom).astype(bf16)
            for c in copies(i):
                c.start()
            return 0

        lax.fori_loop(0, 2 * steps, step, 0)
        for i in range(2 * steps - slots, 2 * steps):
            for c in copies(i):
                c.wait()

    return call(
        body, place, (*ys, *gots, inverse, basis_cat, delta, momentum, weight),
        [
            shape(2, rows, feats), shape(2, rows, cols),
            shape(2, rows, cols, dtype=bf16), shape(2, rank, rows),
        ],
        16, 2 * rows * feats * 256, name="finish",
        out_specs=[anywhere, anywhere, anywhere, vmem],
        scratch_shapes=[
            pltpu.VMEM((2, rows, 3 * rank), bf16),
            pltpu.VMEM((slots, block, feats), f32),
            pltpu.VMEM((slots, block, cols), f32),
            pltpu.VMEM((slots, block, cols), bf16),
            pltpu.SemaphoreType.DMA((3, slots)),
        ],
    )


def swap(x, axis, mask):
    size = lax.axis_size(axis)
    return lax.ppermute(x, axis, [(i, i ^ mask) for i in range(size)])


def after(x, *others):
    return lax.optimization_barrier((x, *others))[0]


def has(place_ref, mask):
    return (place_ref[0] & mask) != 0


def by_core(place, left_t):
    _, rank, feats = left_t.shape

    def body(place_ref, left_ref, keep_ref, send_ref):
        odd = has(place_ref, 1)
        keep_ref[...] = jnp.where(odd, left_ref[1], left_ref[0])
        send_ref[...] = jnp.where(odd, left_ref[0], left_ref[1])

    return call(body, place, (left_t,), [shape(rank, feats)] * 2, 4, name="by_core")


def add(place, mine, got, masks=None):
    count = len(mine)

    def body(place_ref, *refs):
        outs = refs[2 * count :]
        for j in range(count):
            total = refs[j][...] + refs[count + j][...]
            if masks is None:
                outs[j][...] = total
                continue
            half = total.shape[1] // 2
            high = has(place_ref, masks[j])
            outs[j][...] = jnp.where(high, total[:, half:], total[:, :half])
            outs[count + j][...] = jnp.where(high, total[:, :half], total[:, half:])

    out = [shape(*x.shape) for x in mine]
    if masks is not None:
        out = [shape(x.shape[0], x.shape[1] // 2) for x in mine] * 2
    res = call(body, place, (*mine, *got), out, 4, name="add")
    return res if masks is None else (res[:count], res[count:])


def add_bands(place, keep, got, masks):
    rank, feats = keep.shape
    band, half = rank // 2, feats // 2

    def body(place_ref, keep_ref, got_ref, *outs):
        for j in range(2):
            at = slice(j * band, (j + 1) * band)
            total = keep_ref[at, :] + got_ref[at, :]
            high = has(place_ref, masks[j])
            outs[j][...] = jnp.where(high, total[:, half:], total[:, :half])
            outs[2 + j][...] = jnp.where(high, total[:, :half], total[:, half:])

    res = call(body, place, (keep, got), [shape(band, half)] * 4, 4, name="add_bands")
    return res[:2], res[2:]


def join(place, mine, got, masks, last):
    band, width = mine[0].shape

    def body(place_ref, a0, a1, b0, b1, *outs):
        for j, (a, b) in enumerate(((a0, b0), (a1, b1))):
            high = has(place_ref, masks[j])
            x, y = a[...], b[...]
            both = jnp.concatenate([jnp.where(high, y, x), jnp.where(high, x, y)], 1)
            if last:
                outs[0][j * band : (j + 1) * band, :] = both
            else:
                outs[j][...] = both

    out = [shape(2 * band, 2 * width)] if last else [shape(band, 2 * width)] * 2
    return call(body, place, (*mine, *got), out, 4, name="join")


def left_total(place, left_t, work):
    fsdp, rep = lax.axis_size("fsdp"), lax.axis_size("rep")
    masks = [1 << b for b in range(1, fsdp.bit_length() - 1)]
    orders = list(zip(masks, masks[::-1]))
    rep_masks = [(2 << b) - 1 for b in range(rep.bit_length() - 1)]

    def beside(sends, axis, step_masks, count):
        got = [swap(x, axis, m) for x, m in zip(sends, step_masks)]
        return lax.optimization_barrier((*got, work(sends, count)))[:-1]

    keep, send = by_core(place, left_t)
    got = swap(send, "fsdp", 1)
    keeps, sends = add_bands(place, keep, got, orders[0])
    for step in range(len(masks)):
        got = beside(sends, "fsdp", orders[step], 2 - min(step, 1))
        if step + 1 < len(masks):
            keeps, sends = add(place, keeps, got, orders[step + 1])
        else:
            pieces = add(place, keeps, got)
    for pair in zip(rep_masks, rep_masks[::-1]):
        pieces = add(place, pieces, beside(pieces, "rep", pair, 1))
    for step in reversed(range(len(masks))):
        got = beside(pieces, "fsdp", orders[step], 2 - min(step, 1))
        pieces = join(place, pieces, got, orders[step], step == 0)
    return pieces[0], swap(pieces[0], "fsdp", 1)


def per_device(tokens, upstream, weight, feedback, momentum, right_factor):
    fsdp, replicas = lax.axis_size("fsdp"), lax.axis_size("rep")
    place = jnp.stack([lax.axis_index("fsdp"), lax.axis_index("rep")]).astype(jnp.int32)
    own = tokens[0]
    per, feats = own.shape
    inner = [1 << b for b in range(fsdp.bit_length() - 3)]
    far_x, far_y = fsdp // 4, fsdp // 2
    right_t = jnp.swapaxes(right_factor, 1, 2)
    scale = 1.0 / replicas

    def gather_inner(parts, base):
        parts, offsets = list(parts), [base]
        for m in inner:
            parts = parts + [swap(p, "fsdp", m) for p in parts]
            offsets = offsets + [o ^ m for o in offsets]
        return parts, offsets

    def halves(x, y):
        def body(place_ref, x_ref, y_ref, x_out, y_out):
            x_out[...] = x_ref[: per // 2, :]
            y_out[...] = y_ref[per // 2 :, :]

        return call(body, place, (x, y), [shape(per // 2, feats, dtype=bf16)] * 2, 4, name="halves")

    grads, toks = [], []

    def forward(parts, offsets, left):
        grad, tok, left = forward_chunk(
            place, parts, offsets, held_weight, upstream[0], right_t, left
        )
        grads.append(grad)
        toks.append(tok)
        return left

    got_x = swap(own, "fsdp", far_x)
    got_y = swap(own, "fsdp", far_y)
    parts, offsets = gather_inner([own], 0)
    delta, held_weight, left_t = feedback_left(place, feedback[0], weight, right_t)
    left_t = forward(parts, offsets, left_t)
    got_x, got_y, left_t = lax.optimization_barrier((got_x, got_y, left_t))
    send_x, send_y = halves(got_x, got_y)
    far = [swap(send_x, "fsdp", far_y), swap(send_y, "fsdp", far_x)]
    parts_x, offsets_x = gather_inner([got_x], far_x)
    parts_y, offsets_y = gather_inner([got_y], far_y)
    left_t = forward(parts_x + parts_y, offsets_x + offsets_y, left_t)
    far_0, far_1, left_t = lax.optimization_barrier((*far, left_t))
    parts, offsets = gather_inner([far_0, far_1], far_x ^ far_y)
    left_t = forward(parts, offsets, left_t)

    pending = [(k, part) for k in range(2) for part in range(4)]

    def pieces(count):
        nonlocal delta
        for _ in range(min(count, len(pending))):
            k, part = pending.pop(0)
            delta = gradient(place, delta, grads, toks, k, part, 4)

    def work(sends, count):
        nonlocal delta
        delta = after(delta, *sends)
        pieces(count)
        return delta

    mine, other = left_total(place, left_t, work)
    pieces(len(pending))
    y = [project(place, delta, mine, other, k, scale) for k in range(2)]
    masks = [(2 << b) - 1 for b in range(replicas.bit_length() - 1)]
    for step, pair in enumerate(zip(masks, masks[::-1])):
        got = [swap(p, "rep", m) for p, m in zip(y, pair)]
        if step == 0:
            inverse = factorize(place, after(mine, *y), other, scale)
            got = lax.optimization_barrier((*got, inverse))[:-1]
        if step == 1:
            basis_cat = make_basis(place, after(mine, *y), other, inverse, scale)
        if step + 1 < len(masks):
            y = add(place, y, got)
    feedback_next, momentum_next, weight_next, rn_t = finish(
        place, y, got, inverse, basis_cat, delta, momentum, held_weight, replicas
    )
    return (feedback_next[None], momentum_next, weight_next, jnp.swapaxes(rn_t, 1, 2))


def solution(mesh):
    placed = (
        P("rep", "fsdp", None),
        P("rep", "fsdp", None),
        P(None, "fsdp", None),
        P("rep", None, "fsdp", None),
        P(None, "fsdp", "rep"),
        P(None, "fsdp", None),
    )
    return jax.shard_map(
        per_device,
        mesh=mesh,
        in_specs=placed,
        out_specs=(
            P("rep", None, "fsdp", None),
            P(None, "fsdp", "rep"),
            P(None, "fsdp", "rep"),
            P(None, "fsdp", None),
        ),
        check_vma=False,
    )
```

profile of v0, /device:TPU:0, one launch (start us, length us, event | category | flops | bytes accessed | tf_op | source)
XLA Modules:
  0.0 123.3 jit_solution(9844796070852727318)
XLA Ops:
  1.1 2.6 %collective-permute-start.1 = (bf16[128,2048]{1,0:T(8,128)(2,1)}, bf16[128,2048]{1,0:T(8,128)(2,1)S(1)}, u32[]{:S(2)}, u32[]{:S(2)}) collective-permute-start(bf16[128,2048]{1,0:T(8,128)(2,1)} %bitcast.16), channel_id=1, source_target_pairs={{0,16},{4,20},{8,24},{12,28},{16,0},{20,4},{24,8},{28,12},{1,17},{... | collective-permute-start | bytes 1572872 | tf_op jit(solution)/shard_map/ppermute | solution.py:305
  5.3 3.1 %copy-done.2 = bf16[2,896,2048]{2,1,0:T(8,128)(2,1)S(1)} copy-done((bf16[2,896,2048]{2,1,0:T(8,128)(2,1)S(1)}, bf16[2,896,2048]{2,1,0:T(8,128)(2,1)}, u32[]{:S(2)}) %copy-start.2) | copy-done | bytes 7340056
  9.4 6.7 %feedback_left.1 = (f32[2,896,2048]{2,1,0:T(8,128)S(1)}, bf16[2,896,2048]{2,1,0:T(8,128)(2,1)S(1)}, f32[2,64,2048]{2,1,0:T(8,128)S(1)}) custom-call(s32[2]{0:T(128)S(1)} %pad_add_fusion.place_ref, f32[2,896,2048]{2,1,0:T(8,128)} %bitcast.19, bf16[2,896,2048]{2,1,0:T(8,128)(2,1)S(1)} %copy-done.2, f32[2,64,896]{2,1,0:T(8,128)S(1)} %bitcast.11), custom_call_target="tpu_custom_call" | custom-call | flops 1879048192 | bytes 22478848 | tf_op jit(solution)/shard_map/feedback_left/pallas_call | solution.py:53
  16.1 3.7 %forward_chunk.3 = (bf16[2,896,256]{2,1,0:T(8,128)(2,1)S(1)}, bf16[256,2048]{1,0:T(8,128)(2,1)S(1)}, f32[2,64,2048]{2,1,0:T(8,128)S(1)}) custom-call(s32[2]{0:T(128)S(1)} %pad_add_fusion.place_ref, bf16[128,2048]{1,0:T(8,128)(2,1)S(1)} %bitcast.18, bf16[128,2048]{1,0:T(8,128)(2,1)S(1)} %collective-permute-done.2.refs_1_, ...), custom_call_target="tpu_custom_call" | custom-call | flops 1879048192 | bytes 11730944 | tf_op jit(solution)/shard_map/forward_chunk/pallas_call | solution.py:53
  22.5 3.1 %copy-done.1 = bf16[2,896,2048]{2,1,0:T(8,128)(2,1)S(1)} copy-done((bf16[2,896,2048]{2,1,0:T(8,128)(2,1)S(1)}, bf16[2,896,2048]{2,1,0:T(8,128)(2,1)}, u32[]{:S(2)}) %copy-start.1) | copy-done | bytes 7340056
  25.6 5.8 %forward_chunk.4 = (bf16[2,896,512]{2,1,0:T(8,128)(2,1)S(1)}, bf16[512,2048]{1,0:T(8,128)(2,1)S(1)}, f32[2,64,2048]{2,1,0:T(8,128)S(1)}) custom-call(s32[2]{0:T(128)S(1)} %pad_add_fusion.place_ref, bf16[128,2048]{1,0:T(8,128)(2,1)S(1)} %collective-permute-done.x_ref.refs_0_, bf16[128,2048]{1,0:T(8,128)(2,1)S(1)} %collective-permute-done.5.refs_1_, ...), custom_call_target="tpu_custom_call" | custom-call | flops 3758096384 | bytes 12779520 | tf_op jit(solution)/shard_map/forward_chunk/pallas_call | solution.py:53
  33.5 3.7 %forward_chunk.5 = (bf16[2,896,256]{2,1,0:T(8,128)(2,1)S(1)}, bf16[256,2048]{1,0:T(8,128)(2,1)S(1)}, f32[2,64,2048]{2,1,0:T(8,128)S(1)}) custom-call(s32[2]{0:T(128)S(1)} %pad_add_fusion.place_ref, bf16[64,2048]{1,0:T(8,128)(2,1)S(1)} %collective-permute-done.3.refs_0_, bf16[64,2048]{1,0:T(8,128)(2,1)S(1)} %collective-permute-done.4.refs_1_, ...), custom_call_target="tpu_custom_call" | custom-call | flops 1879048192 | bytes 11730944 | tf_op jit(solution)/shard_map/forward_chunk/pallas_call | solution.py:53
  38.0 1.8 %collective-permute-done.9.got_ref = f32[64,2048]{1,0:T(8,128)S(1)} collective-permute-done((f32[64,2048]{1,0:T(8,128)S(1)}, f32[64,2048]{1,0:T(8,128)S(1)}, u32[]{:S(2)}, u32[]{:S(2)}) %collective-permute-start.9) | collective-permute-done | bytes 524320 | tf_op jit(solution)/shard_map/ppermute | solution.py:305
  43.0 1.9 %gradient.8.fb_ref = f32[2,896,2048]{2,1,0:T(8,128)S(1)} custom-call(s32[2]{0:T(128)S(1)} %pad_add_fusion.place_ref, f32[2,896,2048]{2,1,0:T(8,128)S(1)} %get-tuple-element.88.fb_ref, bf16[2,896,256]{2,1,0:T(8,128)(2,1)S(1)} %get-tuple-element.89.refs_0_, bf16[2,896,512]{2,1,0:T(8,128)(2,1)S(1)} %get-tuple-element.90.refs_1_, ...), custom_call_target="tpu_custom_call", output_to_operand_aliasing={{}: (1, {})} | custom-call | flops 939524096 | bytes 22544384 | tf_op jit(solution)/shard_map/gradient/pallas_call | solution.py:53
  44.9 1.7 %gradient.9.fb_ref = f32[2,896,2048]{2,1,0:T(8,128)S(1)} custom-call(s32[2]{0:T(128)S(1)} %pad_add_fusion.place_ref, f32[2,896,2048]{2,1,0:T(8,128)S(1)} %gradient.8.fb_ref, bf16[2,896,256]{2,1,0:T(8,128)(2,1)S(1)} %get-tuple-element.89.refs_0_, bf16[2,896,512]{2,1,0:T(8,128)(2,1)S(1)} %get-tuple-element.90.refs_1_, ...), custom_call_target="tpu_custom_call", output_to_operand_aliasing={{}: (1, {})} | custom-call | flops 939524096 | bytes 22544384 | tf_op jit(solution)/shard_map/gradient/pallas_call | solution.py:53
  55.4 2.5 %collective-permute-start.15 = (f32[32,512]{1,0:T(8,128)S(1)}, f32[32,512]{1,0:T(8,128)S(1)}, u32[]{:S(2)}, u32[]{:S(2)}) collective-permute-start(f32[32,512]{1,0:T(8,128)S(1)} %get-tuple-element.107.refs_1_), channel_id=1, source_target_pairs={{0,3},{1,2},{2,1},{3,0},{4,7},{5,6},{6,5},{7,4},{8,11},{9,10},{10,... | collective-permute-start | bytes 196616 | tf_op jit(solution)/shard_map/ppermute | solution.py:305
  57.8 1.7 %gradient.11.fb_ref = f32[2,896,2048]{2,1,0:T(8,128)S(1)} custom-call(s32[2]{0:T(128)S(1)} %pad_add_fusion.place_ref, f32[2,896,2048]{2,1,0:T(8,128)S(1)} %gradient.10.fb_ref, bf16[2,896,256]{2,1,0:T(8,128)(2,1)S(1)} %get-tuple-element.89.refs_0_, bf16[2,896,512]{2,1,0:T(8,128)(2,1)S(1)} %get-tuple-element.90.refs_1_, ...), custom_call_target="tpu_custom_call", output_to_operand_aliasing={{}: (1, {})} | custom-call | flops 939524096 | bytes 22544384 | tf_op jit(solution)/shard_map/gradient/pallas_call | solution.py:53
  59.6 2.0 %collective-permute-done.15.refs_3_ = f32[32,512]{1,0:T(8,128)S(1)} collective-permute-done((f32[32,512]{1,0:T(8,128)S(1)}, f32[32,512]{1,0:T(8,128)S(1)}, u32[]{:S(2)}, u32[]{:S(2)}) %collective-permute-start.15) | collective-permute-done | bytes 65568 | tf_op jit(solution)/shard_map/ppermute | solution.py:305
  62.1 2.5 %collective-permute-start.16 = (f32[32,512]{1,0:T(8,128)S(1)}, f32[32,512]{1,0:T(8,128)S(1)}, u32[]{:S(2)}, u32[]{:S(2)}) collective-permute-start(f32[32,512]{1,0:T(8,128)S(1)} %get-tuple-element.111.refs_0_), channel_id=1, source_target_pairs={{0,3},{1,2},{2,1},{3,0},{4,7},{5,6},{6,5},{7,4},{8,11},{9,10},{10,... | collective-permute-start | bytes 196616 | tf_op jit(solution)/shard_map/ppermute | solution.py:305
  66.5 1.8 %collective-permute-done.16.refs_2_ = f32[32,512]{1,0:T(8,128)S(1)} collective-permute-done((f32[32,512]{1,0:T(8,128)S(1)}, f32[32,512]{1,0:T(8,128)S(1)}, u32[]{:S(2)}, u32[]{:S(2)}) %collective-permute-start.16) | collective-permute-done | bytes 65568 | tf_op jit(solution)/shard_map/ppermute | solution.py:305
  81.6 1.9 %collective-permute-done.22.other_ref = f32[64,2048]{1,0:T(8,128)S(1)} collective-permute-done((f32[64,2048]{1,0:T(8,128)S(1)}, f32[64,2048]{1,0:T(8,128)S(1)}, u32[]{:S(2)}, u32[]{:S(2)}) %collective-permute-start.22) | collective-permute-done | bytes 524320 | tf_op jit(solution)/shard_map/ppermute | solution.py:305
  83.5 3.0 %project.2.refs_0_ = f32[64,896]{1,0:T(8,128)S(1)} custom-call(s32[2]{0:T(128)S(1)} %pad_add_fusion.place_ref, f32[2,896,2048]{2,1,0:T(8,128)S(1)} %gradient.15.delta_ref, f32[64,2048]{1,0:T(8,128)S(1)} %join.3.mine_ref, f32[64,2048]{1,0:T(8,128)S(1)} %collective-permute-done.22.other_ref), custom_call_target="tpu_custom_call" | custom-call | flops 939524096 | bytes 15728640 | tf_op jit(solution)/shard_map/project/pallas_call | solution.py:53
  87.3 3.0 %project.3.refs_1_ = f32[64,896]{1,0:T(8,128)S(1)} custom-call(s32[2]{0:T(128)S(1)} %pad_add_fusion.place_ref, f32[2,896,2048]{2,1,0:T(8,128)S(1)} %gradient.15.delta_ref, f32[64,2048]{1,0:T(8,128)S(1)} %join.3.mine_ref, f32[64,2048]{1,0:T(8,128)S(1)} %collective-permute-done.22.other_ref), custom_call_target="tpu_custom_call" | custom-call | flops 939524096 | bytes 15728640 | tf_op jit(solution)/shard_map/project/pallas_call | solution.py:53
  91.7 7.2 %factorize.1.inv_ref = f32[2,64,64]{2,1,0:T(8,128)S(1)} custom-call(s32[2]{0:T(128)S(1)} %pad_add_fusion.place_ref, f32[64,2048]{1,0:T(8,128)S(1)} %join.3.mine_ref, f32[64,2048]{1,0:T(8,128)S(1)} %collective-permute-done.22.other_ref), custom_call_target="tpu_custom_call" | custom-call | flops 2000000000 | bytes 1048576 | tf_op jit(solution)/shard_map/factorize/pallas_call | solution.py:53
  100.2 2.2 %collective-permute-start.25 = (f32[64,896]{1,0:T(8,128)S(1)}, f32[64,896]{1,0:T(8,128)S(1)}, u32[]{:S(2)}, u32[]{:S(2)}) collective-permute-start(f32[64,896]{1,0:T(8,128)S(1)} %get-tuple-element.129.y0_ref), channel_id=1, source_target_pairs={{0,3},{1,2},{2,1},{3,0},{4,7},{5,6},{6,5},{7,4},{8,11},{9,10},{10,... | collective-permute-start | bytes 688136 | tf_op jit(solution)/shard_map/ppermute | solution.py:305
  102.4 3.3 %collective-permute-start.26 = (f32[64,896]{1,0:T(8,128)S(1)}, f32[64,896]{1,0:T(8,128)S(1)}, u32[]{:S(2)}, u32[]{:S(2)}) collective-permute-start(f32[64,896]{1,0:T(8,128)S(1)} %get-tuple-element.130.y1_ref), channel_id=1, source_target_pairs={{0,1},{1,0},{2,3},{3,2},{4,5},{5,4},{6,7},{7,6},{8,9},{9,8},{10,11... | collective-permute-start | bytes 688136 | tf_op jit(solution)/shard_map/ppermute | solution.py:305
  107.2 3.2 %collective-permute-done.25.got0_ref = f32[64,896]{1,0:T(8,128)S(1)} collective-permute-done((f32[64,896]{1,0:T(8,128)S(1)}, f32[64,896]{1,0:T(8,128)S(1)}, u32[]{:S(2)}, u32[]{:S(2)}) %collective-permute-start.25) | collective-permute-done | bytes 229408 | tf_op jit(solution)/shard_map/ppermute | solution.py:305
  110.5 3.1 %collective-permute-done.26.got1_ref = f32[64,896]{1,0:T(8,128)S(1)} collective-permute-done((f32[64,896]{1,0:T(8,128)S(1)}, f32[64,896]{1,0:T(8,128)S(1)}, u32[]{:S(2)}, u32[]{:S(2)}) %collective-permute-start.26) | collective-permute-done | bytes 229408 | tf_op jit(solution)/shard_map/ppermute | solution.py:305
  113.6 9.5 %finish.1 = (f32[2,896,2048]{2,1,0:T(8,128)}, f32[2,896,512]{2,1,0:T(8,128)}, bf16[2,896,512]{2,1,0:T(8,128)(2,1)}, f32[2,64,896]{2,1,0:T(8,128)}) custom-call(s32[2]{0:T(128)S(1)} %pad_add_fusion.place_ref, f32[64,896]{1,0:T(8,128)S(1)} %get-tuple-element.129.y0_ref, f32[64,896]{1,0:T(8,128)S(1)} %get-tuple-element.130.y1_ref, ...), custom_call_target="tpu_custom_call" | custom-call | flops 1879048192 | bytes 28213248 | tf_op jit(solution)/shard_map/finish/pallas_call | solution.py:53
  (72 shorter events, 41.4 us)
Async XLA Ops:
  0.6 15.5 %collective-permute-start.2 = (bf16[128,2048]{1,0:T(8,128)(2,1)}, bf16[128,2048]{1,0:T(8,128)(2,1)S(1)}, u32[]{:S(2)}, u32[]{:S(2)}) collective-permute-start(bf16[128,2048]{1,0:T(8,128)(2,1)} %bitcast.15), channel_id=1, source_target_pairs={{0,4},{4,0},{8,12},{12,8},{16,20},{20,16},{24,28},{28,24},{1,5},{5... | collective-permute-start | bytes 1572872 | tf_op jit(solution)/shard_map/ppermute | solution.py:305
  1.1 18.7 %collective-permute-start.1 = (bf16[128,2048]{1,0:T(8,128)(2,1)}, bf16[128,2048]{1,0:T(8,128)(2,1)S(1)}, u32[]{:S(2)}, u32[]{:S(2)}) collective-permute-start(bf16[128,2048]{1,0:T(8,128)(2,1)} %bitcast.16), channel_id=1, source_target_pairs={{0,16},{4,20},{8,24},{12,28},{16,0},{20,4},{24,8},{28,12},{1,17},{... | collective-permute-start | bytes 1572872 | tf_op jit(solution)/shard_map/ppermute | solution.py:305
  3.7 16.1 %collective-permute-start = (bf16[128,2048]{1,0:T(8,128)(2,1)}, bf16[128,2048]{1,0:T(8,128)(2,1)S(1)}, u32[]{:S(2)}, u32[]{:S(2)}) collective-permute-start(bf16[128,2048]{1,0:T(8,128)(2,1)} %bitcast.17), channel_id=1, source_target_pairs={{0,8},{4,12},{8,0},{12,4},{16,24},{20,28},{24,16},{28,20},{1,9},{5... | collective-permute-start | bytes 1572872 | tf_op jit(solution)/shard_map/ppermute | solution.py:305
  19.8 2.0 %collective-permute-start.5 = (bf16[128,2048]{1,0:T(8,128)(2,1)S(1)}, bf16[128,2048]{1,0:T(8,128)(2,1)S(1)}, u32[]{:S(2)}, u32[]{:S(2)}) collective-permute-start(bf16[128,2048]{1,0:T(8,128)(2,1)S(1)} %collective-permute-done.x_ref.refs_0_), channel_id=1, source_target_pairs={{0,4},{4,0},{8,12},{12,8},{16,20},{20,16},{24,28},{28,24},{1,5},{5... | collective-permute-start | bytes 1572872 | tf_op jit(solution)/shard_map/ppermute | solution.py:305
  19.9 2.6 %collective-permute-start.6 = (bf16[128,2048]{1,0:T(8,128)(2,1)S(1)}, bf16[128,2048]{1,0:T(8,128)(2,1)S(1)}, u32[]{:S(2)}, u32[]{:S(2)}) collective-permute-start(bf16[128,2048]{1,0:T(8,128)(2,1)S(1)} %collective-permute-done.1.y_ref.refs_2_), channel_id=1, source_target_pairs={{0,4},{4,0},{8,12},{12,8},{16,20},{20,16},{24,28},{28,24},{1,5},{5... | collective-permute-start | bytes 1572872 | tf_op jit(solution)/shard_map/ppermute | solution.py:305
  21.0 10.5 %collective-permute-start.3 = (bf16[64,2048]{1,0:T(8,128)(2,1)S(1)}, bf16[64,2048]{1,0:T(8,128)(2,1)S(1)}, u32[]{:S(2)}, u32[]{:S(2)}) collective-permute-start(bf16[64,2048]{1,0:T(8,128)(2,1)S(1)} %get-tuple-element.76), channel_id=1, source_target_pairs={{0,16},{4,20},{8,24},{12,28},{16,0},{20,4},{24,8},{28,12},{1,17},{... | collective-permute-start | bytes 786440 | tf_op jit(solution)/shard_map/ppermute | solution.py:305
  21.6 9.9 %collective-permute-start.4 = (bf16[64,2048]{1,0:T(8,128)(2,1)S(1)}, bf16[64,2048]{1,0:T(8,128)(2,1)S(1)}, u32[]{:S(2)}, u32[]{:S(2)}) collective-permute-start(bf16[64,2048]{1,0:T(8,128)(2,1)S(1)} %get-tuple-element.77), channel_id=1, source_target_pairs={{0,8},{4,12},{8,0},{12,4},{16,24},{20,28},{24,16},{28,20},{1,9},{5... | collective-permute-start | bytes 786440 | tf_op jit(solution)/shard_map/ppermute | solution.py:305
  40.4 6.2 %collective-permute-start.10 = (f32[32,1024]{1,0:T(8,128)S(1)}, f32[32,1024]{1,0:T(8,128)S(1)}, u32[]{:S(2)}, u32[]{:S(2)}) collective-permute-start(f32[32,1024]{1,0:T(8,128)S(1)} %get-tuple-element.86), channel_id=1, source_target_pairs={{0,8},{4,12},{8,0},{12,4},{16,24},{20,28},{24,16},{28,20},{1,9},{5... | collective-permute-start | bytes 393224 | tf_op jit(solution)/shard_map/ppermute | solution.py:305
  41.5 5.3 %collective-permute-start.11 = (f32[32,1024]{1,0:T(8,128)S(1)}, f32[32,1024]{1,0:T(8,128)S(1)}, u32[]{:S(2)}, u32[]{:S(2)}) collective-permute-start(f32[32,1024]{1,0:T(8,128)S(1)} %get-tuple-element.87), channel_id=1, source_target_pairs={{0,16},{4,20},{8,24},{12,28},{16,0},{20,4},{24,8},{28,12},{1,17},{... | collective-permute-start | bytes 393224 | tf_op jit(solution)/shard_map/ppermute | solution.py:305
  47.3 4.3 %collective-permute-start.12 = (f32[32,512]{1,0:T(8,128)S(1)}, f32[32,512]{1,0:T(8,128)S(1)}, u32[]{:S(2)}, u32[]{:S(2)}) collective-permute-start(f32[32,512]{1,0:T(8,128)S(1)} %get-tuple-element.99), channel_id=1, source_target_pairs={{0,16},{4,20},{8,24},{12,28},{16,0},{20,4},{24,8},{28,12},{1,17},{... | collective-permute-start | bytes 196616 | tf_op jit(solution)/shard_map/ppermute | solution.py:305
  48.9 4.3 %collective-permute-start.13 = (f32[32,512]{1,0:T(8,128)S(1)}, f32[32,512]{1,0:T(8,128)S(1)}, u32[]{:S(2)}, u32[]{:S(2)}) collective-permute-start(f32[32,512]{1,0:T(8,128)S(1)} %get-tuple-element.100), channel_id=1, source_target_pairs={{0,8},{4,12},{8,0},{12,4},{16,24},{20,28},{24,16},{28,20},{1,9},{5... | collective-permute-start | bytes 196616 | tf_op jit(solution)/shard_map/ppermute | solution.py:305
  53.7 5.8 %collective-permute-start.14 = (f32[32,512]{1,0:T(8,128)S(1)}, f32[32,512]{1,0:T(8,128)S(1)}, u32[]{:S(2)}, u32[]{:S(2)}) collective-permute-start(f32[32,512]{1,0:T(8,128)S(1)} %get-tuple-element.106.refs_0_), channel_id=1, source_target_pairs={{0,1},{1,0},{2,3},{3,2},{4,5},{5,4},{6,7},{7,6},{8,9},{9,8},{10,11... | collective-permute-start | bytes 196616 | tf_op jit(solution)/shard_map/ppermute | solution.py:305
  55.4 6.2 %collective-permute-start.15 = (f32[32,512]{1,0:T(8,128)S(1)}, f32[32,512]{1,0:T(8,128)S(1)}, u32[]{:S(2)}, u32[]{:S(2)}) collective-permute-start(f32[32,512]{1,0:T(8,128)S(1)} %get-tuple-element.107.refs_1_), channel_id=1, source_target_pairs={{0,3},{1,2},{2,1},{3,0},{4,7},{5,6},{6,5},{7,4},{8,11},{9,10},{10,... | collective-permute-start | bytes 196616 | tf_op jit(solution)/shard_map/ppermute | solution.py:305
  62.1 6.1 %collective-permute-start.16 = (f32[32,512]{1,0:T(8,128)S(1)}, f32[32,512]{1,0:T(8,128)S(1)}, u32[]{:S(2)}, u32[]{:S(2)}) collective-permute-start(f32[32,512]{1,0:T(8,128)S(1)} %get-tuple-element.111.refs_0_), channel_id=1, source_target_pairs={{0,3},{1,2},{2,1},{3,0},{4,7},{5,6},{6,5},{7,4},{8,11},{9,10},{10,... | collective-permute-start | bytes 196616 | tf_op jit(solution)/shard_map/ppermute | solution.py:305
  64.6 4.3 %collective-permute-start.17 = (f32[32,512]{1,0:T(8,128)S(1)}, f32[32,512]{1,0:T(8,128)S(1)}, u32[]{:S(2)}, u32[]{:S(2)}) collective-permute-start(f32[32,512]{1,0:T(8,128)S(1)} %get-tuple-element.112.refs_1_), channel_id=1, source_target_pairs={{0,1},{1,0},{2,3},{3,2},{4,5},{5,4},{6,7},{7,6},{8,9},{9,8},{10,11... | collective-permute-start | bytes 196616 | tf_op jit(solution)/shard_map/ppermute | solution.py:305
  69.5 4.7 %collective-permute-start.18 = (f32[32,512]{1,0:T(8,128)S(1)}, f32[32,512]{1,0:T(8,128)S(1)}, u32[]{:S(2)}, u32[]{:S(2)}) collective-permute-start(f32[32,512]{1,0:T(8,128)S(1)} %get-tuple-element.116.a0), channel_id=1, source_target_pairs={{0,16},{4,20},{8,24},{12,28},{16,0},{20,4},{24,8},{28,12},{1,17},{... | collective-permute-start | bytes 196616 | tf_op jit(solution)/shard_map/ppermute | solution.py:305
  70.1 4.3 %collective-permute-start.19 = (f32[32,512]{1,0:T(8,128)S(1)}, f32[32,512]{1,0:T(8,128)S(1)}, u32[]{:S(2)}, u32[]{:S(2)}) collective-permute-start(f32[32,512]{1,0:T(8,128)S(1)} %get-tuple-element.117.a1), channel_id=1, source_target_pairs={{0,8},{4,12},{8,0},{12,4},{16,24},{20,28},{24,16},{28,20},{1,9},{5... | collective-permute-start | bytes 196616 | tf_op jit(solution)/shard_map/ppermute | solution.py:305
  74.9 5.5 %collective-permute-start.20 = (f32[32,1024]{1,0:T(8,128)S(1)}, f32[32,1024]{1,0:T(8,128)S(1)}, u32[]{:S(2)}, u32[]{:S(2)}) collective-permute-start(f32[32,1024]{1,0:T(8,128)S(1)} %get-tuple-element.121.a0), channel_id=1, source_target_pairs={{0,8},{4,12},{8,0},{12,4},{16,24},{20,28},{24,16},{28,20},{1,9},{5... | collective-permute-start | bytes 393224 | tf_op jit(solution)/shard_map/ppermute | solution.py:305
  76.0 5.0 %collective-permute-start.21 = (f32[32,1024]{1,0:T(8,128)S(1)}, f32[32,1024]{1,0:T(8,128)S(1)}, u32[]{:S(2)}, u32[]{:S(2)}) collective-permute-start(f32[32,1024]{1,0:T(8,128)S(1)} %get-tuple-element.122.a1), channel_id=1, source_target_pairs={{0,16},{4,20},{8,24},{12,28},{16,0},{20,4},{24,8},{28,12},{1,17},{... | collective-permute-start | bytes 393224 | tf_op jit(solution)/shard_map/ppermute | solution.py:305
  81.6 2.0 %collective-permute-start.22 = (f32[64,2048]{1,0:T(8,128)S(1)}, f32[64,2048]{1,0:T(8,128)S(1)}, u32[]{:S(2)}, u32[]{:S(2)}) collective-permute-start(f32[64,2048]{1,0:T(8,128)S(1)} %join.3.mine_ref), channel_id=1, source_target_pairs={{0,4},{4,0},{8,12},{12,8},{16,20},{20,16},{24,28},{28,24},{1,5},{5... | collective-permute-start | bytes 1572872 | tf_op jit(solution)/shard_map/ppermute | solution.py:305
  86.5 12.3 %collective-permute-start.23 = (f32[64,896]{1,0:T(8,128)S(1)}, f32[64,896]{1,0:T(8,128)S(1)}, u32[]{:S(2)}, u32[]{:S(2)}) collective-permute-start(f32[64,896]{1,0:T(8,128)S(1)} %project.2.refs_0_), channel_id=1, source_target_pairs={{0,1},{1,0},{2,3},{3,2},{4,5},{5,4},{6,7},{7,6},{8,9},{9,8},{10,11... | collective-permute-start | bytes 688136 | tf_op jit(solution)/shard_map/ppermute | solution.py:305
  90.2 9.3 %collective-permute-start.24 = (f32[64,896]{1,0:T(8,128)S(1)}, f32[64,896]{1,0:T(8,128)S(1)}, u32[]{:S(2)}, u32[]{:S(2)}) collective-permute-start(f32[64,896]{1,0:T(8,128)S(1)} %project.3.refs_1_), channel_id=1, source_target_pairs={{0,3},{1,2},{2,1},{3,0},{4,7},{5,6},{6,5},{7,4},{8,11},{9,10},{10,... | collective-permute-start | bytes 688136 | tf_op jit(solution)/shard_map/ppermute | solution.py:305
  100.2 10.3 %collective-permute-start.25 = (f32[64,896]{1,0:T(8,128)S(1)}, f32[64,896]{1,0:T(8,128)S(1)}, u32[]{:S(2)}, u32[]{:S(2)}) collective-permute-start(f32[64,896]{1,0:T(8,128)S(1)} %get-tuple-element.129.y0_ref), channel_id=1, source_target_pairs={{0,3},{1,2},{2,1},{3,0},{4,7},{5,6},{6,5},{7,4},{8,11},{9,10},{10,... | collective-permute-start | bytes 688136 | tf_op jit(solution)/shard_map/ppermute | solution.py:305
  102.4 11.2 %collective-permute-start.26 = (f32[64,896]{1,0:T(8,128)S(1)}, f32[64,896]{1,0:T(8,128)S(1)}, u32[]{:S(2)}, u32[]{:S(2)}) collective-permute-start(f32[64,896]{1,0:T(8,128)S(1)} %get-tuple-element.130.y1_ref), channel_id=1, source_target_pairs={{0,1},{1,0},{2,3},{3,2},{4,5},{5,4},{6,7},{7,6},{8,9},{9,8},{10,11... | collective-permute-start | bytes 688136 | tf_op jit(solution)/shard_map/ppermute | solution.py:305
  (10 other events, 58.7 us)
where the time goes:
time: 124 us; the launch traced here: 123 us
  Pallas kernels  63.5 us (51%)
  starting transfers between devices  29.6 us (24%)
  waiting for transfers between devices  21.8 us (18%)
  local copies, waits for them, and re-layouts  7.2 us (6%)
    pallas_call x27, Pallas kernels, call(): pl.pallas_call(body, out_shape=out_shape, compiler_params=pltpu.CompilerP...  63.5 us
    ppermute x27, starting transfers between devices, swap(): return lax.ppermute(x, axis, [(i, i ^ mask) for i in range(size)])  29.6 us
    ppermute x27, waiting for transfers between devices, swap(): return lax.ppermute(x, axis, [(i, i ^ mask) for i in range(size)])  21.8 us
    unnamed x14, local copies, waits for them, and re-layouts  7.2 us
  transfers between devices with their start and end apart: 27, of which 18 were waited for; matrix products, arithmetic and copies ran while one was open for 0% of the time, Pallas kernels for 34%

commit v1 on v0

v1 whole, which is shorter than its diff:
```python
import jax
import jax.numpy as jnp
from jax import lax
from jax.experimental import pallas as pl
from jax.experimental.pallas import tpu as pltpu
from jax.sharding import PartitionSpec as P

momentum_decay = 0.9
step_rate = 0.05
highest = lax.Precision.HIGHEST
f32 = jnp.float32
bf16 = jnp.bfloat16
contract_last = (((1,), (1,)), ((), ()))
MIB = 1024 * 1024
vmem = pl.BlockSpec(memory_space=pltpu.VMEM)
smem = pl.BlockSpec(memory_space=pltpu.SMEM)
anywhere = pl.BlockSpec(memory_space=pl.ANY)
hbm = pl.BlockSpec(memory_space=pltpu.HBM)


def kept(like):
    return pltpu.VMEM(like.shape, like.dtype)


def in_vmem(x):
    return pltpu.with_memory_space_constraint(x, pltpu.VMEM)


def in_hbm(x):
    return pltpu.with_memory_space_constraint(x, pltpu.HBM)


def split2(x):
    hi = x.astype(bf16)
    return hi, (x - hi.astype(f32)).astype(bf16)


def stacked(x):
    return jnp.concatenate(split2(x), 0)


def fold(x):
    half = x.shape[0] // 2
    return x[:half] + x[half:]


def dot(a, b):
    return jnp.dot(a, b, preferred_element_type=f32)


def dot_nt(a, b):
    return lax.dot_general(a, b, contract_last, preferred_element_type=f32)


def shape(*dims, dtype=f32):
    return jax.ShapeDtypeStruct(dims, dtype)


def call(body, place, operands, out_shape, mib, macs=0, **more):
    nbytes = sum(x.size * x.dtype.itemsize for x in operands)
    spec = dict(
        in_specs=[smem] + [vmem] * len(operands),
        out_specs=jax.tree.map(lambda _: vmem, out_shape),
    ) | more
    return pl.pallas_call(
        body,
        out_shape=out_shape,
        compiler_params=pltpu.CompilerParams(vmem_limit_bytes=mib * MIB),
        cost_estimate=pl.CostEstimate(flops=2 * macs, bytes_accessed=nbytes, transcendentals=0),
        **spec,
    )(place, *operands)


def divisor(size, most, unit):
    return max(b for b in range(unit, min(size, most) + 1, unit) if size % b == 0)


def span(i, size):
    return pl.ds(pl.multiple_of(i * size, size), size)


def grant(total, feats):
    return 14 if total * feats <= 4 * MIB else 28


def feedback_left(place, feedback, right_t):
    _, rows, feats = feedback.shape
    rank = right_t.shape[1]
    block = 512
    steps = feats // block

    def body(place_ref, fb_ref, r_ref, held_ref, out_ref, sems):
        def copy(k, d):
            cols = slice(d * block, (d + 1) * block)
            return pltpu.make_async_copy(
                fb_ref.at[k, :, cols], held_ref.at[k, :, cols], sems.at[k, d]
            )

        order = [(k, d) for k in range(2) for d in range(steps)]
        for k, d in order:
            copy(k, d).start()
        for k, d in order:
            cols = slice(d * block, (d + 1) * block)
            r_cat = stacked(r_ref[k])
            copy(k, d).wait()
            fb_hi, fb_lo = split2(held_ref[k, :, cols])
            out_ref[k, :, cols] = fold(dot(r_cat, fb_hi)) + dot(r_cat[:rank], fb_lo)

    return call(
        body, place, (in_hbm(feedback), right_t), [kept(feedback), shape(2, rank, feats)], 10,
        2 * rows * feats * 256, name="feedback_left", in_specs=[smem, hbm, vmem],
        scratch_shapes=[pltpu.SemaphoreType.DMA((2, steps))],
    )


def left_part(right, grad, tok):
    return fold(dot(stacked(fold(dot(stacked(right), grad))), tok))


def forward_chunk(place, parts, offsets, weight, upstream, right_t, left_in, last=False):
    count = len(parts)
    feats = parts[0].shape[1]
    width = sum(p.shape[0] for p in parts)
    per = width // len(offsets)
    rows = weight.shape[1]
    rank = right_t.shape[1]

    def body(place_ref, *refs):
        tok_refs, refs = refs[:count], refs[count:]
        w_ref, up_ref, r_ref, left_ref, grad_ref, tok_ref, left_out = refs
        me = place_ref[0]
        at = 0
        for t in tok_refs:
            tok_ref[at : at + t.shape[0], :] = t[...]
            at += t.shape[0]
        gate_pre = dot_nt(w_ref[0], tok_ref[...])
        up_pre = dot_nt(w_ref[1], tok_ref[...])
        cot = jnp.concatenate([up_ref[:, span(me ^ o, per)] for o in offsets], 1).astype(f32)
        s = jax.nn.sigmoid(gate_pre)
        cot_s = cot * s
        grad_ref[0] = (cot_s * up_pre * (1.0 + gate_pre * (1.0 - s))).astype(bf16)
        grad_ref[1] = (cot_s * gate_pre).astype(bf16)
        if last:
            k = (me & 1) ^ 1
            left_out[...] = left_ref[k] + left_part(r_ref[k], grad_ref[k], tok_ref[...])
        else:
            for k in range(2):
                left_out[k] = left_ref[k] + left_part(r_ref[k], grad_ref[k], tok_ref[...])

    return call(
        body, place, (*parts, weight, upstream, right_t, left_in),
        [
            shape(2, rows, width, dtype=bf16), shape(width, feats, dtype=bf16),
            shape(rank, feats) if last else shape(2, rank, feats),
        ],
        grant(width, feats), 2 * rows * feats * width, name="forward_chunk",
    )


def keep_left(place, right_t, grad, tok, left_in):
    _, rank, feats = left_in.shape

    def body(place_ref, r_ref, g_ref, t_ref, left_ref, out_ref):
        k = place_ref[0] & 1
        out_ref[...] = left_ref[k] + left_part(r_ref[k], g_ref[k], t_ref[...])

    return call(
        body, place, (right_t, grad, tok, left_in), shape(rank, feats), 8,
        grad.size * rank, name="keep_left",
    )


def gradient(place, delta, grads, toks, start, stop):
    _, rows, feats = delta.shape
    total = sum(t.shape[0] for t in toks)
    block = 256
    count = len(toks)

    def body(place_ref, fb_ref, *refs):
        for at in range(start, stop, block):
            cols = slice(at, at + block)
            for k in range(2):
                acc = fb_ref[k, :, cols]
                for g, t in zip(refs[:count], refs[count : 2 * count]):
                    acc = acc + dot(g[k], t[:, cols])
                refs[2 * count][k, :, cols] = acc

    return call(
        body, place, (in_vmem(delta), *grads, *toks), kept(delta),
        min(8, grant(total // 2, feats)), 2 * rows * (stop - start) * total,
        name="gradient", input_output_aliases={1: 0},
    )


def project(place, delta, left_t, flip, scale):
    _, rows, feats = delta.shape
    rank = left_t.shape[0]
    block = 512

    def body(place_ref, delta_ref, left_ref, *outs):
        k = (place_ref[0] & 1) ^ flip
        acc = None
        for d in range(feats // block):
            cols = slice(d * block, (d + 1) * block)
            cat = stacked(left_ref[:, cols] * scale)
            hi, lo = split2(delta_ref[k, :, cols])
            part = fold(dot_nt(cat, hi)) + dot_nt(cat[:rank], lo)
            acc = part if acc is None else acc + part
        outs[0][...] = acc[: rank // 2]
        outs[1][...] = acc[rank // 2 :]

    return call(
        body, place, (in_vmem(delta), left_t), [shape(rank // 2, rows)] * 2, 8, rows * feats * 256,
        name="project",
    )


def factorize(place, mine, other, scale):
    rank, feats = mine.shape

    def body(place_ref, mine_ref, other_ref, inv_ref):
        core = place_ref[0] & 1
        row_id = lax.broadcasted_iota(jnp.int32, (rank, 2 * rank), 0)
        eye = (
            lax.broadcasted_iota(jnp.int32, (rank, rank), 0)
            == lax.broadcasted_iota(jnp.int32, (rank, rank), 1)
        ).astype(f32)
        work, roots = [], []
        for k in range(2):
            x = jnp.where(core == k, mine_ref[...], other_ref[...]) * scale
            gram = lax.dot_general(x, x, contract_last, precision=highest, preferred_element_type=f32)
            work.append(jnp.concatenate([gram, eye], 1))
            roots.append(jnp.zeros((rank, 2 * rank), f32))
        group = 4
        for first in range(0, rank, group):
            for k in range(2):
                a = work[k]
                columns = [
                    jnp.broadcast_to(a[:, j : j + 1], a.shape) for j in range(first, first + group)
                ]
                for t in range(group):
                    j = first + t
                    pivot = columns[t][j : j + 1, :]
                    ratio = jnp.where(row_id > j, columns[t] * (1.0 / pivot), 0.0)
                    for u in range(t + 1, group):
                        columns[u] = columns[u] - ratio * columns[u][j : j + 1, :]
                    roots[k] = jnp.where(row_id == j, lax.rsqrt(pivot), roots[k])
                    a = a - ratio * a[j : j + 1, :]
                work[k] = a
        for k in range(2):
            inv_ref[k] = (work[k] * roots[k])[:, rank:]

    return call(
        body, place, (mine, other), shape(2, rank, rank), 8, 1000000000, name="factorize"
    )


def make_basis(place, mine, other, inverse, scale):
    rank, feats = mine.shape

    def body(place_ref, mine_ref, other_ref, inv_ref, cat_ref):
        core = place_ref[0] & 1
        for k in range(2):
            x = jnp.where(core == k, mine_ref[...], other_ref[...]) * scale
            basis = jnp.dot(inv_ref[k], x, precision=highest, preferred_element_type=f32)
            b_hi, b_lo = split2(basis)
            cat_ref[k] = jnp.concatenate([b_hi, b_lo, b_hi], 0)

    return call(
        body, place, (mine, other, inverse), shape(2, 3 * rank, feats, dtype=bf16), 8, 500000000,
        name="make_basis",
    )


def finish(place, ys, gots, inverse, basis_cat, delta, momentum, weight, replicas, flip, outs):
    _, rows, feats = delta.shape
    rank = inverse.shape[1]
    cols = momentum.shape[2]
    block = divisor(rows, 128, 16)
    steps = rows // block
    slots = min(4, steps)
    held = () if outs is None else tuple(outs)

    def body(
        place_ref, y0_ref, y1_ref, got0_ref, got1_ref, inv_ref, cat_ref, delta_ref, mom_ref, w_ref, *refs
    ):
        fb_out, mom_out, w_out, rn_out = refs[len(held) : len(held) + 4]
        rn_t, rn_cat, fb_slot, mom_slot, w_slot, sems, rn_sem = refs[len(held) + 4 :]
        slab = span(place_ref[1], cols)
        k = (place_ref[0] & 1) ^ flip
        mean = jnp.concatenate([y0_ref[...] + got0_ref[...], y1_ref[...] + got1_ref[...]], 0)
        rn_t[...] = jnp.dot(
            inv_ref[k], mean * (1.0 / replicas), precision=highest, preferred_element_type=f32
        )
        rn_copy = pltpu.make_async_copy(rn_t, rn_out.at[k], rn_sem)
        rn_copy.start()
        hi, lo = split2(rn_t[...].T)
        rn_cat[...] = jnp.concatenate([hi, hi, lo], 1)

        def copies(i):
            at, slot = slice(i * block, (i + 1) * block), i % slots
            return [
                pltpu.make_async_copy(src.at[slot], dst.at[k, at, :], sems.at[j, slot])
                for j, (src, dst) in enumerate(
                    ((fb_slot, fb_out), (mom_slot, mom_out), (w_slot, w_out))
                )
            ]

        for i in range(steps):
            at, slot = slice(i * block, (i + 1) * block), i % slots
            if i >= slots:
                for c in copies(i - slots):
                    c.wait()
            part = rn_cat[at, :]
            fb_slot[slot] = delta_ref[k, at, :] - dot(part, cat_ref[k])
            mom = momentum_decay * mom_ref[k, at, :] + dot(part, cat_ref[k, :, slab])
            mom_slot[slot] = mom
            w_slot[slot] = (w_ref[k, at, slab].astype(f32) - step_rate * mom).astype(bf16)
            for c in copies(i):
                c.start()
        for i in range(steps - slots, steps):
            for c in copies(i):
                c.wait()
        rn_copy.wait()

    operands = (*ys, *gots, inverse, basis_cat, in_vmem(delta), momentum, weight)
    return call(
        body, place, (*operands, *held),
        [
            shape(2, rows, feats), shape(2, rows, cols),
            shape(2, rows, cols, dtype=bf16), shape(2, rank, rows),
        ],
        10, rows * feats * 256, name="finish",
        in_specs=[smem] + [vmem] * len(operands) + [hbm] * len(held),
        out_specs=[hbm] * 4,
        input_output_aliases={1 + len(operands) + i: i for i in range(len(held))},
        scratch_shapes=[
            pltpu.VMEM((rank, rows), f32),
            pltpu.VMEM((rows, 3 * rank), bf16),
            pltpu.VMEM((slots, block, feats), f32),
            pltpu.VMEM((slots, block, cols), f32),
            pltpu.VMEM((slots, block, cols), bf16),
            pltpu.SemaphoreType.DMA((3, slots)),
            pltpu.SemaphoreType.DMA,
        ],
    )


def swap(x, axis, mask):
    size = lax.axis_size(axis)
    return lax.ppermute(x, axis, [(i, i ^ mask) for i in range(size)])


def after(x, *others):
    return lax.optimization_barrier((x, *others))[0]


def has(place_ref, mask):
    return (place_ref[0] & mask) != 0


def tree(terms):
    while len(terms) > 1:
        terms = [a + b for a, b in zip(terms[::2], terms[1::2])]
    return terms[0]


def add(place, terms):
    def body(place_ref, *refs):
        refs[-1][...] = tree([r[...] for r in refs[:-1]])

    return call(body, place, terms, shape(*terms[0].shape), 4, name="add")


def add_pairs(place, ours, gots):
    count = len(ours)

    def body(place_ref, *refs):
        for j in range(count):
            refs[2 * count + j][...] = refs[j][...] + refs[count + j][...]

    out = [shape(*x.shape) for x in ours]
    return call(body, place, (*ours, *gots), out, 4, name="add_pairs")


def part_of(place_ref, mask=0):
    return (place_ref[0] ^ mask) // 2


def add_cores(place, keep, got, parts):
    rank, feats = keep.shape
    width = feats // parts

    def body(place_ref, keep_ref, got_ref, *outs):
        for m, out in enumerate(outs):
            cols = span(part_of(place_ref, 2 * m), width)
            out[...] = keep_ref[:, cols] + got_ref[:, cols]

    return call(body, place, (keep, got), [shape(rank, width)] * parts, 4, name="add_cores")


def join(place, pieces):
    rank, width = pieces[0].shape

    def body(place_ref, *refs):
        for m, piece in enumerate(refs[:-1]):
            refs[-1][:, span(part_of(place_ref, 2 * m), width)] = piece[...]

    return call(body, place, pieces, shape(rank, width * len(pieces)), 4, name="join")


def left_total(place, keep, got, work):
    fsdp, rep = lax.axis_size("fsdp"), lax.axis_size("rep")
    parts = fsdp // 2

    def beside(sends, axis, masks, i):
        got = [swap(x, axis, m) for x, m in zip(sends, masks)]
        return list(lax.optimization_barrier((*got, work(sends, i)))[:-1])

    far = range(2, fsdp, 2)
    mine, *sends = add_cores(place, keep, got, parts)
    mine = add(place, [mine] + beside(sends, "fsdp", far, 0))
    mine = add(place, [mine] + beside([mine] * (rep - 1), "rep", range(1, rep), 1))
    mine = join(place, [mine] + beside([mine] * (parts - 1), "fsdp", far, 2))
    return mine, swap(mine, "fsdp", 1)


def per_device(tokens, upstream, weight, feedback, momentum, right_factor):
    fsdp, replicas = lax.axis_size("fsdp"), lax.axis_size("rep")
    place = jnp.stack([lax.axis_index("fsdp"), lax.axis_index("rep")]).astype(jnp.int32)
    own = tokens[0]
    per, feats = own.shape
    inner = [1 << b for b in range(fsdp.bit_length() - 3)]
    far_x, far_y = fsdp // 4, fsdp // 2
    right_t = jnp.swapaxes(right_factor, 1, 2)
    scale = 1.0 / replicas

    def gather_inner(parts, base):
        parts, offsets = list(parts), [base]
        for m in inner:
            parts = parts + [swap(p, "fsdp", m) for p in parts]
            offsets = offsets + [o ^ m for o in offsets]
        return parts, offsets

    def halves(x, y):
        def body(place_ref, x_ref, y_ref, x_out, y_out):
            x_out[...] = x_ref[: per // 2, :]
            y_out[...] = y_ref[per // 2 :, :]

        return call(body, place, (x, y), [shape(per // 2, feats, dtype=bf16)] * 2, 4, name="halves")

    grads, toks = [], []

    def forward(parts, offsets, left, last=False):
        grad, tok, left = forward_chunk(
            place, parts, offsets, weight, upstream[0], right_t, left, last
        )
        grads.append(grad)
        toks.append(tok)
        return left

    got_x = swap(own, "fsdp", far_x)
    got_y = swap(own, "fsdp", far_y)
    parts, offsets = gather_inner([own], 0)
    delta, left_t = feedback_left(place, feedback[0], right_t)
    left_t = forward(parts, offsets, left_t)
    got_x, got_y, left_t = lax.optimization_barrier((got_x, got_y, left_t))
    send_x, send_y = halves(got_x, got_y)
    far = [swap(send_x, "fsdp", far_y), swap(send_y, "fsdp", far_x)]
    parts_x, offsets_x = gather_inner([got_x], far_x)
    parts_y, offsets_y = gather_inner([got_y], far_y)
    left_t = forward(parts_x + parts_y, offsets_x + offsets_y, left_t)
    far_0, far_1, left_t = lax.optimization_barrier((*far, left_t))
    parts, offsets = gather_inner([far_0, far_1], far_x ^ far_y)
    got = swap(forward(parts, offsets, left_t, last=True), "fsdp", 1)
    keep = keep_left(place, right_t, grads[-1], toks[-1], left_t)

    cuts = [0, feats // 4, 3 * feats // 4, feats]

    def work(sends, i):
        nonlocal delta
        delta = gradient(place, after(delta, *sends), grads, toks, cuts[i], cuts[i + 1])
        return delta

    mine, other = left_total(place, keep, got, work)
    masks = [(2 << b) - 1 for b in range(replicas.bit_length() - 1)]
    orders = list(zip(masks, masks[::-1]))
    last = len(orders) - 1

    def exchange(bands, step):
        return [swap(x, "rep", m) for x, m in zip(bands, orders[step])]

    y_a = project(place, delta, mine, 0, scale)
    y_b = None
    for t in range(last + 1):
        got_a = exchange(y_a, t)
        if t == 0:
            y_b = project(place, delta, after(other, *y_a), 1, scale)
        got_b = exchange(y_b, t)
        if t == 0:
            inverse = factorize(place, after(mine, *y_b), other, scale)
            *got, inverse = lax.optimization_barrier((*got_a, *got_b, inverse))
            got_a, got_b = got[:2], got[2:]
        if t < last:
            y_a = add_pairs(place, y_a, got_a)
            y_b = add_pairs(place, y_b, got_b)
    basis_cat = make_basis(place, after(mine, *y_a, *y_b), other, inverse, scale)
    common = inverse, basis_cat, delta, momentum, weight, replicas
    *done, rn_t = finish(place, y_a, got_a, *common, 0, None)
    *got_b, rn_t = lax.optimization_barrier((*got_b, rn_t))
    feedback_next, momentum_next, weight_next, rn_t = finish(
        place, y_b, got_b, *common, 1, (*done, rn_t)
    )
    return (feedback_next[None], momentum_next, weight_next, jnp.swapaxes(rn_t, 1, 2))


def solution(mesh):
    placed = (
        P("rep", "fsdp", None),
        P("rep", "fsdp", None),
        P(None, "fsdp", None),
        P("rep", None, "fsdp", None),
        P(None, "fsdp", "rep"),
        P(None, "fsdp", None),
    )
    return jax.shard_map(
        per_device,
        mesh=mesh,
        in_specs=placed,
        out_specs=(
            P("rep", None, "fsdp", None),
            P(None, "fsdp", "rep"),
            P(None, "fsdp", "rep"),
            P(None, "fsdp", None),
        ),
        check_vma=False,
    )
```

time: 124 us -> 108 us (0.87)
  local copies, waits for them, and re-layouts: 7.2 us -> 1.41 us
  Pallas kernels: 63.5 us -> 58 us
  waiting for transfers between devices: 21.8 us -> 17.6 us
    unnamed x14, local copies, waits for them, and re-layouts: 7.2 us -> 1.41 us
    pallas_call x27 -> x21, Pallas kernels: 63.5 us -> 58 us  [call(): pl.pallas_call(body, out_shape=out_shape, compiler_params=pltpu.CompilerP...]
    ppermute x27 -> x28, waiting for transfers between devices: 21.8 us -> 17.6 us  [swap(): return lax.ppermute(x, axis, [(i, i ^ mask) for i in range(size)])]
    ppermute x27 -> x28, starting transfers between devices: 29.6 us -> 29.7 us  [swap(): return lax.ppermute(x, axis, [(i, i ^ mask) for i in range(size)])]
  transfers between devices with their start and end apart: 27 -> 28, of which waited for: 18 -> 14; matrix products, arithmetic and copies ran while one was open for 0% -> 0% of each run, Pallas kernels for 34% -> 43%
where the time goes in v1:
time: 108 us
  Pallas kernels  58 us (54%)
  starting transfers between devices  29.7 us (28%)
  waiting for transfers between devices  17.6 us (16%)
  local copies, waits for them, and re-layouts  1.41 us (1%)
  between operations  1.09 us (1%)
    pallas_call x21, Pallas kernels, call(): pl.pallas_call(body, out_shape=out_shape, compiler_params=pltpu.CompilerP...  58 us
    ppermute x28, starting transfers between devices, swap(): return lax.ppermute(x, axis, [(i, i ^ mask) for i in range(size)])  29.7 us
    ppermute x28, waiting for transfers between devices, swap(): return lax.ppermute(x, axis, [(i, i ^ mask) for i in range(size)])  17.6 us
  transfers between devices with their start and end apart: 28, of which 14 were waited for; matrix products, arithmetic and copies ran while one was open for 0% of the time, Pallas kernels for 43%

profile of v1, /device:TPU:0, one launch (start us, length us, event | category | flops | bytes accessed | tf_op | source)
XLA Modules:
  0.0 107.8 jit_solution(12084396193210154854)
XLA Ops:
  1.1 2.6 %collective-permute-start.1 = (bf16[128,2048]{1,0:T(8,128)(2,1)}, bf16[128,2048]{1,0:T(8,128)(2,1)S(1)}, u32[]{:S(2)}, u32[]{:S(2)}) collective-permute-start(bf16[128,2048]{1,0:T(8,128)(2,1)} %bitcast.19), channel_id=1, source_target_pairs={{0,16},{4,20},{8,24},{12,28},{16,0},{20,4},{24,8},{28,12},{1,17},{... | collective-permute-start | bytes 1572872 | tf_op jit(solution)/shard_map/ppermute | solution.py:351
  6.5 6.9 %feedback_left.1 = (f32[2,896,2048]{2,1,0:T(8,128)S(1)}, f32[2,64,2048]{2,1,0:T(8,128)S(1)}) custom-call(s32[2]{0:T(128)S(1)} %pad_add_fusion.place_ref, f32[2,896,2048]{2,1,0:T(8,128)} %bitcast.22, f32[2,64,896]{2,1,0:T(8,128)S(1)} %bitcast.10), custom_call_target="tpu_custom_call" | custom-call | flops 1879048192 | bytes 15138816 | tf_op jit(solution)/shard_map/feedback_left/pallas_call | solution.py:65
  13.7 3.7 %forward_chunk.3 = (bf16[2,896,256]{2,1,0:T(8,128)(2,1)S(1)}, bf16[256,2048]{1,0:T(8,128)(2,1)S(1)}, f32[2,64,2048]{2,1,0:T(8,128)S(1)}) custom-call(s32[2]{0:T(128)S(1)} %pad_add_fusion.place_ref, bf16[128,2048]{1,0:T(8,128)(2,1)S(1)} %bitcast.21, bf16[128,2048]{1,0:T(8,128)(2,1)S(1)} %collective-permute-done.2.refs_1_, bf16[2,896,2048]{2,1,0:T(8,128)(2,1)S(1)} %bitcast.9, ...), custom_call_target="tpu_custom_call" | custom-call | flops 1879048192 | bytes 11730944 | tf_op jit(solution)/shard_map/forward_chunk/pallas_call | solution.py:65
  19.4 1.7 %collective-permute-start.4 = (bf16[64,2048]{1,0:T(8,128)(2,1)S(1)}, bf16[64,2048]{1,0:T(8,128)(2,1)S(1)}, u32[]{:S(2)}, u32[]{:S(2)}) collective-permute-start(bf16[64,2048]{1,0:T(8,128)(2,1)S(1)} %get-tuple-element.72), channel_id=1, source_target_pairs={{0,8},{4,12},{8,0},{12,4},{16,24},{20,28},{24,16},{28,20},{1,9},{5... | collective-permute-start | bytes 786440 | tf_op jit(solution)/shard_map/ppermute | solution.py:351
  21.1 5.8 %forward_chunk.4 = (bf16[2,896,512]{2,1,0:T(8,128)(2,1)S(1)}, bf16[512,2048]{1,0:T(8,128)(2,1)S(1)}, f32[2,64,2048]{2,1,0:T(8,128)S(1)}) custom-call(s32[2]{0:T(128)S(1)} %pad_add_fusion.place_ref, bf16[128,2048]{1,0:T(8,128)(2,1)S(1)} %collective-permute-done.x_ref.refs_0_, bf16[128,2048]{1,0:T(8,128)(2,1)S(1)} %collective-permute-done.5.refs_1_, ...), custom_call_target="tpu_custom_call" | custom-call | flops 3758096384 | bytes 12779520 | tf_op jit(solution)/shard_map/forward_chunk/pallas_call | solution.py:65
  29.3 3.4 %forward_chunk.5 = (bf16[2,896,256]{2,1,0:T(8,128)(2,1)S(1)}, bf16[256,2048]{1,0:T(8,128)(2,1)S(1)}, f32[64,2048]{1,0:T(8,128)S(1)}) custom-call(s32[2]{0:T(128)S(1)} %pad_add_fusion.place_ref, bf16[64,2048]{1,0:T(8,128)(2,1)S(1)} %collective-permute-done.3.refs_0_, bf16[64,2048]{1,0:T(8,128)(2,1)S(1)} %collective-permute-done.4.refs_1_, ...), custom_call_target="tpu_custom_call" | custom-call | flops 1879048192 | bytes 11730944 | tf_op jit(solution)/shard_map/forward_chunk/pallas_call | solution.py:65
  35.3 1.7 %collective-permute-start.10 = (f32[64,512]{1,0:T(8,128)S(1)}, f32[64,512]{1,0:T(8,128)S(1)}, u32[]{:S(2)}, u32[]{:S(2)}) collective-permute-start(f32[64,512]{1,0:T(8,128)S(1)} %get-tuple-element.81), channel_id=1, source_target_pairs={{0,8},{4,12},{8,0},{12,4},{16,24},{20,28},{24,16},{28,20},{1,9},{5... | collective-permute-start | bytes 393224 | tf_op jit(solution)/shard_map/ppermute | solution.py:351
  38.9 2.7 %gradient.3.fb_ref = f32[2,896,2048]{2,1,0:T(8,128)S(1)} custom-call(s32[2]{0:T(128)S(1)} %pad_add_fusion.place_ref, f32[2,896,2048]{2,1,0:T(8,128)S(1)} %get-tuple-element.84.fb_ref, bf16[2,896,256]{2,1,0:T(8,128)(2,1)S(1)} %get-tuple-element.85.refs_0_, bf16[2,896,512]{2,1,0:T(8,128)(2,1)S(1)} %get-tuple-element.86.refs_1_, ...), custom_call_target="tpu_custom_call", output_to_operand_aliasing={{}: (1, {})} | custom-call | flops 1879048192 | bytes 22544384 | tf_op jit(solution)/shard_map/gradient/pallas_call | solution.py:65
  41.6 3.5 %collective-permute-done.11.refs_2_ = f32[64,512]{1,0:T(8,128)S(1)} collective-permute-done((f32[64,512]{1,0:T(8,128)S(1)}, f32[64,512]{1,0:T(8,128)S(1)}, u32[]{:S(2)}, u32[]{:S(2)}) %collective-permute-start.11) | collective-permute-done | bytes 131104 | tf_op jit(solution)/shard_map/ppermute | solution.py:351
  45.7 3.7 %collective-permute-start.15 = (f32[64,512]{1,0:T(8,128)S(1)}, f32[64,512]{1,0:T(8,128)S(1)}, u32[]{:S(2)}, u32[]{:S(2)}) collective-permute-start(f32[64,512]{1,0:T(8,128)S(1)} %add.4.refs_0_), channel_id=1, source_target_pairs={{0,3},{1,2},{2,1},{3,0},{4,7},{5,6},{6,5},{7,4},{8,11},{9,10},{10,... | collective-permute-start | bytes 393224 | tf_op jit(solution)/shard_map/ppermute | solution.py:351
  50.1 4.7 %gradient.4.fb_ref = f32[2,896,2048]{2,1,0:T(8,128)S(1)} custom-call(s32[2]{0:T(128)S(1)} %pad_add_fusion.place_ref, f32[2,896,2048]{2,1,0:T(8,128)S(1)} %gradient.3.fb_ref, bf16[2,896,256]{2,1,0:T(8,128)(2,1)S(1)} %get-tuple-element.85.refs_0_, bf16[2,896,512]{2,1,0:T(8,128)(2,1)S(1)} %get-tuple-element.86.refs_1_, ...), custom_call_target="tpu_custom_call", output_to_operand_aliasing={{}: (1, {})} | custom-call | flops 3758096384 | bytes 22544384 | tf_op jit(solution)/shard_map/gradient/pallas_call | solution.py:65
  54.9 4.6 %collective-permute-done.14.refs_2_ = f32[64,512]{1,0:T(8,128)S(1)} collective-permute-done((f32[64,512]{1,0:T(8,128)S(1)}, f32[64,512]{1,0:T(8,128)S(1)}, u32[]{:S(2)}, u32[]{:S(2)}) %collective-permute-start.14) | collective-permute-done | bytes 131104 | tf_op jit(solution)/shard_map/ppermute | solution.py:351
  60.0 1.7 %collective-permute-start.18 = (f32[64,512]{1,0:T(8,128)S(1)}, f32[64,512]{1,0:T(8,128)S(1)}, u32[]{:S(2)}, u32[]{:S(2)}) collective-permute-start(f32[64,512]{1,0:T(8,128)S(1)} %add.5.refs_0_), channel_id=1, source_target_pairs={{0,24},{4,28},{8,16},{12,20},{16,8},{20,12},{24,0},{28,4},{1,25},{... | collective-permute-start | bytes 393224 | tf_op jit(solution)/shard_map/ppermute | solution.py:351
  63.6 2.7 %gradient.5.delta_ref = f32[2,896,2048]{2,1,0:T(8,128)S(1)} custom-call(s32[2]{0:T(128)S(1)} %pad_add_fusion.place_ref, f32[2,896,2048]{2,1,0:T(8,128)S(1)} %gradient.4.fb_ref, bf16[2,896,256]{2,1,0:T(8,128)(2,1)S(1)} %get-tuple-element.85.refs_0_, bf16[2,896,512]{2,1,0:T(8,128)(2,1)S(1)} %get-tuple-element.86.refs_1_, ...), custom_call_target="tpu_custom_call", output_to_operand_aliasing={{}: (1, {})} | custom-call | flops 1879048192 | bytes 22544384 | tf_op jit(solution)/shard_map/gradient/pallas_call | solution.py:65
  69.3 3.0 %project.2 = (f32[32,896]{1,0:T(8,128)S(1)}, f32[32,896]{1,0:T(8,128)S(1)}) custom-call(s32[2]{0:T(128)S(1)} %pad_add_fusion.place_ref, f32[2,896,2048]{2,1,0:T(8,128)S(1)} %gradient.5.delta_ref, f32[64,2048]{1,0:T(8,128)S(1)} %join.1.left_ref.mine_ref), custom_call_target="tpu_custom_call" | custom-call | flops 939524096 | bytes 15204352 | tf_op jit(solution)/shard_map/project/pallas_call | solution.py:65
  72.3 2.2 %collective-permute-start.21 = (f32[32,896]{1,0:T(8,128)S(1)}, f32[32,896]{1,0:T(8,128)S(1)}, u32[]{:S(2)}, u32[]{:S(2)}) collective-permute-start(f32[32,896]{1,0:T(8,128)S(1)} %get-tuple-element.102.refs_1_), channel_id=1, source_target_pairs={{0,3},{1,2},{2,1},{3,0},{4,7},{5,6},{6,5},{7,4},{8,11},{9,10},{10,... | collective-permute-start | bytes 344072 | tf_op jit(solution)/shard_map/ppermute | solution.py:351
  74.5 3.0 %project.3 = (f32[32,896]{1,0:T(8,128)S(1)}, f32[32,896]{1,0:T(8,128)S(1)}) custom-call(s32[2]{0:T(128)S(1)} %pad_add_fusion.place_ref, f32[2,896,2048]{2,1,0:T(8,128)S(1)} %gradient.5.delta_ref, f32[64,2048]{1,0:T(8,128)S(1)} %collective-permute-done.19.left_ref.other_ref), custom_call_target="tpu_custom_call" | custom-call | flops 939524096 | bytes 15204352 | tf_op jit(solution)/shard_map/project/pallas_call | solution.py:65
  78.6 1.7 %collective-permute-start.23 = (f32[32,896]{1,0:T(8,128)S(1)}, f32[32,896]{1,0:T(8,128)S(1)}, u32[]{:S(2)}, u32[]{:S(2)}) collective-permute-start(f32[32,896]{1,0:T(8,128)S(1)} %get-tuple-element.105.refs_1_), channel_id=1, source_target_pairs={{0,3},{1,2},{2,1},{3,0},{4,7},{5,6},{6,5},{7,4},{8,11},{9,10},{10,... | collective-permute-start | bytes 344072 | tf_op jit(solution)/shard_map/ppermute | solution.py:351
  80.3 4.9 %factorize.1.inv_ref = f32[2,64,64]{2,1,0:T(8,128)S(1)} custom-call(s32[2]{0:T(128)S(1)} %pad_add_fusion.place_ref, f32[64,2048]{1,0:T(8,128)S(1)} %join.1.left_ref.mine_ref, f32[64,2048]{1,0:T(8,128)S(1)} %collective-permute-done.19.left_ref.other_ref), custom_call_target="tpu_custom_call" | custom-call | flops 2000000000 | bytes 1048576 | tf_op jit(solution)/shard_map/factorize/pallas_call | solution.py:65
  86.3 2.2 %collective-permute-start.26 = (f32[32,896]{1,0:T(8,128)S(1)}, f32[32,896]{1,0:T(8,128)S(1)}, u32[]{:S(2)}, u32[]{:S(2)}) collective-permute-start(f32[32,896]{1,0:T(8,128)S(1)} %get-tuple-element.113.y0_ref), channel_id=1, source_target_pairs={{0,3},{1,2},{2,1},{3,0},{4,7},{5,6},{6,5},{7,4},{8,11},{9,10},{10,... | collective-permute-start | bytes 344072 | tf_op jit(solution)/shard_map/ppermute | solution.py:351
  89.4 1.8 %collective-permute-start.24 = (f32[32,896]{1,0:T(8,128)S(1)}, f32[32,896]{1,0:T(8,128)S(1)}, u32[]{:S(2)}, u32[]{:S(2)}) collective-permute-start(f32[32,896]{1,0:T(8,128)S(1)} %get-tuple-element.109.y0_ref), channel_id=1, source_target_pairs={{0,3},{1,2},{2,1},{3,0},{4,7},{5,6},{6,5},{7,4},{8,11},{9,10},{10,... | collective-permute-start | bytes 344072 | tf_op jit(solution)/shard_map/ppermute | solution.py:351
  94.4 2.8 %collective-permute-done.27.got1_ref = f32[32,896]{1,0:T(8,128)S(1)} collective-permute-done((f32[32,896]{1,0:T(8,128)S(1)}, f32[32,896]{1,0:T(8,128)S(1)}, u32[]{:S(2)}, u32[]{:S(2)}) %collective-permute-start.27) | collective-permute-done | bytes 114720 | tf_op jit(solution)/shard_map/ppermute | solution.py:351
  97.1 5.2 %finish.2 = (f32[2,896,2048]{2,1,0:T(8,128)}, f32[2,896,512]{2,1,0:T(8,128)}, bf16[2,896,512]{2,1,0:T(8,128)(2,1)}, f32[2,64,896]{2,1,0:T(8,128)}) custom-call(s32[2]{0:T(128)S(1)} %pad_add_fusion.place_ref, f32[32,896]{1,0:T(8,128)S(1)} %get-tuple-element.113.y0_ref, f32[32,896]{1,0:T(8,128)S(1)} %get-tuple-element.114.y1_ref, ...), custom_call_target="tpu_custom_call" | custom-call | flops 939524096 | bytes 27754496 | tf_op jit(solution)/shard_map/finish/pallas_call | solution.py:65
  102.4 5.2 %finish.3 = (f32[2,896,2048]{2,1,0:T(8,128)}, f32[2,896,512]{2,1,0:T(8,128)}, bf16[2,896,512]{2,1,0:T(8,128)(2,1)}, f32[2,64,896]{2,1,0:T(8,128)}) custom-call(s32[2]{0:T(128)S(1)} %pad_add_fusion.place_ref, f32[32,896]{1,0:T(8,128)S(1)} %get-tuple-element.109.y0_ref, ...), custom_call_target="tpu_custom_call", output_to_operand_aliasing={{0}: (10, {}), {1}: (11, {}), {2}: (12, {}), {3}: (13, {})} | custom-call | flops 939524096 | bytes 48398336 | tf_op jit(solution)/shard_map/finish/pallas_call | solution.py:65
  (69 shorter events, 25.3 us)
Async XLA Ops:
  0.6 12.8 %collective-permute-start.2 = (bf16[128,2048]{1,0:T(8,128)(2,1)}, bf16[128,2048]{1,0:T(8,128)(2,1)S(1)}, u32[]{:S(2)}, u32[]{:S(2)}) collective-permute-start(bf16[128,2048]{1,0:T(8,128)(2,1)} %bitcast.18), channel_id=1, source_target_pairs={{0,4},{4,0},{8,12},{12,8},{16,20},{20,16},{24,28},{28,24},{1,5},{5... | collective-permute-start | bytes 1572872 | tf_op jit(solution)/shard_map/ppermute | solution.py:351
  1.1 16.2 %collective-permute-start.1 = (bf16[128,2048]{1,0:T(8,128)(2,1)}, bf16[128,2048]{1,0:T(8,128)(2,1)S(1)}, u32[]{:S(2)}, u32[]{:S(2)}) collective-permute-start(bf16[128,2048]{1,0:T(8,128)(2,1)} %bitcast.19), channel_id=1, source_target_pairs={{0,16},{4,20},{8,24},{12,28},{16,0},{20,4},{24,8},{28,12},{1,17},{... | collective-permute-start | bytes 1572872 | tf_op jit(solution)/shard_map/ppermute | solution.py:351
  3.7 14.2 %collective-permute-start = (bf16[128,2048]{1,0:T(8,128)(2,1)}, bf16[128,2048]{1,0:T(8,128)(2,1)S(1)}, u32[]{:S(2)}, u32[]{:S(2)}) collective-permute-start(bf16[128,2048]{1,0:T(8,128)(2,1)} %bitcast.20), channel_id=1, source_target_pairs={{0,8},{4,12},{8,0},{12,4},{16,24},{20,28},{24,16},{28,20},{1,9},{5... | collective-permute-start | bytes 1572872 | tf_op jit(solution)/shard_map/ppermute | solution.py:351
  17.9 3.2 %collective-permute-start.5 = (bf16[128,2048]{1,0:T(8,128)(2,1)S(1)}, bf16[128,2048]{1,0:T(8,128)(2,1)S(1)}, u32[]{:S(2)}, u32[]{:S(2)}) collective-permute-start(bf16[128,2048]{1,0:T(8,128)(2,1)S(1)} %collective-permute-done.x_ref.refs_0_), channel_id=1, source_target_pairs={{0,4},{4,0},{8,12},{12,8},{16,20},{20,16},{24,28},{28,24},{1,5},{5... | collective-permute-start | bytes 1572872 | tf_op jit(solution)/shard_map/ppermute | solution.py:351
  19.0 8.3 %collective-permute-start.3 = (bf16[64,2048]{1,0:T(8,128)(2,1)S(1)}, bf16[64,2048]{1,0:T(8,128)(2,1)S(1)}, u32[]{:S(2)}, u32[]{:S(2)}) collective-permute-start(bf16[64,2048]{1,0:T(8,128)(2,1)S(1)} %get-tuple-element.71), channel_id=1, source_target_pairs={{0,16},{4,20},{8,24},{12,28},{16,0},{20,4},{24,8},{28,12},{1,17},{... | collective-permute-start | bytes 786440 | tf_op jit(solution)/shard_map/ppermute | solution.py:351
  19.4 8.0 %collective-permute-start.4 = (bf16[64,2048]{1,0:T(8,128)(2,1)S(1)}, bf16[64,2048]{1,0:T(8,128)(2,1)S(1)}, u32[]{:S(2)}, u32[]{:S(2)}) collective-permute-start(bf16[64,2048]{1,0:T(8,128)(2,1)S(1)} %get-tuple-element.72), channel_id=1, source_target_pairs={{0,8},{4,12},{8,0},{12,4},{16,24},{20,28},{24,16},{28,20},{1,9},{5... | collective-permute-start | bytes 786440 | tf_op jit(solution)/shard_map/ppermute | solution.py:351
  35.3 6.3 %collective-permute-start.10 = (f32[64,512]{1,0:T(8,128)S(1)}, f32[64,512]{1,0:T(8,128)S(1)}, u32[]{:S(2)}, u32[]{:S(2)}) collective-permute-start(f32[64,512]{1,0:T(8,128)S(1)} %get-tuple-element.81), channel_id=1, source_target_pairs={{0,8},{4,12},{8,0},{12,4},{16,24},{20,28},{24,16},{28,20},{1,9},{5... | collective-permute-start | bytes 393224 | tf_op jit(solution)/shard_map/ppermute | solution.py:351
  37.0 8.1 %collective-permute-start.11 = (f32[64,512]{1,0:T(8,128)S(1)}, f32[64,512]{1,0:T(8,128)S(1)}, u32[]{:S(2)}, u32[]{:S(2)}) collective-permute-start(f32[64,512]{1,0:T(8,128)S(1)} %get-tuple-element.82), channel_id=1, source_target_pairs={{0,16},{4,20},{8,24},{12,28},{16,0},{20,4},{24,8},{28,12},{1,17},{... | collective-permute-start | bytes 393224 | tf_op jit(solution)/shard_map/ppermute | solution.py:351
  38.6 6.6 %collective-permute-start.12 = (f32[64,512]{1,0:T(8,128)S(1)}, f32[64,512]{1,0:T(8,128)S(1)}, u32[]{:S(2)}, u32[]{:S(2)}) collective-permute-start(f32[64,512]{1,0:T(8,128)S(1)} %get-tuple-element.83), channel_id=1, source_target_pairs={{0,24},{4,28},{8,16},{12,20},{16,8},{20,12},{24,0},{28,4},{1,25},{... | collective-permute-start | bytes 393224 | tf_op jit(solution)/shard_map/ppermute | solution.py:351
  45.7 9.2 %collective-permute-start.15 = (f32[64,512]{1,0:T(8,128)S(1)}, f32[64,512]{1,0:T(8,128)S(1)}, u32[]{:S(2)}, u32[]{:S(2)}) collective-permute-start(f32[64,512]{1,0:T(8,128)S(1)} %add.4.refs_0_), channel_id=1, source_target_pairs={{0,3},{1,2},{2,1},{3,0},{4,7},{5,6},{6,5},{7,4},{8,11},{9,10},{10,... | collective-permute-start | bytes 393224 | tf_op jit(solution)/shard_map/ppermute | solution.py:351
  49.3 10.1 %collective-permute-start.14 = (f32[64,512]{1,0:T(8,128)S(1)}, f32[64,512]{1,0:T(8,128)S(1)}, u32[]{:S(2)}, u32[]{:S(2)}) collective-permute-start(f32[64,512]{1,0:T(8,128)S(1)} %add.4.refs_0_), channel_id=1, source_target_pairs={{0,2},{1,3},{2,0},{3,1},{4,6},{5,7},{6,4},{7,5},{8,10},{9,11},{10,... | collective-permute-start | bytes 393224 | tf_op jit(solution)/shard_map/ppermute | solution.py:351
  49.4 10.1 %collective-permute-start.13 = (f32[64,512]{1,0:T(8,128)S(1)}, f32[64,512]{1,0:T(8,128)S(1)}, u32[]{:S(2)}, u32[]{:S(2)}) collective-permute-start(f32[64,512]{1,0:T(8,128)S(1)} %add.4.refs_0_), channel_id=1, source_target_pairs={{0,1},{1,0},{2,3},{3,2},{4,5},{5,4},{6,7},{7,6},{8,9},{9,8},{10,11... | collective-permute-start | bytes 393224 | tf_op jit(solution)/shard_map/ppermute | solution.py:351
  60.0 7.2 %collective-permute-start.18 = (f32[64,512]{1,0:T(8,128)S(1)}, f32[64,512]{1,0:T(8,128)S(1)}, u32[]{:S(2)}, u32[]{:S(2)}) collective-permute-start(f32[64,512]{1,0:T(8,128)S(1)} %add.5.refs_0_), channel_id=1, source_target_pairs={{0,24},{4,28},{8,16},{12,20},{16,8},{20,12},{24,0},{28,4},{1,25},{... | collective-permute-start | bytes 393224 | tf_op jit(solution)/shard_map/ppermute | solution.py:351
  61.8 6.6 %collective-permute-start.17 = (f32[64,512]{1,0:T(8,128)S(1)}, f32[64,512]{1,0:T(8,128)S(1)}, u32[]{:S(2)}, u32[]{:S(2)}) collective-permute-start(f32[64,512]{1,0:T(8,128)S(1)} %add.5.refs_0_), channel_id=1, source_target_pairs={{0,16},{4,20},{8,24},{12,28},{16,0},{20,4},{24,8},{28,12},{1,17},{... | collective-permute-start | bytes 393224 | tf_op jit(solution)/shard_map/ppermute | solution.py:351
  63.2 5.3 %collective-permute-start.16 = (f32[64,512]{1,0:T(8,128)S(1)}, f32[64,512]{1,0:T(8,128)S(1)}, u32[]{:S(2)}, u32[]{:S(2)}) collective-permute-start(f32[64,512]{1,0:T(8,128)S(1)} %add.5.refs_0_), channel_id=1, source_target_pairs={{0,8},{4,12},{8,0},{12,4},{16,24},{20,28},{24,16},{28,20},{1,9},{5... | collective-permute-start | bytes 393224 | tf_op jit(solution)/shard_map/ppermute | solution.py:351
  69.2 5.3 %collective-permute-start.19 = (f32[64,2048]{1,0:T(8,128)S(1)}, f32[64,2048]{1,0:T(8,128)S(1)}, u32[]{:S(2)}, u32[]{:S(2)}) collective-permute-start(f32[64,2048]{1,0:T(8,128)S(1)} %join.1.left_ref.mine_ref), channel_id=1, source_target_pairs={{0,4},{4,0},{8,12},{12,8},{16,20},{20,16},{24,28},{28,24},{1,5},{5... | collective-permute-start | bytes 1572872 | tf_op jit(solution)/shard_map/ppermute | solution.py:351
  72.2 12.9 %collective-permute-start.20 = (f32[32,896]{1,0:T(8,128)S(1)}, f32[32,896]{1,0:T(8,128)S(1)}, u32[]{:S(2)}, u32[]{:S(2)}) collective-permute-start(f32[32,896]{1,0:T(8,128)S(1)} %get-tuple-element.101.refs_0_), channel_id=1, source_target_pairs={{0,1},{1,0},{2,3},{3,2},{4,5},{5,4},{6,7},{7,6},{8,9},{9,8},{10,11... | collective-permute-start | bytes 344072 | tf_op jit(solution)/shard_map/ppermute | solution.py:351
  72.3 12.9 %collective-permute-start.21 = (f32[32,896]{1,0:T(8,128)S(1)}, f32[32,896]{1,0:T(8,128)S(1)}, u32[]{:S(2)}, u32[]{:S(2)}) collective-permute-start(f32[32,896]{1,0:T(8,128)S(1)} %get-tuple-element.102.refs_1_), channel_id=1, source_target_pairs={{0,3},{1,2},{2,1},{3,0},{4,7},{5,6},{6,5},{7,4},{8,11},{9,10},{10,... | collective-permute-start | bytes 344072 | tf_op jit(solution)/shard_map/ppermute | solution.py:351
  77.4 7.7 %collective-permute-start.22 = (f32[32,896]{1,0:T(8,128)S(1)}, f32[32,896]{1,0:T(8,128)S(1)}, u32[]{:S(2)}, u32[]{:S(2)}) collective-permute-start(f32[32,896]{1,0:T(8,128)S(1)} %get-tuple-element.104.refs_0_), channel_id=1, source_target_pairs={{0,1},{1,0},{2,3},{3,2},{4,5},{5,4},{6,7},{7,6},{8,9},{9,8},{10,11... | collective-permute-start | bytes 344072 | tf_op jit(solution)/shard_map/ppermute | solution.py:351
  78.6 7.2 %collective-permute-start.23 = (f32[32,896]{1,0:T(8,128)S(1)}, f32[32,896]{1,0:T(8,128)S(1)}, u32[]{:S(2)}, u32[]{:S(2)}) collective-permute-start(f32[32,896]{1,0:T(8,128)S(1)} %get-tuple-element.105.refs_1_), channel_id=1, source_target_pairs={{0,3},{1,2},{2,1},{3,0},{4,7},{5,6},{6,5},{7,4},{8,11},{9,10},{10,... | collective-permute-start | bytes 344072 | tf_op jit(solution)/shard_map/ppermute | solution.py:351
  86.3 8.1 %collective-permute-start.26 = (f32[32,896]{1,0:T(8,128)S(1)}, f32[32,896]{1,0:T(8,128)S(1)}, u32[]{:S(2)}, u32[]{:S(2)}) collective-permute-start(f32[32,896]{1,0:T(8,128)S(1)} %get-tuple-element.113.y0_ref), channel_id=1, source_target_pairs={{0,3},{1,2},{2,1},{3,0},{4,7},{5,6},{6,5},{7,4},{8,11},{9,10},{10,... | collective-permute-start | bytes 344072 | tf_op jit(solution)/shard_map/ppermute | solution.py:351
  88.5 8.6 %collective-permute-start.27 = (f32[32,896]{1,0:T(8,128)S(1)}, f32[32,896]{1,0:T(8,128)S(1)}, u32[]{:S(2)}, u32[]{:S(2)}) collective-permute-start(f32[32,896]{1,0:T(8,128)S(1)} %get-tuple-element.114.y1_ref), channel_id=1, source_target_pairs={{0,1},{1,0},{2,3},{3,2},{4,5},{5,4},{6,7},{7,6},{8,9},{9,8},{10,11... | collective-permute-start | bytes 344072 | tf_op jit(solution)/shard_map/ppermute | solution.py:351
  89.4 13.0 %collective-permute-start.24 = (f32[32,896]{1,0:T(8,128)S(1)}, f32[32,896]{1,0:T(8,128)S(1)}, u32[]{:S(2)}, u32[]{:S(2)}) collective-permute-start(f32[32,896]{1,0:T(8,128)S(1)} %get-tuple-element.109.y0_ref), channel_id=1, source_target_pairs={{0,3},{1,2},{2,1},{3,0},{4,7},{5,6},{6,5},{7,4},{8,11},{9,10},{10,... | collective-permute-start | bytes 344072 | tf_op jit(solution)/shard_map/ppermute | solution.py:351
  91.2 11.2 %collective-permute-start.25 = (f32[32,896]{1,0:T(8,128)S(1)}, f32[32,896]{1,0:T(8,128)S(1)}, u32[]{:S(2)}, u32[]{:S(2)}) collective-permute-start(f32[32,896]{1,0:T(8,128)S(1)} %get-tuple-element.110.y1_ref), channel_id=1, source_target_pairs={{0,1},{1,0},{2,3},{3,2},{4,5},{5,4},{6,7},{7,6},{8,9},{9,8},{10,11... | collective-permute-start | bytes 344072 | tf_op jit(solution)/shard_map/ppermute | solution.py:351
  (11 other events, 58.7 us)

commit v2 on v1

--- a/solution.py
+++ b/solution.py
@@ -231,7 +231,7 @@
             gram = lax.dot_general(x, x, contract_last, precision=highest, preferred_element_type=f32)
             work.append(jnp.concatenate([gram, eye], 1))
             roots.append(jnp.zeros((rank, 2 * rank), f32))
-        group = 4
+        group = 8
         for first in range(0, rank, group):
             for k in range(2):
                 a = work[k]
@@ -251,7 +251,7 @@
             inv_ref[k] = (work[k] * roots[k])[:, rank:]
 
     return call(
-        body, place, (mine, other), shape(2, rank, rank), 8, 1000000000, name="factorize"
+        body, place, (mine, other), shape(2, rank, rank), 8, 1000000, name="factorize"
     )
 
 
@@ -267,7 +267,7 @@
             cat_ref[k] = jnp.concatenate([b_hi, b_lo, b_hi], 0)
 
     return call(
-        body, place, (mine, other, inverse), shape(2, 3 * rank, feats, dtype=bf16), 8, 500000000,
+        body, place, (mine, other, inverse), shape(2, 3 * rank, feats, dtype=bf16), 8, 1000000,
         name="make_basis",
     )
 
@@ -491,19 +491,18 @@
         return [swap(x, "rep", m) for x, m in zip(bands, orders[step])]
 
     y_a = project(place, delta, mine, 0, scale)
-    y_b = None
-    for t in range(last + 1):
-        got_a = exchange(y_a, t)
-        if t == 0:
-            y_b = project(place, delta, after(other, *y_a), 1, scale)
-        got_b = exchange(y_b, t)
-        if t == 0:
-            inverse = factorize(place, after(mine, *y_b), other, scale)
-            *got, inverse = lax.optimization_barrier((*got_a, *got_b, inverse))
-            got_a, got_b = got[:2], got[2:]
-        if t < last:
-            y_a = add_pairs(place, y_a, got_a)
-            y_b = add_pairs(place, y_b, got_b)
+    got_a = exchange(y_a, 0)
+    y_b = project(place, delta, after(other, *y_a), 1, scale)
+    got_b = exchange(y_b, 0)
+    *got_a, _ = lax.optimization_barrier((*got_a, y_b[0]))
+    for t in range(last):
+        y_a = add_pairs(place, y_a, got_a)
+        got_a = exchange(y_a, t + 1)
+    inverse = factorize(place, after(mine, *y_a), other, scale)
+    *got_b, inverse = lax.optimization_barrier((*got_b, inverse))
+    for t in range(last):
+        y_b = add_pairs(place, y_b, got_b)
+        got_b = exchange(y_b, t + 1)
     basis_cat = make_basis(place, after(mine, *y_a, *y_b), other, inverse, scale)
     common = inverse, basis_cat, delta, momentum, weight, replicas
     *done, rn_t = finish(place, y_a, got_a, *common, 0, None)

time: 108 us -> 105 us (0.972)
  waiting for transfers between devices: 17.6 us -> 14.8 us
    ppermute x28, waiting for transfers between devices: 17.6 us -> 14.8 us  [swap(): return lax.ppermute(x, axis, [(i, i ^ mask) for i in range(size)])]
  transfers between devices with their start and end apart: 28 -> 28, of which waited for: 14 -> 12; matrix products, arithmetic and copies ran while one was open for 0% -> 0% of each run, Pallas kernels for 43% -> 44%
where the time goes in v2:
time: 105 us
  Pallas kernels  57.1 us (54%)
  starting transfers between devices  30.1 us (29%)
  waiting for transfers between devices  14.8 us (14%)
  local copies, waits for them, and re-layouts  1.41 us (1%)
  between operations  1.11 us (1%)
    pallas_call x21, Pallas kernels, call(): pl.pallas_call(body, out_shape=out_shape, compiler_params=pltpu.CompilerP...  57.1 us
    ppermute x28, starting transfers between devices, swap(): return lax.ppermute(x, axis, [(i, i ^ mask) for i in range(size)])  30.1 us
    ppermute x28, waiting for transfers between devices, swap(): return lax.ppermute(x, axis, [(i, i ^ mask) for i in range(size)])  14.8 us
  transfers between devices with their start and end apart: 28, of which 12 were waited for; matrix products, arithmetic and copies ran while one was open for 0% of the time, Pallas kernels for 44%

profile of v2, /device:TPU:0, one launch (start us, length us, event | category | flops | bytes accessed | tf_op | source)
XLA Modules:
  0.0 104.6 jit_solution(17507367879529187701)
XLA Ops:
  1.1 2.6 %collective-permute-start.1 = (bf16[128,2048]{1,0:T(8,128)(2,1)}, bf16[128,2048]{1,0:T(8,128)(2,1)S(1)}, u32[]{:S(2)}, u32[]{:S(2)}) collective-permute-start(bf16[128,2048]{1,0:T(8,128)(2,1)} %bitcast.19), channel_id=1, source_target_pairs={{0,16},{4,20},{8,24},{12,28},{16,0},{20,4},{24,8},{28,12},{1,17},{... | collective-permute-start | bytes 1572872 | tf_op jit(solution)/shard_map/ppermute | solution.py:351
  6.5 6.9 %feedback_left.1 = (f32[2,896,2048]{2,1,0:T(8,128)S(1)}, f32[2,64,2048]{2,1,0:T(8,128)S(1)}) custom-call(s32[2]{0:T(128)S(1)} %pad_add_fusion.place_ref, f32[2,896,2048]{2,1,0:T(8,128)} %bitcast.22, f32[2,64,896]{2,1,0:T(8,128)S(1)} %bitcast.10), custom_call_target="tpu_custom_call" | custom-call | flops 1879048192 | bytes 15138816 | tf_op jit(solution)/shard_map/feedback_left/pallas_call | solution.py:65
  13.7 3.7 %forward_chunk.3 = (bf16[2,896,256]{2,1,0:T(8,128)(2,1)S(1)}, bf16[256,2048]{1,0:T(8,128)(2,1)S(1)}, f32[2,64,2048]{2,1,0:T(8,128)S(1)}) custom-call(s32[2]{0:T(128)S(1)} %pad_add_fusion.place_ref, bf16[128,2048]{1,0:T(8,128)(2,1)S(1)} %bitcast.21, bf16[128,2048]{1,0:T(8,128)(2,1)S(1)} %collective-permute-done.2.refs_1_, bf16[2,896,2048]{2,1,0:T(8,128)(2,1)S(1)} %bitcast.9, ...), custom_call_target="tpu_custom_call" | custom-call | flops 1879048192 | bytes 11730944 | tf_op jit(solution)/shard_map/forward_chunk/pallas_call | solution.py:65
  19.4 1.7 %collective-permute-start.4 = (bf16[64,2048]{1,0:T(8,128)(2,1)S(1)}, bf16[64,2048]{1,0:T(8,128)(2,1)S(1)}, u32[]{:S(2)}, u32[]{:S(2)}) collective-permute-start(bf16[64,2048]{1,0:T(8,128)(2,1)S(1)} %get-tuple-element.72), channel_id=1, source_target_pairs={{0,8},{4,12},{8,0},{12,4},{16,24},{20,28},{24,16},{28,20},{1,9},{5... | collective-permute-start | bytes 786440 | tf_op jit(solution)/shard_map/ppermute | solution.py:351
  21.1 5.8 %forward_chunk.4 = (bf16[2,896,512]{2,1,0:T(8,128)(2,1)S(1)}, bf16[512,2048]{1,0:T(8,128)(2,1)S(1)}, f32[2,64,2048]{2,1,0:T(8,128)S(1)}) custom-call(s32[2]{0:T(128)S(1)} %pad_add_fusion.place_ref, bf16[128,2048]{1,0:T(8,128)(2,1)S(1)} %collective-permute-done.x_ref.refs_0_, bf16[128,2048]{1,0:T(8,128)(2,1)S(1)} %collective-permute-done.5.refs_1_, ...), custom_call_target="tpu_custom_call" | custom-call | flops 3758096384 | bytes 12779520 | tf_op jit(solution)/shard_map/forward_chunk/pallas_call | solution.py:65
  29.3 3.4 %forward_chunk.5 = (bf16[2,896,256]{2,1,0:T(8,128)(2,1)S(1)}, bf16[256,2048]{1,0:T(8,128)(2,1)S(1)}, f32[64,2048]{1,0:T(8,128)S(1)}) custom-call(s32[2]{0:T(128)S(1)} %pad_add_fusion.place_ref, bf16[64,2048]{1,0:T(8,128)(2,1)S(1)} %collective-permute-done.3.refs_0_, bf16[64,2048]{1,0:T(8,128)(2,1)S(1)} %collective-permute-done.4.refs_1_, ...), custom_call_target="tpu_custom_call" | custom-call | flops 1879048192 | bytes 11730944 | tf_op jit(solution)/shard_map/forward_chunk/pallas_call | solution.py:65
  35.3 1.7 %collective-permute-start.10 = (f32[64,512]{1,0:T(8,128)S(1)}, f32[64,512]{1,0:T(8,128)S(1)}, u32[]{:S(2)}, u32[]{:S(2)}) collective-permute-start(f32[64,512]{1,0:T(8,128)S(1)} %get-tuple-element.81), channel_id=1, source_target_pairs={{0,8},{4,12},{8,0},{12,4},{16,24},{20,28},{24,16},{28,20},{1,9},{5... | collective-permute-start | bytes 393224 | tf_op jit(solution)/shard_map/ppermute | solution.py:351
  38.9 2.7 %gradient.3.fb_ref = f32[2,896,2048]{2,1,0:T(8,128)S(1)} custom-call(s32[2]{0:T(128)S(1)} %pad_add_fusion.place_ref, f32[2,896,2048]{2,1,0:T(8,128)S(1)} %get-tuple-element.84.fb_ref, bf16[2,896,256]{2,1,0:T(8,128)(2,1)S(1)} %get-tuple-element.85.refs_0_, bf16[2,896,512]{2,1,0:T(8,128)(2,1)S(1)} %get-tuple-element.86.refs_1_, ...), custom_call_target="tpu_custom_call", output_to_operand_aliasing={{}: (1, {})} | custom-call | flops 1879048192 | bytes 22544384 | tf_op jit(solution)/shard_map/gradient/pallas_call | solution.py:65
  41.6 3.5 %collective-permute-done.11.refs_2_ = f32[64,512]{1,0:T(8,128)S(1)} collective-permute-done((f32[64,512]{1,0:T(8,128)S(1)}, f32[64,512]{1,0:T(8,128)S(1)}, u32[]{:S(2)}, u32[]{:S(2)}) %collective-permute-start.11) | collective-permute-done | bytes 131104 | tf_op jit(solution)/shard_map/ppermute | solution.py:351
  45.7 3.7 %collective-permute-start.15 = (f32[64,512]{1,0:T(8,128)S(1)}, f32[64,512]{1,0:T(8,128)S(1)}, u32[]{:S(2)}, u32[]{:S(2)}) collective-permute-start(f32[64,512]{1,0:T(8,128)S(1)} %add.4.refs_0_), channel_id=1, source_target_pairs={{0,3},{1,2},{2,1},{3,0},{4,7},{5,6},{6,5},{7,4},{8,11},{9,10},{10,... | collective-permute-start | bytes 393224 | tf_op jit(solution)/shard_map/ppermute | solution.py:351
  50.1 4.7 %gradient.4.fb_ref = f32[2,896,2048]{2,1,0:T(8,128)S(1)} custom-call(s32[2]{0:T(128)S(1)} %pad_add_fusion.place_ref, f32[2,896,2048]{2,1,0:T(8,128)S(1)} %gradient.3.fb_ref, bf16[2,896,256]{2,1,0:T(8,128)(2,1)S(1)} %get-tuple-element.85.refs_0_, bf16[2,896,512]{2,1,0:T(8,128)(2,1)S(1)} %get-tuple-element.86.refs_1_, ...), custom_call_target="tpu_custom_call", output_to_operand_aliasing={{}: (1, {})} | custom-call | flops 3758096384 | bytes 22544384 | tf_op jit(solution)/shard_map/gradient/pallas_call | solution.py:65
  54.9 4.6 %collective-permute-done.14.refs_2_ = f32[64,512]{1,0:T(8,128)S(1)} collective-permute-done((f32[64,512]{1,0:T(8,128)S(1)}, f32[64,512]{1,0:T(8,128)S(1)}, u32[]{:S(2)}, u32[]{:S(2)}) %collective-permute-start.14) | collective-permute-done | bytes 131104 | tf_op jit(solution)/shard_map/ppermute | solution.py:351
  60.0 1.7 %collective-permute-start.18 = (f32[64,512]{1,0:T(8,128)S(1)}, f32[64,512]{1,0:T(8,128)S(1)}, u32[]{:S(2)}, u32[]{:S(2)}) collective-permute-start(f32[64,512]{1,0:T(8,128)S(1)} %add.5.refs_0_), channel_id=1, source_target_pairs={{0,24},{4,28},{8,16},{12,20},{16,8},{20,12},{24,0},{28,4},{1,25},{... | collective-permute-start | bytes 393224 | tf_op jit(solution)/shard_map/ppermute | solution.py:351
  63.6 2.7 %gradient.5.delta_ref = f32[2,896,2048]{2,1,0:T(8,128)S(1)} custom-call(s32[2]{0:T(128)S(1)} %pad_add_fusion.place_ref, f32[2,896,2048]{2,1,0:T(8,128)S(1)} %gradient.4.fb_ref, bf16[2,896,256]{2,1,0:T(8,128)(2,1)S(1)} %get-tuple-element.85.refs_0_, bf16[2,896,512]{2,1,0:T(8,128)(2,1)S(1)} %get-tuple-element.86.refs_1_, ...), custom_call_target="tpu_custom_call", output_to_operand_aliasing={{}: (1, {})} | custom-call | flops 1879048192 | bytes 22544384 | tf_op jit(solution)/shard_map/gradient/pallas_call | solution.py:65
  69.3 3.0 %project.2 = (f32[32,896]{1,0:T(8,128)S(1)}, f32[32,896]{1,0:T(8,128)S(1)}) custom-call(s32[2]{0:T(128)S(1)} %pad_add_fusion.place_ref, f32[2,896,2048]{2,1,0:T(8,128)S(1)} %gradient.5.delta_ref, f32[64,2048]{1,0:T(8,128)S(1)} %join.1.left_ref.mine_ref), custom_call_target="tpu_custom_call" | custom-call | flops 939524096 | bytes 15204352 | tf_op jit(solution)/shard_map/project/pallas_call | solution.py:65
  72.3 2.2 %collective-permute-start.23 = (f32[32,896]{1,0:T(8,128)S(1)}, f32[32,896]{1,0:T(8,128)S(1)}, u32[]{:S(2)}, u32[]{:S(2)}) collective-permute-start(f32[32,896]{1,0:T(8,128)S(1)} %get-tuple-element.102.refs_1_), channel_id=1, source_target_pairs={{0,3},{1,2},{2,1},{3,0},{4,7},{5,6},{6,5},{7,4},{8,11},{9,10},{10,... | collective-permute-start | bytes 344072 | tf_op jit(solution)/shard_map/ppermute | solution.py:351
  74.5 3.0 %project.3 = (f32[32,896]{1,0:T(8,128)S(1)}, f32[32,896]{1,0:T(8,128)S(1)}) custom-call(s32[2]{0:T(128)S(1)} %pad_add_fusion.place_ref, f32[2,896,2048]{2,1,0:T(8,128)S(1)} %gradient.5.delta_ref, f32[64,2048]{1,0:T(8,128)S(1)} %collective-permute-done.19.left_ref.other_ref), custom_call_target="tpu_custom_call" | custom-call | flops 939524096 | bytes 15204352 | tf_op jit(solution)/shard_map/project/pallas_call | solution.py:65
  77.5 1.8 %collective-permute-start.21 = (f32[32,896]{1,0:T(8,128)S(1)}, f32[32,896]{1,0:T(8,128)S(1)}, u32[]{:S(2)}, u32[]{:S(2)}) collective-permute-start(f32[32,896]{1,0:T(8,128)S(1)} %get-tuple-element.105.refs_1_), channel_id=1, source_target_pairs={{0,3},{1,2},{2,1},{3,0},{4,7},{5,6},{6,5},{7,4},{8,11},{9,10},{10,... | collective-permute-start | bytes 344072 | tf_op jit(solution)/shard_map/ppermute | solution.py:351
  81.3 1.8 %collective-permute-start.26 = (f32[32,896]{1,0:T(8,128)S(1)}, f32[32,896]{1,0:T(8,128)S(1)}, u32[]{:S(2)}, u32[]{:S(2)}) collective-permute-start(f32[32,896]{1,0:T(8,128)S(1)} %get-tuple-element.108.y0_ref), channel_id=1, source_target_pairs={{0,3},{1,2},{2,1},{3,0},{4,7},{5,6},{6,5},{7,4},{8,11},{9,10},{10,... | collective-permute-start | bytes 344072 | tf_op jit(solution)/shard_map/ppermute | solution.py:351
  83.1 3.6 %collective-permute-start.27 = (f32[32,896]{1,0:T(8,128)S(1)}, f32[32,896]{1,0:T(8,128)S(1)}, u32[]{:S(2)}, u32[]{:S(2)}) collective-permute-start(f32[32,896]{1,0:T(8,128)S(1)} %get-tuple-element.109.y1_ref), channel_id=1, source_target_pairs={{0,1},{1,0},{2,3},{3,2},{4,5},{5,4},{6,7},{7,6},{8,9},{9,8},{10,11... | collective-permute-start | bytes 344072 | tf_op jit(solution)/shard_map/ppermute | solution.py:351
  86.7 3.9 %factorize.1.inv_ref = f32[2,64,64]{2,1,0:T(8,128)S(1)} custom-call(s32[2]{0:T(128)S(1)} %pad_add_fusion.place_ref, f32[64,2048]{1,0:T(8,128)S(1)} %join.1.left_ref.mine_ref, f32[64,2048]{1,0:T(8,128)S(1)} %collective-permute-done.19.left_ref.other_ref), custom_call_target="tpu_custom_call" | custom-call | flops 2000000 | bytes 1048576 | tf_op jit(solution)/shard_map/factorize/pallas_call | solution.py:65
  92.3 1.5 %make_basis.1.cat_ref = bf16[2,192,2048]{2,1,0:T(8,128)(2,1)S(1)} custom-call(s32[2]{0:T(128)S(1)} %pad_add_fusion.place_ref, f32[64,2048]{1,0:T(8,128)S(1)} %join.1.left_ref.mine_ref, f32[64,2048]{1,0:T(8,128)S(1)} %collective-permute-done.19.left_ref.other_ref, f32[2,64,64]{2,1,0:T(8,128)S(1)} %factorize.1.inv_ref), custom_call_target="tpu_custom_call" | custom-call | flops 2000000 | bytes 1081344 | tf_op jit(solution)/shard_map/make_basis/pallas_call | solution.py:65
  93.9 5.2 %finish.2 = (f32[2,896,2048]{2,1,0:T(8,128)}, f32[2,896,512]{2,1,0:T(8,128)}, bf16[2,896,512]{2,1,0:T(8,128)(2,1)}, f32[2,64,896]{2,1,0:T(8,128)}) custom-call(s32[2]{0:T(128)S(1)} %pad_add_fusion.place_ref, f32[32,896]{1,0:T(8,128)S(1)} %get-tuple-element.108.y0_ref, f32[32,896]{1,0:T(8,128)S(1)} %get-tuple-element.109.y1_ref, ...), custom_call_target="tpu_custom_call" | custom-call | flops 939524096 | bytes 27754496 | tf_op jit(solution)/shard_map/finish/pallas_call | solution.py:65
  99.2 5.2 %finish.3 = (f32[2,896,2048]{2,1,0:T(8,128)}, f32[2,896,512]{2,1,0:T(8,128)}, bf16[2,896,512]{2,1,0:T(8,128)(2,1)}, f32[2,64,896]{2,1,0:T(8,128)}) custom-call(s32[2]{0:T(128)S(1)} %pad_add_fusion.place_ref, f32[32,896]{1,0:T(8,128)S(1)} %get-tuple-element.113.y0_ref, ...), custom_call_target="tpu_custom_call", output_to_operand_aliasing={{0}: (10, {}), {1}: (11, {}), {2}: (12, {}), {3}: (13, {})} | custom-call | flops 939524096 | bytes 48398336 | tf_op jit(solution)/shard_map/finish/pallas_call | solution.py:65
  (69 shorter events, 22.8 us)
Async XLA Ops:
  0.6 12.8 %collective-permute-start.2 = (bf16[128,2048]{1,0:T(8,128)(2,1)}, bf16[128,2048]{1,0:T(8,128)(2,1)S(1)}, u32[]{:S(2)}, u32[]{:S(2)}) collective-permute-start(bf16[128,2048]{1,0:T(8,128)(2,1)} %bitcast.18), channel_id=1, source_target_pairs={{0,4},{4,0},{8,12},{12,8},{16,20},{20,16},{24,28},{28,24},{1,5},{5... | collective-permute-start | bytes 1572872 | tf_op jit(solution)/shard_map/ppermute | solution.py:351
  1.1 16.2 %collective-permute-start.1 = (bf16[128,2048]{1,0:T(8,128)(2,1)}, bf16[128,2048]{1,0:T(8,128)(2,1)S(1)}, u32[]{:S(2)}, u32[]{:S(2)}) collective-permute-start(bf16[128,2048]{1,0:T(8,128)(2,1)} %bitcast.19), channel_id=1, source_target_pairs={{0,16},{4,20},{8,24},{12,28},{16,0},{20,4},{24,8},{28,12},{1,17},{... | collective-permute-start | bytes 1572872 | tf_op jit(solution)/shard_map/ppermute | solution.py:351
  3.7 14.2 %collective-permute-start = (bf16[128,2048]{1,0:T(8,128)(2,1)}, bf16[128,2048]{1,0:T(8,128)(2,1)S(1)}, u32[]{:S(2)}, u32[]{:S(2)}) collective-permute-start(bf16[128,2048]{1,0:T(8,128)(2,1)} %bitcast.20), channel_id=1, source_target_pairs={{0,8},{4,12},{8,0},{12,4},{16,24},{20,28},{24,16},{28,20},{1,9},{5... | collective-permute-start | bytes 1572872 | tf_op jit(solution)/shard_map/ppermute | solution.py:351
  17.9 3.2 %collective-permute-start.5 = (bf16[128,2048]{1,0:T(8,128)(2,1)S(1)}, bf16[128,2048]{1,0:T(8,128)(2,1)S(1)}, u32[]{:S(2)}, u32[]{:S(2)}) collective-permute-start(bf16[128,2048]{1,0:T(8,128)(2,1)S(1)} %collective-permute-done.x_ref.refs_0_), channel_id=1, source_target_pairs={{0,4},{4,0},{8,12},{12,8},{16,20},{20,16},{24,28},{28,24},{1,5},{5... | collective-permute-start | bytes 1572872 | tf_op jit(solution)/shard_map/ppermute | solution.py:351
  19.0 8.3 %collective-permute-start.3 = (bf16[64,2048]{1,0:T(8,128)(2,1)S(1)}, bf16[64,2048]{1,0:T(8,128)(2,1)S(1)}, u32[]{:S(2)}, u32[]{:S(2)}) collective-permute-start(bf16[64,2048]{1,0:T(8,128)(2,1)S(1)} %get-tuple-element.71), channel_id=1, source_target_pairs={{0,16},{4,20},{8,24},{12,28},{16,0},{20,4},{24,8},{28,12},{1,17},{... | collective-permute-start | bytes 786440 | tf_op jit(solution)/shard_map/ppermute | solution.py:351
  19.4 8.0 %collective-permute-start.4 = (bf16[64,2048]{1,0:T(8,128)(2,1)S(1)}, bf16[64,2048]{1,0:T(8,128)(2,1)S(1)}, u32[]{:S(2)}, u32[]{:S(2)}) collective-permute-start(bf16[64,2048]{1,0:T(8,128)(2,1)S(1)} %get-tuple-element.72), channel_id=1, source_target_pairs={{0,8},{4,12},{8,0},{12,4},{16,24},{20,28},{24,16},{28,20},{1,9},{5... | collective-permute-start | bytes 786440 | tf_op jit(solution)/shard_map/ppermute | solution.py:351
  35.3 6.3 %collective-permute-start.10 = (f32[64,512]{1,0:T(8,128)S(1)}, f32[64,512]{1,0:T(8,128)S(1)}, u32[]{:S(2)}, u32[]{:S(2)}) collective-permute-start(f32[64,512]{1,0:T(8,128)S(1)} %get-tuple-element.81), channel_id=1, source_target_pairs={{0,8},{4,12},{8,0},{12,4},{16,24},{20,28},{24,16},{28,20},{1,9},{5... | collective-permute-start | bytes 393224 | tf_op jit(solution)/shard_map/ppermute | solution.py:351
  37.0 8.1 %collective-permute-start.11 = (f32[64,512]{1,0:T(8,128)S(1)}, f32[64,512]{1,0:T(8,128)S(1)}, u32[]{:S(2)}, u32[]{:S(2)}) collective-permute-start(f32[64,512]{1,0:T(8,128)S(1)} %get-tuple-element.82), channel_id=1, source_target_pairs={{0,16},{4,20},{8,24},{12,28},{16,0},{20,4},{24,8},{28,12},{1,17},{... | collective-permute-start | bytes 393224 | tf_op jit(solution)/shard_map/ppermute | solution.py:351
  38.6 6.6 %collective-permute-start.12 = (f32[64,512]{1,0:T(8,128)S(1)}, f32[64,512]{1,0:T(8,128)S(1)}, u32[]{:S(2)}, u32[]{:S(2)}) collective-permute-start(f32[64,512]{1,0:T(8,128)S(1)} %get-tuple-element.83), channel_id=1, source_target_pairs={{0,24},{4,28},{8,16},{12,20},{16,8},{20,12},{24,0},{28,4},{1,25},{... | collective-permute-start | bytes 393224 | tf_op jit(solution)/shard_map/ppermute | solution.py:351
  45.7 9.2 %collective-permute-start.15 = (f32[64,512]{1,0:T(8,128)S(1)}, f32[64,512]{1,0:T(8,128)S(1)}, u32[]{:S(2)}, u32[]{:S(2)}) collective-permute-start(f32[64,512]{1,0:T(8,128)S(1)} %add.4.refs_0_), channel_id=1, source_target_pairs={{0,3},{1,2},{2,1},{3,0},{4,7},{5,6},{6,5},{7,4},{8,11},{9,10},{10,... | collective-permute-start | bytes 393224 | tf_op jit(solution)/shard_map/ppermute | solution.py:351
  49.3 10.1 %collective-permute-start.14 = (f32[64,512]{1,0:T(8,128)S(1)}, f32[64,512]{1,0:T(8,128)S(1)}, u32[]{:S(2)}, u32[]{:S(2)}) collective-permute-start(f32[64,512]{1,0:T(8,128)S(1)} %add.4.refs_0_), channel_id=1, source_target_pairs={{0,2},{1,3},{2,0},{3,1},{4,6},{5,7},{6,4},{7,5},{8,10},{9,11},{10,... | collective-permute-start | bytes 393224 | tf_op jit(solution)/shard_map/ppermute | solution.py:351
  49.4 10.1 %collective-permute-start.13 = (f32[64,512]{1,0:T(8,128)S(1)}, f32[64,512]{1,0:T(8,128)S(1)}, u32[]{:S(2)}, u32[]{:S(2)}) collective-permute-start(f32[64,512]{1,0:T(8,128)S(1)} %add.4.refs_0_), channel_id=1, source_target_pairs={{0,1},{1,0},{2,3},{3,2},{4,5},{5,4},{6,7},{7,6},{8,9},{9,8},{10,11... | collective-permute-start | bytes 393224 | tf_op jit(solution)/shard_map/ppermute | solution.py:351
  60.0 7.2 %collective-permute-start.18 = (f32[64,512]{1,0:T(8,128)S(1)}, f32[64,512]{1,0:T(8,128)S(1)}, u32[]{:S(2)}, u32[]{:S(2)}) collective-permute-start(f32[64,512]{1,0:T(8,128)S(1)} %add.5.refs_0_), channel_id=1, source_target_pairs={{0,24},{4,28},{8,16},{12,20},{16,8},{20,12},{24,0},{28,4},{1,25},{... | collective-permute-start | bytes 393224 | tf_op jit(solution)/shard_map/ppermute | solution.py:351
  61.8 6.6 %collective-permute-start.17 = (f32[64,512]{1,0:T(8,128)S(1)}, f32[64,512]{1,0:T(8,128)S(1)}, u32[]{:S(2)}, u32[]{:S(2)}) collective-permute-start(f32[64,512]{1,0:T(8,128)S(1)} %add.5.refs_0_), channel_id=1, source_target_pairs={{0,16},{4,20},{8,24},{12,28},{16,0},{20,4},{24,8},{28,12},{1,17},{... | collective-permute-start | bytes 393224 | tf_op jit(solution)/shard_map/ppermute | solution.py:351
  63.2 5.3 %collective-permute-start.16 = (f32[64,512]{1,0:T(8,128)S(1)}, f32[64,512]{1,0:T(8,128)S(1)}, u32[]{:S(2)}, u32[]{:S(2)}) collective-permute-start(f32[64,512]{1,0:T(8,128)S(1)} %add.5.refs_0_), channel_id=1, source_target_pairs={{0,8},{4,12},{8,0},{12,4},{16,24},{20,28},{24,16},{28,20},{1,9},{5... | collective-permute-start | bytes 393224 | tf_op jit(solution)/shard_map/ppermute | solution.py:351
  69.2 5.3 %collective-permute-start.19 = (f32[64,2048]{1,0:T(8,128)S(1)}, f32[64,2048]{1,0:T(8,128)S(1)}, u32[]{:S(2)}, u32[]{:S(2)}) collective-permute-start(f32[64,2048]{1,0:T(8,128)S(1)} %join.1.left_ref.mine_ref), channel_id=1, source_target_pairs={{0,4},{4,0},{8,12},{12,8},{16,20},{20,16},{24,28},{28,24},{1,5},{5... | collective-permute-start | bytes 1572872 | tf_op jit(solution)/shard_map/ppermute | solution.py:351
  72.2 7.2 %collective-permute-start.22 = (f32[32,896]{1,0:T(8,128)S(1)}, f32[32,896]{1,0:T(8,128)S(1)}, u32[]{:S(2)}, u32[]{:S(2)}) collective-permute-start(f32[32,896]{1,0:T(8,128)S(1)} %get-tuple-element.101.refs_0_), channel_id=1, source_target_pairs={{0,1},{1,0},{2,3},{3,2},{4,5},{5,4},{6,7},{7,6},{8,9},{9,8},{10,11... | collective-permute-start | bytes 344072 | tf_op jit(solution)/shard_map/ppermute | solution.py:351
  72.3 8.5 %collective-permute-start.23 = (f32[32,896]{1,0:T(8,128)S(1)}, f32[32,896]{1,0:T(8,128)S(1)}, u32[]{:S(2)}, u32[]{:S(2)}) collective-permute-start(f32[32,896]{1,0:T(8,128)S(1)} %get-tuple-element.102.refs_1_), channel_id=1, source_target_pairs={{0,3},{1,2},{2,1},{3,0},{4,7},{5,6},{6,5},{7,4},{8,11},{9,10},{10,... | collective-permute-start | bytes 344072 | tf_op jit(solution)/shard_map/ppermute | solution.py:351
  77.5 13.2 %collective-permute-start.21 = (f32[32,896]{1,0:T(8,128)S(1)}, f32[32,896]{1,0:T(8,128)S(1)}, u32[]{:S(2)}, u32[]{:S(2)}) collective-permute-start(f32[32,896]{1,0:T(8,128)S(1)} %get-tuple-element.105.refs_1_), channel_id=1, source_target_pairs={{0,3},{1,2},{2,1},{3,0},{4,7},{5,6},{6,5},{7,4},{8,11},{9,10},{10,... | collective-permute-start | bytes 344072 | tf_op jit(solution)/shard_map/ppermute | solution.py:351
  79.2 11.5 %collective-permute-start.20 = (f32[32,896]{1,0:T(8,128)S(1)}, f32[32,896]{1,0:T(8,128)S(1)}, u32[]{:S(2)}, u32[]{:S(2)}) collective-permute-start(f32[32,896]{1,0:T(8,128)S(1)} %get-tuple-element.104.refs_0_), channel_id=1, source_target_pairs={{0,1},{1,0},{2,3},{3,2},{4,5},{5,4},{6,7},{7,6},{8,9},{9,8},{10,11... | collective-permute-start | bytes 344072 | tf_op jit(solution)/shard_map/ppermute | solution.py:351
  81.3 12.5 %collective-permute-start.26 = (f32[32,896]{1,0:T(8,128)S(1)}, f32[32,896]{1,0:T(8,128)S(1)}, u32[]{:S(2)}, u32[]{:S(2)}) collective-permute-start(f32[32,896]{1,0:T(8,128)S(1)} %get-tuple-element.108.y0_ref), channel_id=1, source_target_pairs={{0,3},{1,2},{2,1},{3,0},{4,7},{5,6},{6,5},{7,4},{8,11},{9,10},{10,... | collective-permute-start | bytes 344072 | tf_op jit(solution)/shard_map/ppermute | solution.py:351
  83.1 10.8 %collective-permute-start.27 = (f32[32,896]{1,0:T(8,128)S(1)}, f32[32,896]{1,0:T(8,128)S(1)}, u32[]{:S(2)}, u32[]{:S(2)}) collective-permute-start(f32[32,896]{1,0:T(8,128)S(1)} %get-tuple-element.109.y1_ref), channel_id=1, source_target_pairs={{0,1},{1,0},{2,3},{3,2},{4,5},{5,4},{6,7},{7,6},{8,9},{9,8},{10,11... | collective-permute-start | bytes 344072 | tf_op jit(solution)/shard_map/ppermute | solution.py:351
  91.3 7.9 %collective-permute-start.24 = (f32[32,896]{1,0:T(8,128)S(1)}, f32[32,896]{1,0:T(8,128)S(1)}, u32[]{:S(2)}, u32[]{:S(2)}) collective-permute-start(f32[32,896]{1,0:T(8,128)S(1)} %get-tuple-element.113.y0_ref), channel_id=1, source_target_pairs={{0,3},{1,2},{2,1},{3,0},{4,7},{5,6},{6,5},{7,4},{8,11},{9,10},{10,... | collective-permute-start | bytes 344072 | tf_op jit(solution)/shard_map/ppermute | solution.py:351
  92.3 6.8 %collective-permute-start.25 = (f32[32,896]{1,0:T(8,128)S(1)}, f32[32,896]{1,0:T(8,128)S(1)}, u32[]{:S(2)}, u32[]{:S(2)}) collective-permute-start(f32[32,896]{1,0:T(8,128)S(1)} %get-tuple-element.114.y1_ref), channel_id=1, source_target_pairs={{0,1},{1,0},{2,3},{3,2},{4,5},{5,4},{6,7},{7,6},{8,9},{9,8},{10,11... | collective-permute-start | bytes 344072 | tf_op jit(solution)/shard_map/ppermute | solution.py:351
  (11 other events, 63.1 us)

commit v3 on v2

--- a/solution.py
+++ b/solution.py
@@ -7,7 +7,6 @@
 
 momentum_decay = 0.9
 step_rate = 0.05
-highest = lax.Precision.HIGHEST
 f32 = jnp.float32
 bf16 = jnp.bfloat16
 contract_last = (((1,), (1,)), ((), ()))
@@ -33,6 +32,33 @@
 def split2(x):
     hi = x.astype(bf16)
     return hi, (x - hi.astype(f32)).astype(bf16)
+
+
+def split3(x):
+    hi = x.astype(bf16)
+    rest = x - hi.astype(f32)
+    mid = rest.astype(bf16)
+    return hi, mid, (rest - mid.astype(f32)).astype(bf16)
+
+
+def dot_full(a, b):
+    h, m, l = split3(a)
+    p, q, r = split3(b)
+    return dot(jnp.concatenate([h, h, m, h, m, l], 1), jnp.concatenate([p, q, p, r, q, p], 0))
+
+
+def gram_full(x):
+    n = x.shape[0]
+    parts = jnp.concatenate(split3(x), 0)
+    blocks = dot_nt(parts, parts)
+    total = None
+    for order in (4, 3, 2, 1, 0):
+        for i in range(3):
+            if 0 <= order - i <= 2:
+                j = order - i
+                block = blocks[i * n : (i + 1) * n, j * n : (j + 1) * n]
+                total = block if total is None else total + block
+    return total
 
 
 def stacked(x):
@@ -135,7 +161,8 @@
             at += t.shape[0]
         gate_pre = dot_nt(w_ref[0], tok_ref[...])
         up_pre = dot_nt(w_ref[1], tok_ref[...])
-        cot = jnp.concatenate([up_ref[:, span(me ^ o, per)] for o in offsets], 1).astype(f32)
+        shards = [me ^ (even + (me & 1) * (odd - even)) for even, odd in offsets]
+        cot = jnp.concatenate([up_ref[:, span(j, per)] for j in shards], 1).astype(f32)
         s = jax.nn.sigmoid(gate_pre)
         cot_s = cot * s
         grad_ref[0] = (cot_s * up_pre * (1.0 + gate_pre * (1.0 - s))).astype(bf16)
@@ -228,7 +255,7 @@
         work, roots = [], []
         for k in range(2):
             x = jnp.where(core == k, mine_ref[...], other_ref[...]) * scale
-            gram = lax.dot_general(x, x, contract_last, precision=highest, preferred_element_type=f32)
+            gram = gram_full(x)
             work.append(jnp.concatenate([gram, eye], 1))
             roots.append(jnp.zeros((rank, 2 * rank), f32))
         group = 8
@@ -262,7 +289,7 @@
         core = place_ref[0] & 1
         for k in range(2):
             x = jnp.where(core == k, mine_ref[...], other_ref[...]) * scale
-            basis = jnp.dot(inv_ref[k], x, precision=highest, preferred_element_type=f32)
+            basis = dot_full(inv_ref[k], x)
             b_hi, b_lo = split2(basis)
             cat_ref[k] = jnp.concatenate([b_hi, b_lo, b_hi], 0)
 
@@ -289,9 +316,7 @@
         slab = span(place_ref[1], cols)
         k = (place_ref[0] & 1) ^ flip
         mean = jnp.concatenate([y0_ref[...] + got0_ref[...], y1_ref[...] + got1_ref[...]], 0)
-        rn_t[...] = jnp.dot(
-            inv_ref[k], mean * (1.0 / replicas), precision=highest, preferred_element_type=f32
-        )
+        rn_t[...] = dot_full(inv_ref[k], mean * (1.0 / replicas))
         rn_copy = pltpu.make_async_copy(rn_t, rn_out.at[k], rn_sem)
         rn_copy.start()
         hi, lo = split2(rn_t[...].T)
@@ -435,19 +460,17 @@
     right_t = jnp.swapaxes(right_factor, 1, 2)
     scale = 1.0 / replicas
 
-    def gather_inner(parts, base):
-        parts, offsets = list(parts), [base]
+    def gather_inner(part, even_mask, odd_mask):
+        parts, inners = [part], [0]
         for m in inner:
             parts = parts + [swap(p, "fsdp", m) for p in parts]
-            offsets = offsets + [o ^ m for o in offsets]
-        return parts, offsets
-
-    def halves(x, y):
-        def body(place_ref, x_ref, y_ref, x_out, y_out):
-            x_out[...] = x_ref[: per // 2, :]
-            y_out[...] = y_ref[per // 2 :, :]
-
-        return call(body, place, (x, y), [shape(per // 2, feats, dtype=bf16)] * 2, 4, name="halves")
+            inners = inners + [o ^ m for o in inners]
+        masks = even_mask, odd_mask
+        return parts, [(o ^ masks[o & 1], o ^ masks[1 - (o & 1)]) for o in inners]
+
+    def swap_far(x, even_mask, odd_mask):
+        masks = even_mask, odd_mask
+        return lax.ppermute(x, "fsdp", [(i, i ^ masks[i & 1]) for i in range(fsdp)])
 
     grads, toks = [], []
 
@@ -459,20 +482,19 @@
         toks.append(tok)
         return left
 
-    got_x = swap(own, "fsdp", far_x)
-    got_y = swap(own, "fsdp", far_y)
-    parts, offsets = gather_inner([own], 0)
+    got_1 = swap_far(own, far_x, far_y)
+    got_2 = swap_far(own, far_y, far_x)
+    chunk_0 = gather_inner(own, 0, 0)
     delta, left_t = feedback_left(place, feedback[0], right_t)
-    left_t = forward(parts, offsets, left_t)
-    got_x, got_y, left_t = lax.optimization_barrier((got_x, got_y, left_t))
-    send_x, send_y = halves(got_x, got_y)
-    far = [swap(send_x, "fsdp", far_y), swap(send_y, "fsdp", far_x)]
-    parts_x, offsets_x = gather_inner([got_x], far_x)
-    parts_y, offsets_y = gather_inner([got_y], far_y)
-    left_t = forward(parts_x + parts_y, offsets_x + offsets_y, left_t)
-    far_0, far_1, left_t = lax.optimization_barrier((*far, left_t))
-    parts, offsets = gather_inner([far_0, far_1], far_x ^ far_y)
-    got = swap(forward(parts, offsets, left_t, last=True), "fsdp", 1)
+    left_t = forward(*chunk_0, left_t)
+    got_1, got_2, left_t = lax.optimization_barrier((got_1, got_2, left_t))
+    got_3 = swap_far(got_1, far_y, far_x)
+    chunk_1 = gather_inner(got_1, far_x, far_y)
+    chunk_2 = gather_inner(got_2, far_y, far_x)
+    left_t = forward(chunk_1[0] + chunk_2[0], chunk_1[1] + chunk_2[1], left_t)
+    got_3, left_t = lax.optimization_barrier((got_3, left_t))
+    chunk_3 = gather_inner(got_3, far_x ^ far_y, far_x ^ far_y)
+    got = swap(forward(*chunk_3, left_t, last=True), "fsdp", 1)
     keep = keep_left(place, right_t, grads[-1], toks[-1], left_t)
 
     cuts = [0, feats // 4, 3 * feats // 4, feats]

time: 105 us -> 103 us (0.981)
  starting transfers between devices: 30.1 us -> 28.5 us
  waiting for transfers between devices: 14.8 us -> 15.9 us
    ppermute x28 -> x23, starting transfers between devices: 30.1 us -> 23.7 us  [swap(): return lax.ppermute(x, axis, [(i, i ^ mask) for i in range(size)])]
    ppermute x0 -> x3, starting transfers between devices: none -> 4.84 us  [swap_far(): return lax.ppermute(x, 'fsdp', [(i, i ^ masks[i & 1]) for i in range(fsdp)])]
    ppermute x0 -> x3, waiting for transfers between devices: none -> 1.19 us  [swap_far(): return lax.ppermute(x, 'fsdp', [(i, i ^ masks[i & 1]) for i in range(fsdp)])]
    pallas_call x21 -> x20, Pallas kernels: 57.1 us -> 56.1 us  [call(): pl.pallas_call(body, out_shape=out_shape, compiler_params=pltpu.CompilerP...]
    ppermute x28 -> x23, waiting for transfers between devices: 14.8 us -> 14.7 us  [swap(): return lax.ppermute(x, axis, [(i, i ^ mask) for i in range(size)])]
  transfers between devices with their start and end apart: 28 -> 26, of which waited for: 12 -> 11; matrix products, arithmetic and copies ran while one was open for 0% -> 0% of each run, Pallas kernels for 44% -> 44%
where the time goes in v3:
time: 103 us
  Pallas kernels  56.1 us (54%)
  starting transfers between devices  28.5 us (28%)
  waiting for transfers between devices  15.9 us (15%)
  local copies, waits for them, and re-layouts  1.41 us (1%)
  between operations  1.1 us (1%)
    pallas_call x20, Pallas kernels, call(): pl.pallas_call(body, out_shape=out_shape, compiler_params=pltpu.CompilerP...  56.1 us
    ppermute x23, starting transfers between devices, swap(): return lax.ppermute(x, axis, [(i, i ^ mask) for i in range(size)])  23.7 us
    ppermute x23, waiting for transfers between devices, swap(): return lax.ppermute(x, axis, [(i, i ^ mask) for i in range(size)])  14.7 us
    ppermute x3, starting transfers between devices, swap_far(): return lax.ppermute(x, 'fsdp', [(i, i ^ masks[i & 1]) for i in range(fsdp)])  4.84 us
  transfers between devices with their start and end apart: 26, of which 11 were waited for; matrix products, arithmetic and copies ran while one was open for 0% of the time, Pallas kernels for 44%

profile of v3, /device:TPU:0, one launch (start us, length us, event | category | flops | bytes accessed | tf_op | source)
XLA Modules:
  0.0 103.1 jit_solution(2818603286232341918)
XLA Ops:
  1.1 2.6 %collective-permute-start.1 = (bf16[128,2048]{1,0:T(8,128)(2,1)}, bf16[128,2048]{1,0:T(8,128)(2,1)S(1)}, u32[]{:S(2)}, u32[]{:S(2)}) collective-permute-start(bf16[128,2048]{1,0:T(8,128)(2,1)} %bitcast.19), channel_id=1, source_target_pairs={{0,16},{4,12},{8,24},{12,4},{16,0},{20,28},{24,8},{28,20},{1,17},{... | collective-permute-start | bytes 1572872 | tf_op jit(solution)/shard_map/ppermute | solution.py:473
  3.7 1.5 %collective-permute-start = (bf16[128,2048]{1,0:T(8,128)(2,1)}, bf16[128,2048]{1,0:T(8,128)(2,1)S(1)}, u32[]{:S(2)}, u32[]{:S(2)}) collective-permute-start(bf16[128,2048]{1,0:T(8,128)(2,1)} %bitcast.20), channel_id=1, source_target_pairs={{0,8},{4,20},{8,0},{12,28},{16,24},{20,4},{24,16},{28,12},{1,9},{5... | collective-permute-start | bytes 1572872 | tf_op jit(solution)/shard_map/ppermute | solution.py:473
  6.5 6.9 %feedback_left.1 = (f32[2,896,2048]{2,1,0:T(8,128)S(1)}, f32[2,64,2048]{2,1,0:T(8,128)S(1)}) custom-call(s32[2]{0:T(128)S(1)} %pad_add_fusion.place_ref, f32[2,896,2048]{2,1,0:T(8,128)} %bitcast.22, f32[2,64,896]{2,1,0:T(8,128)S(1)} %bitcast.10), custom_call_target="tpu_custom_call" | custom-call | flops 1879048192 | bytes 15138816 | tf_op jit(solution)/shard_map/feedback_left/pallas_call | solution.py:91
  13.7 3.7 %forward_chunk.3 = (bf16[2,896,256]{2,1,0:T(8,128)(2,1)S(1)}, bf16[256,2048]{1,0:T(8,128)(2,1)S(1)}, f32[2,64,2048]{2,1,0:T(8,128)S(1)}) custom-call(s32[2]{0:T(128)S(1)} %pad_add_fusion.place_ref, bf16[128,2048]{1,0:T(8,128)(2,1)S(1)} %bitcast.21, bf16[128,2048]{1,0:T(8,128)(2,1)S(1)} %collective-permute-done.2.refs_1_, bf16[2,896,2048]{2,1,0:T(8,128)(2,1)S(1)} %bitcast.9, ...), custom_call_target="tpu_custom_call" | custom-call | flops 1879048192 | bytes 11730944 | tf_op jit(solution)/shard_map/forward_chunk/pallas_call | solution.py:91
  20.1 5.8 %forward_chunk.4 = (bf16[2,896,512]{2,1,0:T(8,128)(2,1)S(1)}, bf16[512,2048]{1,0:T(8,128)(2,1)S(1)}, f32[2,64,2048]{2,1,0:T(8,128)S(1)}) custom-call(s32[2]{0:T(128)S(1)} %pad_add_fusion.place_ref, bf16[128,2048]{1,0:T(8,128)(2,1)S(1)} %collective-permute-done.refs_0_, bf16[128,2048]{1,0:T(8,128)(2,1)S(1)} %collective-permute-done.4.refs_1_, ...), custom_call_target="tpu_custom_call" | custom-call | flops 3758096384 | bytes 12779520 | tf_op jit(solution)/shard_map/forward_chunk/pallas_call | solution.py:91
  27.2 1.9 %collective-permute-done.6.refs_1_ = bf16[128,2048]{1,0:T(8,128)(2,1)S(1)} collective-permute-done((bf16[128,2048]{1,0:T(8,128)(2,1)S(1)}, bf16[128,2048]{1,0:T(8,128)(2,1)S(1)}, u32[]{:S(2)}, u32[]{:S(2)}) %collective-permute-start.6) | collective-permute-done | bytes 524320 | tf_op jit(solution)/shard_map/ppermute | solution.py:376
  29.1 3.5 %forward_chunk.5 = (bf16[2,896,256]{2,1,0:T(8,128)(2,1)S(1)}, bf16[256,2048]{1,0:T(8,128)(2,1)S(1)}, f32[64,2048]{1,0:T(8,128)S(1)}) custom-call(s32[2]{0:T(128)S(1)} %pad_add_fusion.place_ref, bf16[128,2048]{1,0:T(8,128)(2,1)S(1)} %collective-permute-done.3.refs_0_, bf16[128,2048]{1,0:T(8,128)(2,1)S(1)} %collective-permute-done.6.refs_1_, ...), custom_call_target="tpu_custom_call" | custom-call | flops 1879048192 | bytes 11730944 | tf_op jit(solution)/shard_map/forward_chunk/pallas_call | solution.py:91
  35.9 1.7 %collective-permute-start.9 = (f32[64,512]{1,0:T(8,128)S(1)}, f32[64,512]{1,0:T(8,128)S(1)}, u32[]{:S(2)}, u32[]{:S(2)}) collective-permute-start(f32[64,512]{1,0:T(8,128)S(1)} %get-tuple-element.76), channel_id=1, source_target_pairs={{0,16},{4,20},{8,24},{12,28},{16,0},{20,4},{24,8},{28,12},{1,17},{... | collective-permute-start | bytes 393224 | tf_op jit(solution)/shard_map/ppermute | solution.py:376
  38.7 2.9 %gradient.3.fb_ref = f32[2,896,2048]{2,1,0:T(8,128)S(1)} custom-call(s32[2]{0:T(128)S(1)} %pad_add_fusion.place_ref, f32[2,896,2048]{2,1,0:T(8,128)S(1)} %get-tuple-element.78.fb_ref, bf16[2,896,256]{2,1,0:T(8,128)(2,1)S(1)} %get-tuple-element.79.refs_0_, bf16[2,896,512]{2,1,0:T(8,128)(2,1)S(1)} %get-tuple-element.80.refs_1_, ...), custom_call_target="tpu_custom_call", output_to_operand_aliasing={{}: (1, {})} | custom-call | flops 1879048192 | bytes 22544384 | tf_op jit(solution)/shard_map/gradient/pallas_call | solution.py:91
  41.6 2.5 %collective-permute-done.9.refs_2_ = f32[64,512]{1,0:T(8,128)S(1)} collective-permute-done((f32[64,512]{1,0:T(8,128)S(1)}, f32[64,512]{1,0:T(8,128)S(1)}, u32[]{:S(2)}, u32[]{:S(2)}) %collective-permute-start.9) | collective-permute-done | bytes 131104 | tf_op jit(solution)/shard_map/ppermute | solution.py:376
  44.6 3.9 %collective-permute-start.13 = (f32[64,512]{1,0:T(8,128)S(1)}, f32[64,512]{1,0:T(8,128)S(1)}, u32[]{:S(2)}, u32[]{:S(2)}) collective-permute-start(f32[64,512]{1,0:T(8,128)S(1)} %add.4.refs_0_), channel_id=1, source_target_pairs={{0,3},{1,2},{2,1},{3,0},{4,7},{5,6},{6,5},{7,4},{8,11},{9,10},{10,... | collective-permute-start | bytes 393224 | tf_op jit(solution)/shard_map/ppermute | solution.py:376
  49.1 4.7 %gradient.4.fb_ref = f32[2,896,2048]{2,1,0:T(8,128)S(1)} custom-call(s32[2]{0:T(128)S(1)} %pad_add_fusion.place_ref, f32[2,896,2048]{2,1,0:T(8,128)S(1)} %gradient.3.fb_ref, bf16[2,896,256]{2,1,0:T(8,128)(2,1)S(1)} %get-tuple-element.79.refs_0_, bf16[2,896,512]{2,1,0:T(8,128)(2,1)S(1)} %get-tuple-element.80.refs_1_, ...), custom_call_target="tpu_custom_call", output_to_operand_aliasing={{}: (1, {})} | custom-call | flops 3758096384 | bytes 22544384 | tf_op jit(solution)/shard_map/gradient/pallas_call | solution.py:91
  53.8 4.3 %collective-permute-done.12.refs_2_ = f32[64,512]{1,0:T(8,128)S(1)} collective-permute-done((f32[64,512]{1,0:T(8,128)S(1)}, f32[64,512]{1,0:T(8,128)S(1)}, u32[]{:S(2)}, u32[]{:S(2)}) %collective-permute-start.12) | collective-permute-done | bytes 131104 | tf_op jit(solution)/shard_map/ppermute | solution.py:376
  58.7 2.2 %collective-permute-start.16 = (f32[64,512]{1,0:T(8,128)S(1)}, f32[64,512]{1,0:T(8,128)S(1)}, u32[]{:S(2)}, u32[]{:S(2)}) collective-permute-start(f32[64,512]{1,0:T(8,128)S(1)} %add.5.refs_0_), channel_id=1, source_target_pairs={{0,24},{4,28},{8,16},{12,20},{16,8},{20,12},{24,0},{28,4},{1,25},{... | collective-permute-start | bytes 393224 | tf_op jit(solution)/shard_map/ppermute | solution.py:376
  62.3 2.7 %gradient.5.delta_ref = f32[2,896,2048]{2,1,0:T(8,128)S(1)} custom-call(s32[2]{0:T(128)S(1)} %pad_add_fusion.place_ref, f32[2,896,2048]{2,1,0:T(8,128)S(1)} %gradient.4.fb_ref, bf16[2,896,256]{2,1,0:T(8,128)(2,1)S(1)} %get-tuple-element.79.refs_0_, bf16[2,896,512]{2,1,0:T(8,128)(2,1)S(1)} %get-tuple-element.80.refs_1_, ...), custom_call_target="tpu_custom_call", output_to_operand_aliasing={{}: (1, {})} | custom-call | flops 1879048192 | bytes 22544384 | tf_op jit(solution)/shard_map/gradient/pallas_call | solution.py:91
  68.4 3.0 %project.2 = (f32[32,896]{1,0:T(8,128)S(1)}, f32[32,896]{1,0:T(8,128)S(1)}) custom-call(s32[2]{0:T(128)S(1)} %pad_add_fusion.place_ref, f32[2,896,2048]{2,1,0:T(8,128)S(1)} %gradient.5.delta_ref, f32[64,2048]{1,0:T(8,128)S(1)} %join.1.left_ref.mine_ref), custom_call_target="tpu_custom_call" | custom-call | flops 939524096 | bytes 15204352 | tf_op jit(solution)/shard_map/project/pallas_call | solution.py:91
  71.4 2.2 %collective-permute-start.21 = (f32[32,896]{1,0:T(8,128)S(1)}, f32[32,896]{1,0:T(8,128)S(1)}, u32[]{:S(2)}, u32[]{:S(2)}) collective-permute-start(f32[32,896]{1,0:T(8,128)S(1)} %get-tuple-element.96.refs_1_), channel_id=1, source_target_pairs={{0,3},{1,2},{2,1},{3,0},{4,7},{5,6},{6,5},{7,4},{8,11},{9,10},{10,... | collective-permute-start | bytes 344072 | tf_op jit(solution)/shard_map/ppermute | solution.py:376
  73.6 3.0 %project.3 = (f32[32,896]{1,0:T(8,128)S(1)}, f32[32,896]{1,0:T(8,128)S(1)}) custom-call(s32[2]{0:T(128)S(1)} %pad_add_fusion.place_ref, f32[2,896,2048]{2,1,0:T(8,128)S(1)} %gradient.5.delta_ref, f32[64,2048]{1,0:T(8,128)S(1)} %collective-permute-done.17.left_ref.other_ref), custom_call_target="tpu_custom_call" | custom-call | flops 939524096 | bytes 15204352 | tf_op jit(solution)/shard_map/project/pallas_call | solution.py:91
  76.6 1.8 %collective-permute-start.19 = (f32[32,896]{1,0:T(8,128)S(1)}, f32[32,896]{1,0:T(8,128)S(1)}, u32[]{:S(2)}, u32[]{:S(2)}) collective-permute-start(f32[32,896]{1,0:T(8,128)S(1)} %get-tuple-element.99.refs_1_), channel_id=1, source_target_pairs={{0,3},{1,2},{2,1},{3,0},{4,7},{5,6},{6,5},{7,4},{8,11},{9,10},{10,... | collective-permute-start | bytes 344072 | tf_op jit(solution)/shard_map/ppermute | solution.py:376
  80.4 1.8 %collective-permute-start.24 = (f32[32,896]{1,0:T(8,128)S(1)}, f32[32,896]{1,0:T(8,128)S(1)}, u32[]{:S(2)}, u32[]{:S(2)}) collective-permute-start(f32[32,896]{1,0:T(8,128)S(1)} %get-tuple-element.102.y0_ref), channel_id=1, source_target_pairs={{0,3},{1,2},{2,1},{3,0},{4,7},{5,6},{6,5},{7,4},{8,11},{9,10},{10,... | collective-permute-start | bytes 344072 | tf_op jit(solution)/shard_map/ppermute | solution.py:376
  82.2 3.6 %collective-permute-start.25 = (f32[32,896]{1,0:T(8,128)S(1)}, f32[32,896]{1,0:T(8,128)S(1)}, u32[]{:S(2)}, u32[]{:S(2)}) collective-permute-start(f32[32,896]{1,0:T(8,128)S(1)} %get-tuple-element.103.y1_ref), channel_id=1, source_target_pairs={{0,1},{1,0},{2,3},{3,2},{4,5},{5,4},{6,7},{7,6},{8,9},{9,8},{10,11... | collective-permute-start | bytes 344072 | tf_op jit(solution)/shard_map/ppermute | solution.py:376
  85.8 3.6 %factorize.1.inv_ref = f32[2,64,64]{2,1,0:T(8,128)S(1)} custom-call(s32[2]{0:T(128)S(1)} %pad_add_fusion.place_ref, f32[64,2048]{1,0:T(8,128)S(1)} %join.1.left_ref.mine_ref, f32[64,2048]{1,0:T(8,128)S(1)} %collective-permute-done.17.left_ref.other_ref), custom_call_target="tpu_custom_call" | custom-call | flops 2000000 | bytes 1048576 | tf_op jit(solution)/shard_map/factorize/pallas_call | solution.py:91
  92.5 5.2 %finish.2 = (f32[2,896,2048]{2,1,0:T(8,128)}, f32[2,896,512]{2,1,0:T(8,128)}, bf16[2,896,512]{2,1,0:T(8,128)(2,1)}, f32[2,64,896]{2,1,0:T(8,128)}) custom-call(s32[2]{0:T(128)S(1)} %pad_add_fusion.place_ref, f32[32,896]{1,0:T(8,128)S(1)} %get-tuple-element.102.y0_ref, f32[32,896]{1,0:T(8,128)S(1)} %get-tuple-element.103.y1_ref, ...), custom_call_target="tpu_custom_call" | custom-call | flops 939524096 | bytes 27754496 | tf_op jit(solution)/shard_map/finish/pallas_call | solution.py:91
  97.7 5.2 %finish.3 = (f32[2,896,2048]{2,1,0:T(8,128)}, f32[2,896,512]{2,1,0:T(8,128)}, bf16[2,896,512]{2,1,0:T(8,128)(2,1)}, f32[2,64,896]{2,1,0:T(8,128)}) custom-call(s32[2]{0:T(128)S(1)} %pad_add_fusion.place_ref, f32[32,896]{1,0:T(8,128)S(1)} %get-tuple-element.107.y0_ref, ...), custom_call_target="tpu_custom_call", output_to_operand_aliasing={{0}: (10, {}), {1}: (11, {}), {2}: (12, {}), {3}: (13, {})} | custom-call | flops 939524096 | bytes 48398336 | tf_op jit(solution)/shard_map/finish/pallas_call | solution.py:91
  (64 shorter events, 22.0 us)
Async XLA Ops:
  0.6 12.8 %collective-permute-start.2 = (bf16[128,2048]{1,0:T(8,128)(2,1)}, bf16[128,2048]{1,0:T(8,128)(2,1)S(1)}, u32[]{:S(2)}, u32[]{:S(2)}) collective-permute-start(bf16[128,2048]{1,0:T(8,128)(2,1)} %bitcast.18), channel_id=1, source_target_pairs={{0,4},{4,0},{8,12},{12,8},{16,20},{20,16},{24,28},{28,24},{1,5},{5... | collective-permute-start | bytes 1572872 | tf_op jit(solution)/shard_map/ppermute | solution.py:376
  1.1 16.2 %collective-permute-start.1 = (bf16[128,2048]{1,0:T(8,128)(2,1)}, bf16[128,2048]{1,0:T(8,128)(2,1)S(1)}, u32[]{:S(2)}, u32[]{:S(2)}) collective-permute-start(bf16[128,2048]{1,0:T(8,128)(2,1)} %bitcast.19), channel_id=1, source_target_pairs={{0,16},{4,12},{8,24},{12,4},{16,0},{20,28},{24,8},{28,20},{1,17},{... | collective-permute-start | bytes 1572872 | tf_op jit(solution)/shard_map/ppermute | solution.py:473
  3.7 13.6 %collective-permute-start = (bf16[128,2048]{1,0:T(8,128)(2,1)}, bf16[128,2048]{1,0:T(8,128)(2,1)S(1)}, u32[]{:S(2)}, u32[]{:S(2)}) collective-permute-start(bf16[128,2048]{1,0:T(8,128)(2,1)} %bitcast.20), channel_id=1, source_target_pairs={{0,8},{4,20},{8,0},{12,28},{16,24},{20,4},{24,16},{28,12},{1,9},{5... | collective-permute-start | bytes 1572872 | tf_op jit(solution)/shard_map/ppermute | solution.py:473
  17.4 2.0 %collective-permute-start.5 = (bf16[128,2048]{1,0:T(8,128)(2,1)S(1)}, bf16[128,2048]{1,0:T(8,128)(2,1)S(1)}, u32[]{:S(2)}, u32[]{:S(2)}) collective-permute-start(bf16[128,2048]{1,0:T(8,128)(2,1)S(1)} %collective-permute-done.1.refs_2_), channel_id=1, source_target_pairs={{0,4},{4,0},{8,12},{12,8},{16,20},{20,16},{24,28},{28,24},{1,5},{5... | collective-permute-start | bytes 1572872 | tf_op jit(solution)/shard_map/ppermute | solution.py:376
  17.5 2.6 %collective-permute-start.4 = (bf16[128,2048]{1,0:T(8,128)(2,1)S(1)}, bf16[128,2048]{1,0:T(8,128)(2,1)S(1)}, u32[]{:S(2)}, u32[]{:S(2)}) collective-permute-start(bf16[128,2048]{1,0:T(8,128)(2,1)S(1)} %collective-permute-done.refs_0_), channel_id=1, source_target_pairs={{0,4},{4,0},{8,12},{12,8},{16,20},{20,16},{24,28},{28,24},{1,5},{5... | collective-permute-start | bytes 1572872 | tf_op jit(solution)/shard_map/ppermute | solution.py:376
  18.0 9.2 %collective-permute-start.3 = (bf16[128,2048]{1,0:T(8,128)(2,1)S(1)}, bf16[128,2048]{1,0:T(8,128)(2,1)S(1)}, u32[]{:S(2)}, u32[]{:S(2)}) collective-permute-start(bf16[128,2048]{1,0:T(8,128)(2,1)S(1)} %collective-permute-done.refs_0_), channel_id=1, source_target_pairs={{0,16},{4,12},{8,24},{12,4},{16,0},{20,28},{24,8},{28,20},{1,17},{... | collective-permute-start | bytes 1572872 | tf_op jit(solution)/shard_map/ppermute | solution.py:473
  35.1 6.4 %collective-permute-start.8 = (f32[64,512]{1,0:T(8,128)S(1)}, f32[64,512]{1,0:T(8,128)S(1)}, u32[]{:S(2)}, u32[]{:S(2)}) collective-permute-start(f32[64,512]{1,0:T(8,128)S(1)} %get-tuple-element.75), channel_id=1, source_target_pairs={{0,8},{4,12},{8,0},{12,4},{16,24},{20,28},{24,16},{28,20},{1,9},{5... | collective-permute-start | bytes 393224 | tf_op jit(solution)/shard_map/ppermute | solution.py:376
  35.9 8.1 %collective-permute-start.9 = (f32[64,512]{1,0:T(8,128)S(1)}, f32[64,512]{1,0:T(8,128)S(1)}, u32[]{:S(2)}, u32[]{:S(2)}) collective-permute-start(f32[64,512]{1,0:T(8,128)S(1)} %get-tuple-element.76), channel_id=1, source_target_pairs={{0,16},{4,20},{8,24},{12,28},{16,0},{20,4},{24,8},{28,12},{1,17},{... | collective-permute-start | bytes 393224 | tf_op jit(solution)/shard_map/ppermute | solution.py:376
  37.7 6.4 %collective-permute-start.10 = (f32[64,512]{1,0:T(8,128)S(1)}, f32[64,512]{1,0:T(8,128)S(1)}, u32[]{:S(2)}, u32[]{:S(2)}) collective-permute-start(f32[64,512]{1,0:T(8,128)S(1)} %get-tuple-element.77), channel_id=1, source_target_pairs={{0,24},{4,28},{8,16},{12,20},{16,8},{20,12},{24,0},{28,4},{1,25},{... | collective-permute-start | bytes 393224 | tf_op jit(solution)/shard_map/ppermute | solution.py:376
  44.6 9.2 %collective-permute-start.13 = (f32[64,512]{1,0:T(8,128)S(1)}, f32[64,512]{1,0:T(8,128)S(1)}, u32[]{:S(2)}, u32[]{:S(2)}) collective-permute-start(f32[64,512]{1,0:T(8,128)S(1)} %add.4.refs_0_), channel_id=1, source_target_pairs={{0,3},{1,2},{2,1},{3,0},{4,7},{5,6},{6,5},{7,4},{8,11},{9,10},{10,... | collective-permute-start | bytes 393224 | tf_op jit(solution)/shard_map/ppermute | solution.py:376
  48.4 9.7 %collective-permute-start.12 = (f32[64,512]{1,0:T(8,128)S(1)}, f32[64,512]{1,0:T(8,128)S(1)}, u32[]{:S(2)}, u32[]{:S(2)}) collective-permute-start(f32[64,512]{1,0:T(8,128)S(1)} %add.4.refs_0_), channel_id=1, source_target_pairs={{0,2},{1,3},{2,0},{3,1},{4,6},{5,7},{6,4},{7,5},{8,10},{9,11},{10,... | collective-permute-start | bytes 393224 | tf_op jit(solution)/shard_map/ppermute | solution.py:376
  48.5 9.7 %collective-permute-start.11 = (f32[64,512]{1,0:T(8,128)S(1)}, f32[64,512]{1,0:T(8,128)S(1)}, u32[]{:S(2)}, u32[]{:S(2)}) collective-permute-start(f32[64,512]{1,0:T(8,128)S(1)} %add.4.refs_0_), channel_id=1, source_target_pairs={{0,1},{1,0},{2,3},{3,2},{4,5},{5,4},{6,7},{7,6},{8,9},{9,8},{10,11... | collective-permute-start | bytes 393224 | tf_op jit(solution)/shard_map/ppermute | solution.py:376
  58.7 7.1 %collective-permute-start.16 = (f32[64,512]{1,0:T(8,128)S(1)}, f32[64,512]{1,0:T(8,128)S(1)}, u32[]{:S(2)}, u32[]{:S(2)}) collective-permute-start(f32[64,512]{1,0:T(8,128)S(1)} %add.5.refs_0_), channel_id=1, source_target_pairs={{0,24},{4,28},{8,16},{12,20},{16,8},{20,12},{24,0},{28,4},{1,25},{... | collective-permute-start | bytes 393224 | tf_op jit(solution)/shard_map/ppermute | solution.py:376
  60.9 6.1 %collective-permute-start.15 = (f32[64,512]{1,0:T(8,128)S(1)}, f32[64,512]{1,0:T(8,128)S(1)}, u32[]{:S(2)}, u32[]{:S(2)}) collective-permute-start(f32[64,512]{1,0:T(8,128)S(1)} %add.5.refs_0_), channel_id=1, source_target_pairs={{0,16},{4,20},{8,24},{12,28},{16,0},{20,4},{24,8},{28,12},{1,17},{... | collective-permute-start | bytes 393224 | tf_op jit(solution)/shard_map/ppermute | solution.py:376
  62.3 5.3 %collective-permute-start.14 = (f32[64,512]{1,0:T(8,128)S(1)}, f32[64,512]{1,0:T(8,128)S(1)}, u32[]{:S(2)}, u32[]{:S(2)}) collective-permute-start(f32[64,512]{1,0:T(8,128)S(1)} %add.5.refs_0_), channel_id=1, source_target_pairs={{0,8},{4,12},{8,0},{12,4},{16,24},{20,28},{24,16},{28,20},{1,9},{5... | collective-permute-start | bytes 393224 | tf_op jit(solution)/shard_map/ppermute | solution.py:376
  68.3 5.3 %collective-permute-start.17 = (f32[64,2048]{1,0:T(8,128)S(1)}, f32[64,2048]{1,0:T(8,128)S(1)}, u32[]{:S(2)}, u32[]{:S(2)}) collective-permute-start(f32[64,2048]{1,0:T(8,128)S(1)} %join.1.left_ref.mine_ref), channel_id=1, source_target_pairs={{0,4},{4,0},{8,12},{12,8},{16,20},{20,16},{24,28},{28,24},{1,5},{5... | collective-permute-start | bytes 1572872 | tf_op jit(solution)/shard_map/ppermute | solution.py:376
  71.3 7.2 %collective-permute-start.20 = (f32[32,896]{1,0:T(8,128)S(1)}, f32[32,896]{1,0:T(8,128)S(1)}, u32[]{:S(2)}, u32[]{:S(2)}) collective-permute-start(f32[32,896]{1,0:T(8,128)S(1)} %get-tuple-element.95.refs_0_), channel_id=1, source_target_pairs={{0,1},{1,0},{2,3},{3,2},{4,5},{5,4},{6,7},{7,6},{8,9},{9,8},{10,11... | collective-permute-start | bytes 344072 | tf_op jit(solution)/shard_map/ppermute | solution.py:376
  71.4 8.5 %collective-permute-start.21 = (f32[32,896]{1,0:T(8,128)S(1)}, f32[32,896]{1,0:T(8,128)S(1)}, u32[]{:S(2)}, u32[]{:S(2)}) collective-permute-start(f32[32,896]{1,0:T(8,128)S(1)} %get-tuple-element.96.refs_1_), channel_id=1, source_target_pairs={{0,3},{1,2},{2,1},{3,0},{4,7},{5,6},{6,5},{7,4},{8,11},{9,10},{10,... | collective-permute-start | bytes 344072 | tf_op jit(solution)/shard_map/ppermute | solution.py:376
  76.6 12.9 %collective-permute-start.19 = (f32[32,896]{1,0:T(8,128)S(1)}, f32[32,896]{1,0:T(8,128)S(1)}, u32[]{:S(2)}, u32[]{:S(2)}) collective-permute-start(f32[32,896]{1,0:T(8,128)S(1)} %get-tuple-element.99.refs_1_), channel_id=1, source_target_pairs={{0,3},{1,2},{2,1},{3,0},{4,7},{5,6},{6,5},{7,4},{8,11},{9,10},{10,... | collective-permute-start | bytes 344072 | tf_op jit(solution)/shard_map/ppermute | solution.py:376
  78.3 11.1 %collective-permute-start.18 = (f32[32,896]{1,0:T(8,128)S(1)}, f32[32,896]{1,0:T(8,128)S(1)}, u32[]{:S(2)}, u32[]{:S(2)}) collective-permute-start(f32[32,896]{1,0:T(8,128)S(1)} %get-tuple-element.98.refs_0_), channel_id=1, source_target_pairs={{0,1},{1,0},{2,3},{3,2},{4,5},{5,4},{6,7},{7,6},{8,9},{9,8},{10,11... | collective-permute-start | bytes 344072 | tf_op jit(solution)/shard_map/ppermute | solution.py:376
  80.4 12.0 %collective-permute-start.24 = (f32[32,896]{1,0:T(8,128)S(1)}, f32[32,896]{1,0:T(8,128)S(1)}, u32[]{:S(2)}, u32[]{:S(2)}) collective-permute-start(f32[32,896]{1,0:T(8,128)S(1)} %get-tuple-element.102.y0_ref), channel_id=1, source_target_pairs={{0,3},{1,2},{2,1},{3,0},{4,7},{5,6},{6,5},{7,4},{8,11},{9,10},{10,... | collective-permute-start | bytes 344072 | tf_op jit(solution)/shard_map/ppermute | solution.py:376
  82.2 10.2 %collective-permute-start.25 = (f32[32,896]{1,0:T(8,128)S(1)}, f32[32,896]{1,0:T(8,128)S(1)}, u32[]{:S(2)}, u32[]{:S(2)}) collective-permute-start(f32[32,896]{1,0:T(8,128)S(1)} %get-tuple-element.103.y1_ref), channel_id=1, source_target_pairs={{0,1},{1,0},{2,3},{3,2},{4,5},{5,4},{6,7},{7,6},{8,9},{9,8},{10,11... | collective-permute-start | bytes 344072 | tf_op jit(solution)/shard_map/ppermute | solution.py:376
  90.1 7.6 %collective-permute-start.22 = (f32[32,896]{1,0:T(8,128)S(1)}, f32[32,896]{1,0:T(8,128)S(1)}, u32[]{:S(2)}, u32[]{:S(2)}) collective-permute-start(f32[32,896]{1,0:T(8,128)S(1)} %get-tuple-element.107.y0_ref), channel_id=1, source_target_pairs={{0,3},{1,2},{2,1},{3,0},{4,7},{5,6},{6,5},{7,4},{8,11},{9,10},{10,... | collective-permute-start | bytes 344072 | tf_op jit(solution)/shard_map/ppermute | solution.py:376
  91.1 6.6 %collective-permute-start.23 = (f32[32,896]{1,0:T(8,128)S(1)}, f32[32,896]{1,0:T(8,128)S(1)}, u32[]{:S(2)}, u32[]{:S(2)}) collective-permute-start(f32[32,896]{1,0:T(8,128)S(1)} %get-tuple-element.108.y1_ref), channel_id=1, source_target_pairs={{0,1},{1,0},{2,3},{3,2},{4,5},{5,4},{6,7},{7,6},{8,9},{9,8},{10,11... | collective-permute-start | bytes 344072 | tf_op jit(solution)/shard_map/ppermute | solution.py:376
  (9 other events, 56.9 us)

commit v4 on v3

--- a/solution.py
+++ b/solution.py
@@ -115,7 +115,10 @@
     block = 512
     steps = feats // block
 
-    def body(place_ref, fb_ref, r_ref, held_ref, out_ref, sems):
+    def body(place_ref, fb_ref, r_ref, held_ref, out_ref, right, sems, right_sem):
+        right_copy = pltpu.make_async_copy(r_ref, right, right_sem)
+        right_copy.start()
+
         def copy(k, d):
             cols = slice(d * block, (d + 1) * block)
             return pltpu.make_async_copy(
@@ -125,17 +128,22 @@
         order = [(k, d) for k in range(2) for d in range(steps)]
         for k, d in order:
             copy(k, d).start()
+        right_copy.wait()
         for k, d in order:
             cols = slice(d * block, (d + 1) * block)
-            r_cat = stacked(r_ref[k])
+            r_cat = stacked(right[k])
             copy(k, d).wait()
             fb_hi, fb_lo = split2(held_ref[k, :, cols])
             out_ref[k, :, cols] = fold(dot(r_cat, fb_hi)) + dot(r_cat[:rank], fb_lo)
 
     return call(
-        body, place, (in_hbm(feedback), right_t), [kept(feedback), shape(2, rank, feats)], 10,
-        2 * rows * feats * 256, name="feedback_left", in_specs=[smem, hbm, vmem],
-        scratch_shapes=[pltpu.SemaphoreType.DMA((2, steps))],
+        body, place, (in_hbm(feedback), in_hbm(right_t)), [kept(feedback), shape(2, rank, feats)], 10,
+        2 * rows * feats * 256, name="feedback_left", in_specs=[smem, hbm, hbm],
+        scratch_shapes=[
+            pltpu.VMEM((2, rank, rows), f32),
+            pltpu.SemaphoreType.DMA((2, steps)),
+            pltpu.SemaphoreType.DMA,
+        ],
     )
 
 
@@ -245,17 +253,18 @@
 def factorize(place, mine, other, scale):
     rank, feats = mine.shape
 
-    def body(place_ref, mine_ref, other_ref, inv_ref):
+    def body(place_ref, mine_ref, other_ref, inv_ref, cat_ref):
         core = place_ref[0] & 1
         row_id = lax.broadcasted_iota(jnp.int32, (rank, 2 * rank), 0)
         eye = (
             lax.broadcasted_iota(jnp.int32, (rank, rank), 0)
             == lax.broadcasted_iota(jnp.int32, (rank, rank), 1)
         ).astype(f32)
-        work, roots = [], []
+        lefts, work, roots = [], [], []
         for k in range(2):
             x = jnp.where(core == k, mine_ref[...], other_ref[...]) * scale
             gram = gram_full(x)
+            lefts.append(x)
             work.append(jnp.concatenate([gram, eye], 1))
             roots.append(jnp.zeros((rank, 2 * rank), f32))
         group = 8
@@ -275,27 +284,14 @@
                     a = a - ratio * a[j : j + 1, :]
                 work[k] = a
         for k in range(2):
-            inv_ref[k] = (work[k] * roots[k])[:, rank:]
-
-    return call(
-        body, place, (mine, other), shape(2, rank, rank), 8, 1000000, name="factorize"
-    )
-
-
-def make_basis(place, mine, other, inverse, scale):
-    rank, feats = mine.shape
-
-    def body(place_ref, mine_ref, other_ref, inv_ref, cat_ref):
-        core = place_ref[0] & 1
-        for k in range(2):
-            x = jnp.where(core == k, mine_ref[...], other_ref[...]) * scale
-            basis = dot_full(inv_ref[k], x)
-            b_hi, b_lo = split2(basis)
+            inv = (work[k] * roots[k])[:, rank:]
+            inv_ref[k] = inv
+            b_hi, b_lo = split2(dot_full(inv, lefts[k]))
             cat_ref[k] = jnp.concatenate([b_hi, b_lo, b_hi], 0)
 
     return call(
-        body, place, (mine, other, inverse), shape(2, 3 * rank, feats, dtype=bf16), 8, 1000000,
-        name="make_basis",
+        body, place, (mine, other),
+        [shape(2, rank, rank), shape(2, 3 * rank, feats, dtype=bf16)], 12, 1000000, name="factorize",
     )
 
 
@@ -520,12 +516,11 @@
     for t in range(last):
         y_a = add_pairs(place, y_a, got_a)
         got_a = exchange(y_a, t + 1)
-    inverse = factorize(place, after(mine, *y_a), other, scale)
+    inverse, basis_cat = factorize(place, after(mine, *y_a), other, scale)
     *got_b, inverse = lax.optimization_barrier((*got_b, inverse))
     for t in range(last):
         y_b = add_pairs(place, y_b, got_b)
         got_b = exchange(y_b, t + 1)
-    basis_cat = make_basis(place, after(mine, *y_a, *y_b), other, inverse, scale)
     common = inverse, basis_cat, delta, momentum, weight, replicas
     *done, rn_t = finish(place, y_a, got_a, *common, 0, None)
     *got_b, rn_t = lax.optimization_barrier((*got_b, rn_t))

time: 103 us -> 105 us (1.019)
  Pallas kernels: 56.1 us -> 58.7 us
  local copies, waits for them, and re-layouts: 1.41 us -> 0.02 us
    pallas_call x20 -> x19, Pallas kernels: 56.1 us -> 58.7 us  [call(): pl.pallas_call(body, out_shape=out_shape, compiler_params=pltpu.CompilerP...]
    unnamed x14 -> x12, local copies, waits for them, and re-layouts: 1.41 us -> 0.02 us
  transfers between devices with their start and end apart: 26 -> 26, of which waited for: 11 -> 13; matrix products, arithmetic and copies ran while one was open for 0% -> 0% of each run, Pallas kernels for 44% -> 46%
where the time goes in v4:
time: 105 us
  Pallas kernels  58.7 us (56%)
  starting transfers between devices  28.1 us (27%)
  waiting for transfers between devices  16.6 us (16%)
  between operations  1.1 us (1%)
    pallas_call x19, Pallas kernels, call(): pl.pallas_call(body, out_shape=out_shape, compiler_params=pltpu.CompilerP...  58.7 us
    ppermute x23, starting transfers between devices, swap(): return lax.ppermute(x, axis, [(i, i ^ mask) for i in range(size)])  23.5 us
    ppermute x23, waiting for transfers between devices, swap(): return lax.ppermute(x, axis, [(i, i ^ mask) for i in range(size)])  15.4 us
    ppermute x3, starting transfers between devices, swap_far(): return lax.ppermute(x, 'fsdp', [(i, i ^ masks[i & 1]) for i in range(fsdp)])  4.59 us
  transfers between devices with their start and end apart: 26, of which 13 were waited for; matrix products, arithmetic and copies ran while one was open for 0% of the time, Pallas kernels for 46%

profile of v4, /device:TPU:0, one launch (start us, length us, event | category | flops | bytes accessed | tf_op | source)
XLA Modules:
  0.0 104.6 jit_solution(17225411418780601009)
XLA Ops:
  1.1 2.6 %collective-permute-start.1 = (bf16[128,2048]{1,0:T(8,128)(2,1)}, bf16[128,2048]{1,0:T(8,128)(2,1)S(1)}, u32[]{:S(2)}, u32[]{:S(2)}) collective-permute-start(bf16[128,2048]{1,0:T(8,128)(2,1)} %bitcast.19), channel_id=1, source_target_pairs={{0,16},{4,12},{8,24},{12,4},{16,0},{20,28},{24,8},{28,20},{1,17},{... | collective-permute-start | bytes 1572872 | tf_op jit(solution)/shard_map/ppermute | solution.py:469
  3.7 1.5 %collective-permute-start = (bf16[128,2048]{1,0:T(8,128)(2,1)}, bf16[128,2048]{1,0:T(8,128)(2,1)S(1)}, u32[]{:S(2)}, u32[]{:S(2)}) collective-permute-start(bf16[128,2048]{1,0:T(8,128)(2,1)} %bitcast.20), channel_id=1, source_target_pairs={{0,8},{4,20},{8,0},{12,28},{16,24},{20,4},{24,16},{28,12},{1,9},{5... | collective-permute-start | bytes 1572872 | tf_op jit(solution)/shard_map/ppermute | solution.py:469
  5.3 10.0 %feedback_left.1 = (f32[2,896,2048]{2,1,0:T(8,128)S(1)}, f32[2,64,2048]{2,1,0:T(8,128)S(1)}) custom-call(s32[2]{0:T(128)S(1)} %pad_add_fusion.place_ref, f32[2,896,2048]{2,1,0:T(8,128)} %bitcast.22, f32[2,64,896]{2,1,0:T(8,128)} %bitcast.10), custom_call_target="tpu_custom_call" | custom-call | flops 1879048192 | bytes 15138816 | tf_op jit(solution)/shard_map/feedback_left/pallas_call | solution.py:91
  15.4 3.7 %forward_chunk.3 = (bf16[2,896,256]{2,1,0:T(8,128)(2,1)S(1)}, bf16[256,2048]{1,0:T(8,128)(2,1)S(1)}, f32[2,64,2048]{2,1,0:T(8,128)S(1)}) custom-call(s32[2]{0:T(128)S(1)} %pad_add_fusion.place_ref, bf16[128,2048]{1,0:T(8,128)(2,1)S(1)} %bitcast.21, bf16[128,2048]{1,0:T(8,128)(2,1)S(1)} %collective-permute-done.2.refs_1_, bf16[2,896,2048]{2,1,0:T(8,128)(2,1)S(1)} %bitcast.9, ...), custom_call_target="tpu_custom_call" | custom-call | flops 1879048192 | bytes 11730944 | tf_op jit(solution)/shard_map/forward_chunk/pallas_call | solution.py:91
  21.9 5.8 %forward_chunk.4 = (bf16[2,896,512]{2,1,0:T(8,128)(2,1)S(1)}, bf16[512,2048]{1,0:T(8,128)(2,1)S(1)}, f32[2,64,2048]{2,1,0:T(8,128)S(1)}) custom-call(s32[2]{0:T(128)S(1)} %pad_add_fusion.place_ref, bf16[128,2048]{1,0:T(8,128)(2,1)S(1)} %collective-permute-done.refs_0_, bf16[128,2048]{1,0:T(8,128)(2,1)S(1)} %collective-permute-done.4.refs_1_, ...), custom_call_target="tpu_custom_call" | custom-call | flops 3758096384 | bytes 12779520 | tf_op jit(solution)/shard_map/forward_chunk/pallas_call | solution.py:91
  28.9 1.9 %collective-permute-done.6.refs_1_ = bf16[128,2048]{1,0:T(8,128)(2,1)S(1)} collective-permute-done((bf16[128,2048]{1,0:T(8,128)(2,1)S(1)}, bf16[128,2048]{1,0:T(8,128)(2,1)S(1)}, u32[]{:S(2)}, u32[]{:S(2)}) %collective-permute-start.6) | collective-permute-done | bytes 524320 | tf_op jit(solution)/shard_map/ppermute | solution.py:372
  30.8 3.4 %forward_chunk.5 = (bf16[2,896,256]{2,1,0:T(8,128)(2,1)S(1)}, bf16[256,2048]{1,0:T(8,128)(2,1)S(1)}, f32[64,2048]{1,0:T(8,128)S(1)}) custom-call(s32[2]{0:T(128)S(1)} %pad_add_fusion.place_ref, bf16[128,2048]{1,0:T(8,128)(2,1)S(1)} %collective-permute-done.3.refs_0_, bf16[128,2048]{1,0:T(8,128)(2,1)S(1)} %collective-permute-done.6.refs_1_, ...), custom_call_target="tpu_custom_call" | custom-call | flops 1879048192 | bytes 11730944 | tf_op jit(solution)/shard_map/forward_chunk/pallas_call | solution.py:91
  37.7 2.7 %collective-permute-start.10 = (f32[64,512]{1,0:T(8,128)S(1)}, f32[64,512]{1,0:T(8,128)S(1)}, u32[]{:S(2)}, u32[]{:S(2)}) collective-permute-start(f32[64,512]{1,0:T(8,128)S(1)} %get-tuple-element.78), channel_id=1, source_target_pairs={{0,24},{4,28},{8,16},{12,20},{16,8},{20,12},{24,0},{28,4},{1,25},{... | collective-permute-start | bytes 393224 | tf_op jit(solution)/shard_map/ppermute | solution.py:372
  40.4 2.9 %gradient.3.fb_ref = f32[2,896,2048]{2,1,0:T(8,128)S(1)} custom-call(s32[2]{0:T(128)S(1)} %pad_add_fusion.place_ref, f32[2,896,2048]{2,1,0:T(8,128)S(1)} %get-tuple-element.79.fb_ref, bf16[2,896,256]{2,1,0:T(8,128)(2,1)S(1)} %get-tuple-element.80.refs_0_, bf16[2,896,512]{2,1,0:T(8,128)(2,1)S(1)} %get-tuple-element.81.refs_1_, ...), custom_call_target="tpu_custom_call", output_to_operand_aliasing={{}: (1, {})} | custom-call | flops 1879048192 | bytes 22544384 | tf_op jit(solution)/shard_map/gradient/pallas_call | solution.py:91
  43.3 2.2 %collective-permute-done.9.refs_2_ = f32[64,512]{1,0:T(8,128)S(1)} collective-permute-done((f32[64,512]{1,0:T(8,128)S(1)}, f32[64,512]{1,0:T(8,128)S(1)}, u32[]{:S(2)}, u32[]{:S(2)}) %collective-permute-start.9) | collective-permute-done | bytes 131104 | tf_op jit(solution)/shard_map/ppermute | solution.py:372
  46.1 3.6 %collective-permute-start.13 = (f32[64,512]{1,0:T(8,128)S(1)}, f32[64,512]{1,0:T(8,128)S(1)}, u32[]{:S(2)}, u32[]{:S(2)}) collective-permute-start(f32[64,512]{1,0:T(8,128)S(1)} %add.4.refs_0_), channel_id=1, source_target_pairs={{0,3},{1,2},{2,1},{3,0},{4,7},{5,6},{6,5},{7,4},{8,11},{9,10},{10,... | collective-permute-start | bytes 393224 | tf_op jit(solution)/shard_map/ppermute | solution.py:372
  50.5 4.7 %gradient.4.fb_ref = f32[2,896,2048]{2,1,0:T(8,128)S(1)} custom-call(s32[2]{0:T(128)S(1)} %pad_add_fusion.place_ref, f32[2,896,2048]{2,1,0:T(8,128)S(1)} %gradient.3.fb_ref, bf16[2,896,256]{2,1,0:T(8,128)(2,1)S(1)} %get-tuple-element.80.refs_0_, bf16[2,896,512]{2,1,0:T(8,128)(2,1)S(1)} %get-tuple-element.81.refs_1_, ...), custom_call_target="tpu_custom_call", output_to_operand_aliasing={{}: (1, {})} | custom-call | flops 3758096384 | bytes 22544384 | tf_op jit(solution)/shard_map/gradient/pallas_call | solution.py:91
  55.3 4.7 %collective-permute-done.12.refs_2_ = f32[64,512]{1,0:T(8,128)S(1)} collective-permute-done((f32[64,512]{1,0:T(8,128)S(1)}, f32[64,512]{1,0:T(8,128)S(1)}, u32[]{:S(2)}, u32[]{:S(2)}) %collective-permute-start.12) | collective-permute-done | bytes 131104 | tf_op jit(solution)/shard_map/ppermute | solution.py:372
  61.9 1.7 %collective-permute-start.15 = (f32[64,512]{1,0:T(8,128)S(1)}, f32[64,512]{1,0:T(8,128)S(1)}, u32[]{:S(2)}, u32[]{:S(2)}) collective-permute-start(f32[64,512]{1,0:T(8,128)S(1)} %add.5.refs_0_), channel_id=1, source_target_pairs={{0,16},{4,20},{8,24},{12,28},{16,0},{20,4},{24,8},{28,12},{1,17},{... | collective-permute-start | bytes 393224 | tf_op jit(solution)/shard_map/ppermute | solution.py:372
  64.2 2.7 %gradient.5.delta_ref = f32[2,896,2048]{2,1,0:T(8,128)S(1)} custom-call(s32[2]{0:T(128)S(1)} %pad_add_fusion.place_ref, f32[2,896,2048]{2,1,0:T(8,128)S(1)} %gradient.4.fb_ref, bf16[2,896,256]{2,1,0:T(8,128)(2,1)S(1)} %get-tuple-element.80.refs_0_, bf16[2,896,512]{2,1,0:T(8,128)(2,1)S(1)} %get-tuple-element.81.refs_1_, ...), custom_call_target="tpu_custom_call", output_to_operand_aliasing={{}: (1, {})} | custom-call | flops 1879048192 | bytes 22544384 | tf_op jit(solution)/shard_map/gradient/pallas_call | solution.py:91
  69.6 3.0 %project.2 = (f32[32,896]{1,0:T(8,128)S(1)}, f32[32,896]{1,0:T(8,128)S(1)}) custom-call(s32[2]{0:T(128)S(1)} %pad_add_fusion.place_ref, f32[2,896,2048]{2,1,0:T(8,128)S(1)} %gradient.5.delta_ref, f32[64,2048]{1,0:T(8,128)S(1)} %join.1.left_ref.mine_ref), custom_call_target="tpu_custom_call" | custom-call | flops 939524096 | bytes 15204352 | tf_op jit(solution)/shard_map/project/pallas_call | solution.py:91
  72.7 2.2 %collective-permute-start.21 = (f32[32,896]{1,0:T(8,128)S(1)}, f32[32,896]{1,0:T(8,128)S(1)}, u32[]{:S(2)}, u32[]{:S(2)}) collective-permute-start(f32[32,896]{1,0:T(8,128)S(1)} %get-tuple-element.97.refs_1_), channel_id=1, source_target_pairs={{0,3},{1,2},{2,1},{3,0},{4,7},{5,6},{6,5},{7,4},{8,11},{9,10},{10,... | collective-permute-start | bytes 344072 | tf_op jit(solution)/shard_map/ppermute | solution.py:372
  74.8 3.0 %project.3 = (f32[32,896]{1,0:T(8,128)S(1)}, f32[32,896]{1,0:T(8,128)S(1)}) custom-call(s32[2]{0:T(128)S(1)} %pad_add_fusion.place_ref, f32[2,896,2048]{2,1,0:T(8,128)S(1)} %gradient.5.delta_ref, f32[64,2048]{1,0:T(8,128)S(1)} %collective-permute-done.17.left_ref.other_ref), custom_call_target="tpu_custom_call" | custom-call | flops 939524096 | bytes 15204352 | tf_op jit(solution)/shard_map/project/pallas_call | solution.py:91
  77.8 1.8 %collective-permute-start.19 = (f32[32,896]{1,0:T(8,128)S(1)}, f32[32,896]{1,0:T(8,128)S(1)}, u32[]{:S(2)}, u32[]{:S(2)}) collective-permute-start(f32[32,896]{1,0:T(8,128)S(1)} %get-tuple-element.100.refs_1_), channel_id=1, source_target_pairs={{0,3},{1,2},{2,1},{3,0},{4,7},{5,6},{6,5},{7,4},{8,11},{9,10},{10,... | collective-permute-start | bytes 344072 | tf_op jit(solution)/shard_map/ppermute | solution.py:372
  81.7 1.8 %collective-permute-start.24 = (f32[32,896]{1,0:T(8,128)S(1)}, f32[32,896]{1,0:T(8,128)S(1)}, u32[]{:S(2)}, u32[]{:S(2)}) collective-permute-start(f32[32,896]{1,0:T(8,128)S(1)} %get-tuple-element.103.y0_ref), channel_id=1, source_target_pairs={{0,3},{1,2},{2,1},{3,0},{4,7},{5,6},{6,5},{7,4},{8,11},{9,10},{10,... | collective-permute-start | bytes 344072 | tf_op jit(solution)/shard_map/ppermute | solution.py:372
  83.5 3.6 %collective-permute-start.25 = (f32[32,896]{1,0:T(8,128)S(1)}, f32[32,896]{1,0:T(8,128)S(1)}, u32[]{:S(2)}, u32[]{:S(2)}) collective-permute-start(f32[32,896]{1,0:T(8,128)S(1)} %get-tuple-element.104.y1_ref), channel_id=1, source_target_pairs={{0,1},{1,0},{2,3},{3,2},{4,5},{5,4},{6,7},{7,6},{8,9},{9,8},{10,11... | collective-permute-start | bytes 344072 | tf_op jit(solution)/shard_map/ppermute | solution.py:372
  87.1 4.5 %factorize.1 = (f32[2,64,64]{2,1,0:T(8,128)S(1)}, bf16[2,192,2048]{2,1,0:T(8,128)(2,1)S(1)}) custom-call(s32[2]{0:T(128)S(1)} %pad_add_fusion.place_ref, f32[64,2048]{1,0:T(8,128)S(1)} %join.1.left_ref.mine_ref, f32[64,2048]{1,0:T(8,128)S(1)} %collective-permute-done.17.left_ref.other_ref), custom_call_target="tpu_custom_call" | custom-call | flops 2000000 | bytes 1048576 | tf_op jit(solution)/shard_map/factorize/pallas_call | solution.py:91
  93.3 5.2 %finish.2 = (f32[2,896,2048]{2,1,0:T(8,128)}, f32[2,896,512]{2,1,0:T(8,128)}, bf16[2,896,512]{2,1,0:T(8,128)(2,1)}, f32[2,64,896]{2,1,0:T(8,128)}) custom-call(s32[2]{0:T(128)S(1)} %pad_add_fusion.place_ref, f32[32,896]{1,0:T(8,128)S(1)} %get-tuple-element.103.y0_ref, f32[32,896]{1,0:T(8,128)S(1)} %get-tuple-element.104.y1_ref, ...), custom_call_target="tpu_custom_call" | custom-call | flops 939524096 | bytes 27754496 | tf_op jit(solution)/shard_map/finish/pallas_call | solution.py:91
  99.3 5.2 %finish.3 = (f32[2,896,2048]{2,1,0:T(8,128)}, f32[2,896,512]{2,1,0:T(8,128)}, bf16[2,896,512]{2,1,0:T(8,128)(2,1)}, f32[2,64,896]{2,1,0:T(8,128)}) custom-call(s32[2]{0:T(128)S(1)} %pad_add_fusion.place_ref, f32[32,896]{1,0:T(8,128)S(1)} %get-tuple-element.109.y0_ref, ...), custom_call_target="tpu_custom_call", output_to_operand_aliasing={{0}: (10, {}), {1}: (11, {}), {2}: (12, {}), {3}: (13, {})} | custom-call | flops 939524096 | bytes 48398336 | tf_op jit(solution)/shard_map/finish/pallas_call | solution.py:91
  (61 shorter events, 19.0 us)
Async XLA Ops:
  0.6 14.7 %collective-permute-start.2 = (bf16[128,2048]{1,0:T(8,128)(2,1)}, bf16[128,2048]{1,0:T(8,128)(2,1)S(1)}, u32[]{:S(2)}, u32[]{:S(2)}) collective-permute-start(bf16[128,2048]{1,0:T(8,128)(2,1)} %bitcast.18), channel_id=1, source_target_pairs={{0,4},{4,0},{8,12},{12,8},{16,20},{20,16},{24,28},{28,24},{1,5},{5... | collective-permute-start | bytes 1572872 | tf_op jit(solution)/shard_map/ppermute | solution.py:372
  1.1 18.0 %collective-permute-start.1 = (bf16[128,2048]{1,0:T(8,128)(2,1)}, bf16[128,2048]{1,0:T(8,128)(2,1)S(1)}, u32[]{:S(2)}, u32[]{:S(2)}) collective-permute-start(bf16[128,2048]{1,0:T(8,128)(2,1)} %bitcast.19), channel_id=1, source_target_pairs={{0,16},{4,12},{8,24},{12,4},{16,0},{20,28},{24,8},{28,20},{1,17},{... | collective-permute-start | bytes 1572872 | tf_op jit(solution)/shard_map/ppermute | solution.py:469
  3.7 15.4 %collective-permute-start = (bf16[128,2048]{1,0:T(8,128)(2,1)}, bf16[128,2048]{1,0:T(8,128)(2,1)S(1)}, u32[]{:S(2)}, u32[]{:S(2)}) collective-permute-start(bf16[128,2048]{1,0:T(8,128)(2,1)} %bitcast.20), channel_id=1, source_target_pairs={{0,8},{4,20},{8,0},{12,28},{16,24},{20,4},{24,16},{28,12},{1,9},{5... | collective-permute-start | bytes 1572872 | tf_op jit(solution)/shard_map/ppermute | solution.py:469
  19.1 2.0 %collective-permute-start.5 = (bf16[128,2048]{1,0:T(8,128)(2,1)S(1)}, bf16[128,2048]{1,0:T(8,128)(2,1)S(1)}, u32[]{:S(2)}, u32[]{:S(2)}) collective-permute-start(bf16[128,2048]{1,0:T(8,128)(2,1)S(1)} %collective-permute-done.1.refs_2_), channel_id=1, source_target_pairs={{0,4},{4,0},{8,12},{12,8},{16,20},{20,16},{24,28},{28,24},{1,5},{5... | collective-permute-start | bytes 1572872 | tf_op jit(solution)/shard_map/ppermute | solution.py:372
  19.2 2.6 %collective-permute-start.4 = (bf16[128,2048]{1,0:T(8,128)(2,1)S(1)}, bf16[128,2048]{1,0:T(8,128)(2,1)S(1)}, u32[]{:S(2)}, u32[]{:S(2)}) collective-permute-start(bf16[128,2048]{1,0:T(8,128)(2,1)S(1)} %collective-permute-done.refs_0_), channel_id=1, source_target_pairs={{0,4},{4,0},{8,12},{12,8},{16,20},{20,16},{24,28},{28,24},{1,5},{5... | collective-permute-start | bytes 1572872 | tf_op jit(solution)/shard_map/ppermute | solution.py:372
  19.7 9.2 %collective-permute-start.3 = (bf16[128,2048]{1,0:T(8,128)(2,1)S(1)}, bf16[128,2048]{1,0:T(8,128)(2,1)S(1)}, u32[]{:S(2)}, u32[]{:S(2)}) collective-permute-start(bf16[128,2048]{1,0:T(8,128)(2,1)S(1)} %collective-permute-done.refs_0_), channel_id=1, source_target_pairs={{0,16},{4,12},{8,24},{12,4},{16,0},{20,28},{24,8},{28,20},{1,17},{... | collective-permute-start | bytes 1572872 | tf_op jit(solution)/shard_map/ppermute | solution.py:469
  36.8 6.4 %collective-permute-start.8 = (f32[64,512]{1,0:T(8,128)S(1)}, f32[64,512]{1,0:T(8,128)S(1)}, u32[]{:S(2)}, u32[]{:S(2)}) collective-permute-start(f32[64,512]{1,0:T(8,128)S(1)} %get-tuple-element.76), channel_id=1, source_target_pairs={{0,8},{4,12},{8,0},{12,4},{16,24},{20,28},{24,16},{28,20},{1,9},{5... | collective-permute-start | bytes 393224 | tf_op jit(solution)/shard_map/ppermute | solution.py:372
  37.4 8.1 %collective-permute-start.9 = (f32[64,512]{1,0:T(8,128)S(1)}, f32[64,512]{1,0:T(8,128)S(1)}, u32[]{:S(2)}, u32[]{:S(2)}) collective-permute-start(f32[64,512]{1,0:T(8,128)S(1)} %get-tuple-element.77), channel_id=1, source_target_pairs={{0,16},{4,20},{8,24},{12,28},{16,0},{20,4},{24,8},{28,12},{1,17},{... | collective-permute-start | bytes 393224 | tf_op jit(solution)/shard_map/ppermute | solution.py:372
  37.7 7.9 %collective-permute-start.10 = (f32[64,512]{1,0:T(8,128)S(1)}, f32[64,512]{1,0:T(8,128)S(1)}, u32[]{:S(2)}, u32[]{:S(2)}) collective-permute-start(f32[64,512]{1,0:T(8,128)S(1)} %get-tuple-element.78), channel_id=1, source_target_pairs={{0,24},{4,28},{8,16},{12,20},{16,8},{20,12},{24,0},{28,4},{1,25},{... | collective-permute-start | bytes 393224 | tf_op jit(solution)/shard_map/ppermute | solution.py:372
  46.1 9.2 %collective-permute-start.13 = (f32[64,512]{1,0:T(8,128)S(1)}, f32[64,512]{1,0:T(8,128)S(1)}, u32[]{:S(2)}, u32[]{:S(2)}) collective-permute-start(f32[64,512]{1,0:T(8,128)S(1)} %add.4.refs_0_), channel_id=1, source_target_pairs={{0,3},{1,2},{2,1},{3,0},{4,7},{5,6},{6,5},{7,4},{8,11},{9,10},{10,... | collective-permute-start | bytes 393224 | tf_op jit(solution)/shard_map/ppermute | solution.py:372
  49.7 10.3 %collective-permute-start.12 = (f32[64,512]{1,0:T(8,128)S(1)}, f32[64,512]{1,0:T(8,128)S(1)}, u32[]{:S(2)}, u32[]{:S(2)}) collective-permute-start(f32[64,512]{1,0:T(8,128)S(1)} %add.4.refs_0_), channel_id=1, source_target_pairs={{0,2},{1,3},{2,0},{3,1},{4,6},{5,7},{6,4},{7,5},{8,10},{9,11},{10,... | collective-permute-start | bytes 393224 | tf_op jit(solution)/shard_map/ppermute | solution.py:372
  49.7 10.3 %collective-permute-start.11 = (f32[64,512]{1,0:T(8,128)S(1)}, f32[64,512]{1,0:T(8,128)S(1)}, u32[]{:S(2)}, u32[]{:S(2)}) collective-permute-start(f32[64,512]{1,0:T(8,128)S(1)} %add.4.refs_0_), channel_id=1, source_target_pairs={{0,1},{1,0},{2,3},{3,2},{4,5},{5,4},{6,7},{7,6},{8,9},{9,8},{10,11... | collective-permute-start | bytes 393224 | tf_op jit(solution)/shard_map/ppermute | solution.py:372
  60.6 6.9 %collective-permute-start.16 = (f32[64,512]{1,0:T(8,128)S(1)}, f32[64,512]{1,0:T(8,128)S(1)}, u32[]{:S(2)}, u32[]{:S(2)}) collective-permute-start(f32[64,512]{1,0:T(8,128)S(1)} %add.5.refs_0_), channel_id=1, source_target_pairs={{0,24},{4,28},{8,16},{12,20},{16,8},{20,12},{24,0},{28,4},{1,25},{... | collective-permute-start | bytes 393224 | tf_op jit(solution)/shard_map/ppermute | solution.py:372
  61.9 7.0 %collective-permute-start.15 = (f32[64,512]{1,0:T(8,128)S(1)}, f32[64,512]{1,0:T(8,128)S(1)}, u32[]{:S(2)}, u32[]{:S(2)}) collective-permute-start(f32[64,512]{1,0:T(8,128)S(1)} %add.5.refs_0_), channel_id=1, source_target_pairs={{0,16},{4,20},{8,24},{12,28},{16,0},{20,4},{24,8},{28,12},{1,17},{... | collective-permute-start | bytes 393224 | tf_op jit(solution)/shard_map/ppermute | solution.py:372
  63.6 5.3 %collective-permute-start.14 = (f32[64,512]{1,0:T(8,128)S(1)}, f32[64,512]{1,0:T(8,128)S(1)}, u32[]{:S(2)}, u32[]{:S(2)}) collective-permute-start(f32[64,512]{1,0:T(8,128)S(1)} %add.5.refs_0_), channel_id=1, source_target_pairs={{0,8},{4,12},{8,0},{12,4},{16,24},{20,28},{24,16},{28,20},{1,9},{5... | collective-permute-start | bytes 393224 | tf_op jit(solution)/shard_map/ppermute | solution.py:372
  69.5 5.3 %collective-permute-start.17 = (f32[64,2048]{1,0:T(8,128)S(1)}, f32[64,2048]{1,0:T(8,128)S(1)}, u32[]{:S(2)}, u32[]{:S(2)}) collective-permute-start(f32[64,2048]{1,0:T(8,128)S(1)} %join.1.left_ref.mine_ref), channel_id=1, source_target_pairs={{0,4},{4,0},{8,12},{12,8},{16,20},{20,16},{24,28},{28,24},{1,5},{5... | collective-permute-start | bytes 1572872 | tf_op jit(solution)/shard_map/ppermute | solution.py:372
  72.6 7.2 %collective-permute-start.20 = (f32[32,896]{1,0:T(8,128)S(1)}, f32[32,896]{1,0:T(8,128)S(1)}, u32[]{:S(2)}, u32[]{:S(2)}) collective-permute-start(f32[32,896]{1,0:T(8,128)S(1)} %get-tuple-element.96.refs_0_), channel_id=1, source_target_pairs={{0,1},{1,0},{2,3},{3,2},{4,5},{5,4},{6,7},{7,6},{8,9},{9,8},{10,11... | collective-permute-start | bytes 344072 | tf_op jit(solution)/shard_map/ppermute | solution.py:372
  72.7 8.5 %collective-permute-start.21 = (f32[32,896]{1,0:T(8,128)S(1)}, f32[32,896]{1,0:T(8,128)S(1)}, u32[]{:S(2)}, u32[]{:S(2)}) collective-permute-start(f32[32,896]{1,0:T(8,128)S(1)} %get-tuple-element.97.refs_1_), channel_id=1, source_target_pairs={{0,3},{1,2},{2,1},{3,0},{4,7},{5,6},{6,5},{7,4},{8,11},{9,10},{10,... | collective-permute-start | bytes 344072 | tf_op jit(solution)/shard_map/ppermute | solution.py:372
  77.8 13.8 %collective-permute-start.19 = (f32[32,896]{1,0:T(8,128)S(1)}, f32[32,896]{1,0:T(8,128)S(1)}, u32[]{:S(2)}, u32[]{:S(2)}) collective-permute-start(f32[32,896]{1,0:T(8,128)S(1)} %get-tuple-element.100.refs_1_), channel_id=1, source_target_pairs={{0,3},{1,2},{2,1},{3,0},{4,7},{5,6},{6,5},{7,4},{8,11},{9,10},{10,... | collective-permute-start | bytes 344072 | tf_op jit(solution)/shard_map/ppermute | solution.py:372
  79.6 12.0 %collective-permute-start.18 = (f32[32,896]{1,0:T(8,128)S(1)}, f32[32,896]{1,0:T(8,128)S(1)}, u32[]{:S(2)}, u32[]{:S(2)}) collective-permute-start(f32[32,896]{1,0:T(8,128)S(1)} %get-tuple-element.99.refs_0_), channel_id=1, source_target_pairs={{0,1},{1,0},{2,3},{3,2},{4,5},{5,4},{6,7},{7,6},{8,9},{9,8},{10,11... | collective-permute-start | bytes 344072 | tf_op jit(solution)/shard_map/ppermute | solution.py:372
  81.7 11.5 %collective-permute-start.24 = (f32[32,896]{1,0:T(8,128)S(1)}, f32[32,896]{1,0:T(8,128)S(1)}, u32[]{:S(2)}, u32[]{:S(2)}) collective-permute-start(f32[32,896]{1,0:T(8,128)S(1)} %get-tuple-element.103.y0_ref), channel_id=1, source_target_pairs={{0,3},{1,2},{2,1},{3,0},{4,7},{5,6},{6,5},{7,4},{8,11},{9,10},{10,... | collective-permute-start | bytes 344072 | tf_op jit(solution)/shard_map/ppermute | solution.py:372
  83.5 9.8 %collective-permute-start.25 = (f32[32,896]{1,0:T(8,128)S(1)}, f32[32,896]{1,0:T(8,128)S(1)}, u32[]{:S(2)}, u32[]{:S(2)}) collective-permute-start(f32[32,896]{1,0:T(8,128)S(1)} %get-tuple-element.104.y1_ref), channel_id=1, source_target_pairs={{0,1},{1,0},{2,3},{3,2},{4,5},{5,4},{6,7},{7,6},{8,9},{9,8},{10,11... | collective-permute-start | bytes 344072 | tf_op jit(solution)/shard_map/ppermute | solution.py:372
  92.2 6.8 %collective-permute-start.22 = (f32[32,896]{1,0:T(8,128)S(1)}, f32[32,896]{1,0:T(8,128)S(1)}, u32[]{:S(2)}, u32[]{:S(2)}) collective-permute-start(f32[32,896]{1,0:T(8,128)S(1)} %get-tuple-element.109.y0_ref), channel_id=1, source_target_pairs={{0,3},{1,2},{2,1},{3,0},{4,7},{5,6},{6,5},{7,4},{8,11},{9,10},{10,... | collective-permute-start | bytes 344072 | tf_op jit(solution)/shard_map/ppermute | solution.py:372
  93.2 6.0 %collective-permute-start.23 = (f32[32,896]{1,0:T(8,128)S(1)}, f32[32,896]{1,0:T(8,128)S(1)}, u32[]{:S(2)}, u32[]{:S(2)}) collective-permute-start(f32[32,896]{1,0:T(8,128)S(1)} %get-tuple-element.110.y1_ref), channel_id=1, source_target_pairs={{0,1},{1,0},{2,3},{3,2},{4,5},{5,4},{6,7},{7,6},{8,9},{9,8},{10,11... | collective-permute-start | bytes 344072 | tf_op jit(solution)/shard_map/ppermute | solution.py:372
  (8 other events, 72.7 us)
